TPU v7x, 32 devices: a whole 2x2x4 slice. The times are simulated.
32 devices in a mesh: groups: 2 (over x), tensor: 16 (over z, y, core).
Axes of the slice: x: 2, y: 2, z: 4, core: 2. Of those that a mesh axis runs over, the one named last changes fastest.
Arguments:
- input_rows: bfloat16 [512, 8192], P(('groups', 'tensor')), parts along dimension 0, may hold values from -6 to 6
- up_weight: bfloat16 [8192, 28672], P(None, 'tensor'), may hold values from -0.0625 to 0.0625
- adapter_down: bfloat16 [32, 64, 8192], P(('groups', 'tensor')), parts along dimension 0, may hold values from -0.0625 to 0.0625
- adapter_up: bfloat16 [32, 64, 28672], P(('groups', 'tensor')), parts along dimension 0, may hold values from -0.75 to 0.75
- ranks: int32 [32], P('groups'), parts along dimension 0, may hold values from 16 to 64, as said below
- adapter_slot: int32 [32], P('groups'), parts along dimension 0, may hold values from 0 to 15, each once
- segment_lengths: int32 [32], P('groups'), parts along dimension 0, may hold values from 1 to 64, 256 in all
- segment_adapter: int32 [32], P('groups'), parts along dimension 0, may hold values from 0 to 15
Outputs:
- up_out: bfloat16 [512, 28672], P('groups', 'tensor'), parts along dimension 0
There are 2 independent parts, one for each index of `groups`. A program takes and returns all parts, laid end to end along the dimension named above; an argument that names none is the same for every part. Nothing has to cross between parts.
Inputs may be any that keep to these rules, and one draw needn't show every extreme that they name: `ranks`: a multiple of 16; the columns j >= the rank of an adapter's 64 are unused. `adapter_slot`: each storage slot holds exactly one adapter. `segment_lengths`: the segments sum to 256.
All inputs are finite; a program needn't handle non-finite values.
Results may differ from a plain program's by a relative error of at most 0.0039.
Values may be sent and summed in bfloat16 or wider, within the bound.
No kernel may reach another device: no remote copies, remote signals or barrier semaphores. Data moves between devices by JAX's collectives and lax.ppermute only.
A program may use at most 128 MiB of HBM per device.

v0:
```python
import functools

import jax
import jax.numpy as jnp
import numpy as np
from jax import lax
from jax.experimental import pallas as pl
from jax.experimental.pallas import tpu as pltpu
from jax.sharding import PartitionSpec as P

ADAPTER_ALPHA = 32.0
POOLED_SHARDS = 16
FIRST_ROWS = 80


def row_tables(row_count, ranks, adapter_slot, segment_lengths, segment_adapter):
    seg_ends = jnp.cumsum(segment_lengths)
    positions = jnp.arange(row_count, dtype=jnp.int32)
    seg_row = jnp.sum((seg_ends[None, :] <= positions[:, None]).astype(jnp.int32), axis=1)
    seg_pick = (
        seg_row[:, None] == jnp.arange(segment_lengths.shape[0], dtype=jnp.int32)[None, :]
    ).astype(jnp.int32)
    adapter_row = jnp.sum(seg_pick * segment_adapter[None, :], axis=1)
    pool_pick = (
        adapter_row[:, None] == jnp.arange(ranks.shape[0], dtype=jnp.int32)[None, :]
    ).astype(jnp.int32)
    slot_row = jnp.sum(pool_pick * adapter_slot[None, :], axis=1)
    row_rank_values = jnp.sum(pool_pick * ranks[None, :], axis=1)
    return (slot_row, row_rank_values)


def vmem(buffers):
    return pltpu.CompilerParams(vmem_limit_bytes=buffers + (8 << 20))


def split_for_pair(up_factor, core, chips):
    rank_width, hidden = up_factor.shape
    width = hidden // (2 * chips)

    def kernel(core_ref, source, mine, other, sems):
        copies = []
        for q in range(chips):
            for target, half in ((mine, core_ref[0]), (other, 1 - core_ref[0])):
                start = pl.multiple_of((2 * q + half) * width, width)
                copies.append(
                    pltpu.make_async_copy(
                        source.at[:, pl.ds(start, width)], target.at[q], sems.at[len(copies)]
                    )
                )
        for copy in copies:
            copy.start()
        for copy in copies:
            copy.wait()

    block = jax.ShapeDtypeStruct((chips, rank_width, width), up_factor.dtype)
    return pl.pallas_call(
        kernel,
        in_specs=[pl.BlockSpec(memory_space=pltpu.SMEM), pl.BlockSpec(memory_space=pl.ANY)],
        out_specs=[pl.BlockSpec(memory_space=pltpu.VMEM)] * 2,
        out_shape=[block, block],
        scratch_shapes=[pltpu.SemaphoreType.DMA((2 * chips,))],
        compiler_params=vmem(2 * rank_width * hidden),
        cost_estimate=pl.CostEstimate(
            flops=0, bytes_accessed=4 * rank_width * hidden, transcendentals=0
        ),
    )(core, up_factor)


def describe(ranks, adapter_slot, segment_lengths, segment_adapter, position, total_rows, limit):
    slots, segments = ranks.shape[0], segment_lengths.shape[0]
    rank_width = limit // 2
    shift = rank_width.bit_length() - 1

    def kernel(
        ranks_ref, home_ref, length_ref, adapter_ref, position_ref,
        gain_ref, choose_ref, fixed_ref, code_ref, begin_ref, full_ref,
        rank_of, rows_of, used, factor, order,
    ):
        for a in range(slots):
            rows_of[a] = 0
            rank_of[home_ref[a]] = ranks_ref[a]
        starts, start = [], jnp.int32(0)
        for i in range(segments):
            slot = home_ref[adapter_ref[i]]
            starts.append((start, start + length_ref[i], slot))
            order[i] = rows_of[slot] - start
            rows_of[slot] = rows_of[slot] + length_ref[i]
            start = start + length_ref[i]
        full = jnp.int32(0)
        for s in range(slots):
            used[s] = jnp.minimum(rows_of[s], rank_of[s])
            factor[s] = (rank_of[s] < rows_of[s]).astype(jnp.int32)
            begin_ref[s] = used[s - 1] if s % 2 else jnp.int32(0)
            if s % 2:
                full = jnp.maximum(full, used[s - 1] + used[s])
        full_ref[0] = full

        def tables(row):
            spot, code = jnp.zeros_like(row), jnp.zeros_like(row)
            for i, (low, high, slot) in enumerate(starts):
                hit = (row >= low) & (row < high)
                spot = jnp.where(hit, row + (order[i] + begin_ref[slot]), spot)
                code = jnp.where(hit, slot + 32 * factor[slot] + 64 * rank_of[slot], code)
            return spot, code & 31, (code >> 5) & 1, code >> 6

        here = position_ref[0]
        spot, slot, by_factor, rank = tables(
            lax.broadcasted_iota(jnp.int32, (total_rows, limit), 0)
        )
        code_ref[...] = slot + 32 * by_factor + 64 * spot
        lane = lax.broadcasted_iota(jnp.int32, (total_rows, limit), 1)
        half, column = lane >> shift, lane & (rank_width - 1)
        scale = ADAPTER_ALPHA / rank.astype(jnp.float32)
        gain_ref[...] = jnp.where((slot == (here ^ half)) & (column < rank), scale, 0.0)

        spot, slot, by_factor, _ = tables(lax.broadcasted_iota(jnp.int32, (8, total_rows), 1))
        mine = ((slot >> 1) == (here >> 1)) & (by_factor == 0)
        spot = jnp.broadcast_to(jnp.where(mine, spot, -1)[:1], (limit, total_rows))
        line = lax.broadcasted_iota(jnp.int32, (limit, total_rows), 0)
        choose_ref[...] = jnp.where(line == spot, 1.0, 0.0).astype(jnp.bfloat16)

        line = lax.broadcasted_iota(jnp.int32, (limit, limit), 0)
        lane = lax.broadcasted_iota(jnp.int32, (limit, limit), 1)
        half, column = lane >> shift, lane & (rank_width - 1)
        other = here ^ 1
        begin = jnp.where(half == 0, begin_ref[here], begin_ref[other])
        bound = jnp.where(
            half == 0, used[here] * factor[here], used[other] * factor[other]
        )
        held = (line == begin + column) & (column < bound)
        fixed_ref[...] = jnp.where(held, 1.0, 0.0).astype(jnp.bfloat16)

    smem, whole = pl.BlockSpec(memory_space=pltpu.SMEM), pl.BlockSpec(memory_space=pltpu.VMEM)
    return pl.pallas_call(
        kernel,
        in_specs=[smem] * 5,
        out_specs=[whole] * 4 + [smem] * 2,
        out_shape=[
            jax.ShapeDtypeStruct((total_rows, limit), jnp.float32),
            jax.ShapeDtypeStruct((limit, total_rows), jnp.bfloat16),
            jax.ShapeDtypeStruct((limit, limit), jnp.bfloat16),
            jax.ShapeDtypeStruct((total_rows, limit), jnp.int32),
            jax.ShapeDtypeStruct((slots,), jnp.int32),
            jax.ShapeDtypeStruct((1,), jnp.int32),
        ],
        scratch_shapes=[pltpu.SMEM((slots,), jnp.int32)] * 4 + [pltpu.SMEM((segments,), jnp.int32)],
        compiler_params=vmem(16 * total_rows * limit),
        cost_estimate=pl.CostEstimate(
            flops=200 * total_rows * limit, bytes_accessed=16 * total_rows * limit, transcendentals=0
        ),
    )(ranks, adapter_slot, segment_lengths, segment_adapter, position)


def collect_rows(blocks, places, down_pair, gain):
    count = len(blocks)
    height, features = blocks[0].shape
    rank_width = down_pair[0].shape[0]
    chunk = 2048 if features % 2048 == 0 else features
    chunks = features // chunk

    def kernel(places_ref, gain_ref, *refs):
        sources, down_refs = refs[:count], refs[count : count + 2]
        rows_ref, coeff_ref, downs, sems = refs[count + 2 :]
        copies = []
        for k in range(chunks):
            columns = pl.ds(k * chunk, chunk)
            for i in range(2):
                copies.append(
                    pltpu.make_async_copy(
                        down_refs[i].at[:, columns],
                        downs.at[pl.ds(i * rank_width, rank_width), columns],
                        sems.at[k, count + i],
                    )
                )
            for i in range(count):
                start = pl.multiple_of(places_ref[i] * height, height)
                copies.append(
                    pltpu.make_async_copy(
                        sources[i].at[:, columns],
                        rows_ref.at[pl.ds(start, height), columns],
                        sems.at[k, i],
                    )
                )
        for copy in copies:
            copy.start()
        shrink = jnp.zeros(gain_ref.shape, jnp.float32)
        for k in range(chunks):
            for copy in copies[k * (count + 2) : (k + 1) * (count + 2)]:
                copy.wait()
            columns = pl.ds(k * chunk, chunk)
            shrink = shrink + lax.dot_general(
                rows_ref[:, columns],
                downs[:, columns],
                (((1,), (1,)), ((), ())),
                preferred_element_type=jnp.float32,
            )
        coeff_ref[...] = (shrink * gain_ref[...]).astype(jnp.bfloat16)

    rows = count * height
    return pl.pallas_call(
        kernel,
        in_specs=[pl.BlockSpec(memory_space=pltpu.SMEM), pl.BlockSpec(memory_space=pltpu.VMEM)]
        + [pl.BlockSpec(memory_space=pl.ANY)] * (count + 2),
        out_specs=[pl.BlockSpec(memory_space=pltpu.VMEM)] * 2,
        out_shape=[
            jax.ShapeDtypeStruct((rows, features), blocks[0].dtype),
            jax.ShapeDtypeStruct((rows, 2 * rank_width), jnp.bfloat16),
        ],
        scratch_shapes=[
            pltpu.VMEM((2 * rank_width, features), down_pair[0].dtype),
            pltpu.SemaphoreType.DMA((chunks, count + 2)),
        ],
        compiler_params=vmem(4 * rows * features),
        cost_estimate=pl.CostEstimate(
            flops=4 * rows * features * rank_width,
            bytes_accessed=4 * rows * features,
            transcendentals=0,
        ),
    )(places, gain, *blocks, *down_pair)


def build_payload(choose, fixed, coeff, mine, other, first, count):
    chips, rank_width, width = mine.shape

    def kernel(choose_ref, fixed_ref, coeff_ref, mine_ref, other_ref, out_ref):
        lines = pl.ds(first, count)
        select = jnp.dot(choose_ref[lines], coeff_ref[...], preferred_element_type=jnp.float32)
        select = (select + fixed_ref[lines].astype(jnp.float32)).astype(jnp.bfloat16)

        @pl.loop(0, chips)
        def _(q):
            out_ref[q] = jnp.dot(
                select,
                jnp.concatenate([mine_ref[q], other_ref[q]], axis=0),
                preferred_element_type=jnp.float32,
            ).astype(out_ref.dtype)

    return pl.pallas_call(
        kernel,
        in_specs=[pl.BlockSpec(memory_space=pltpu.VMEM)] * 5,
        out_specs=pl.BlockSpec(memory_space=pltpu.VMEM),
        out_shape=jax.ShapeDtypeStruct((chips, count, width), mine.dtype),
        compiler_params=vmem(4 * chips * width * (2 * rank_width + count)),
        cost_estimate=pl.CostEstimate(
            flops=4 * chips * count * rank_width * width,
            bytes_accessed=2 * chips * width * (2 * rank_width + count),
            transcendentals=0,
        ),
    )(choose, fixed, coeff, mine, other)


def combine(base, code, begin, more, coeffs, incoming, extra):
    total_rows, width = base.shape
    chips, first, _ = incoming.shape
    second = extra.shape[1]
    limit = first + second
    rank_width = limit // 2
    shift = rank_width.bit_length() - 1
    tile = 256 if width % 256 == 0 else 128

    def kernel(begin_ref, more_ref, base_ref, code_ref, *refs):
        coeff_refs, incoming_ref = refs[: len(coeffs)], refs[len(coeffs)]
        extra_ref, out_ref, late, sem = refs[len(coeffs) + 1 :]
        fetch = pltpu.make_async_copy(extra_ref, late, sem)
        half = functools.reduce(jnp.add, [ref[...].astype(jnp.float32) for ref in coeff_refs])
        both = jnp.concatenate([half, half], axis=1)
        code_value = code_ref[...]
        slot, by_factor, spot = code_value & 31, (code_value >> 5) & 1, code_value >> 6
        lane = lax.broadcasted_iota(jnp.int32, (total_rows, limit), 1)
        owned = jnp.where(by_factor == 1, slot, -1) - (lane >> shift)
        finished = jnp.where(by_factor == 0, spot, -1)[:, :1]
        finished_chip = (slot >> 1)[:, :1]

        def weights(low, count):
            target = finished - low
            target = jnp.where((target >= 0) & (target < count), finished_chip * count + target, -1)
            wide = lax.broadcasted_iota(jnp.int32, (total_rows, chips * count), 1)
            total = jnp.where(wide == target, 1.0, 0.0)
            line = lax.broadcasted_iota(jnp.int32, (limit, chips * count), 0)
            place = lax.broadcasted_iota(jnp.int32, (limit, chips * count), 1)
            for q in range(chips):
                goal = jnp.where(
                    line < rank_width, line, line - rank_width + begin_ref[2 * q + 1]
                ) - low
                moved = (goal >= 0) & (goal < count) & (place == q * count + goal)
                moved = jnp.where(moved, 1.0, 0.0).astype(jnp.bfloat16)
                part = jnp.where(owned == 2 * q, both, 0.0).astype(jnp.bfloat16)
                total = total + jnp.dot(part, moved, preferred_element_type=jnp.float32)
            return total.astype(jnp.bfloat16)

        near = weights(0, first)

        def write(far):
            @pl.loop(0, width // tile)
            def _(i):
                columns = pl.ds(pl.multiple_of(i * tile, tile), tile)
                block = incoming_ref[:, :, columns].reshape(chips * first, tile)
                total = jnp.dot(near, block, preferred_element_type=jnp.float32)
                total += base_ref[:, columns]
                if far is not None:
                    block = late[:, :, columns].reshape(chips * second, tile)
                    total += jnp.dot(far, block, preferred_element_type=jnp.float32)
                out_ref[:, columns] = total.astype(out_ref.dtype)

        @pl.when(more_ref[0] > first)
        def _():
            fetch.start()
            far = weights(first, second)
            fetch.wait()
            write(far)

        @pl.when(more_ref[0] <= first)
        def _():
            write(None)

    smem, whole = pl.BlockSpec(memory_space=pltpu.SMEM), pl.BlockSpec(memory_space=pltpu.VMEM)
    return pl.pallas_call(
        kernel,
        in_specs=[smem] * 2
        + [whole] * (len(coeffs) + 3)
        + [pl.BlockSpec(memory_space=pl.ANY)],
        out_specs=whole,
        out_shape=jax.ShapeDtypeStruct((total_rows, width), jnp.bfloat16),
        scratch_shapes=[pltpu.VMEM(extra.shape, extra.dtype), pltpu.SemaphoreType.DMA(())],
        compiler_params=vmem(8 * total_rows * width + 2 * chips * limit * width),
        cost_estimate=pl.CostEstimate(
            flops=4 * total_rows * chips * limit * width,
            bytes_accessed=6 * total_rows * width + 2 * chips * limit * width,
            transcendentals=0,
        ),
    )(begin, more, base, code, *coeffs, incoming, extra)


def ring_gather(block, shards):
    chips = shards // 2
    depth = chips // 2
    cycle = list(range(0, chips, 2)) + list(range(chips - 1, 0, -2))
    ahead = [
        (2 * cycle[p] + c, 2 * cycle[(p + 1) % chips] + c) for p in range(chips) for c in range(2)
    ]
    back = [(b, a) for a, b in ahead]
    sibling = [(t, t ^ 1) for t in range(shards)]
    held = {0: block}
    for step in range(1, depth + 1):
        held[-step] = lax.ppermute(held[1 - step], "tensor", ahead)
        if step < chips - depth:
            held[step] = lax.ppermute(held[step - 1], "tensor", back)
    blocks = []
    for piece in held.values():
        blocks += [piece, lax.ppermute(piece, "tensor", sibling)]
    table = np.zeros((shards, shards), np.int32)
    for t in range(shards):
        for i, offset in enumerate(held):
            chip = cycle[(cycle.index(t // 2) + offset) % chips]
            table[t, 2 * i], table[t, 2 * i + 1] = 2 * chip + t % 2, 2 * chip + 1 - t % 2
    places = lax.dynamic_index_in_dim(table, lax.axis_index("tensor"), keepdims=False)
    return blocks, places, held[-1]


def largest_over_groups(value):
    groups = lax.axis_size("groups")
    for shift in range(1, groups):
        other = lax.ppermute(value, "groups", [(g, (g + shift) % groups) for g in range(groups)])
        value = jnp.maximum(value, other)
    return value


def pooled(
    input_rows,
    up_weight,
    adapter_down,
    adapter_up,
    ranks,
    adapter_slot,
    segment_lengths,
    segment_adapter,
):
    shards = lax.axis_size("tensor")
    position = lax.axis_index("tensor").astype(jnp.int32)
    chips = shards // 2
    total_rows = input_rows.shape[0] * shards
    rank_width = adapter_up.shape[1]
    limit = 2 * rank_width
    sibling = [(t, t ^ 1) for t in range(shards)]
    same_core = [list(range(c, shards, 2)) for c in range(2)]

    blocks, places, first = ring_gather(input_rows, shards)
    adapter_up, adapter_down, first = lax.optimization_barrier((adapter_up, adapter_down, first))
    mine, other = split_for_pair(adapter_up[0], (position & 1)[None], chips)
    other = lax.ppermute(other, "tensor", sibling)
    down_pair = (adapter_down[0], lax.ppermute(adapter_down[0], "tensor", sibling))
    gain, choose, fixed, code, begin, full = describe(
        ranks, adapter_slot, segment_lengths, segment_adapter, position[None], total_rows, limit
    )
    fullest = largest_over_groups(full)
    rows, coeff = collect_rows(blocks, places, down_pair, gain)

    def exchange(low, count):
        payload = build_payload(choose, fixed, coeff, mine, other, low, count)
        return lax.all_to_all(
            payload,
            "tensor",
            split_axis=0,
            concat_axis=0,
            axis_index_groups=same_core,
            tiled=True,
        )

    incoming = exchange(0, FIRST_ROWS)
    base = jnp.dot(rows, up_weight, preferred_element_type=jnp.float32)
    coeff, fullest, base = lax.optimization_barrier((coeff, fullest, base))
    own = coeff[:, :rank_width] + coeff[:, rank_width:]
    coeffs = [own]
    for step in range(1, chips):
        hop = [(t, (t + 2 * step) % shards) for t in range(shards)]
        coeffs.append(lax.ppermute(own, "tensor", hop))
    rest = limit - FIRST_ROWS
    extra = lax.cond(
        fullest[0] > FIRST_ROWS,
        lambda: exchange(FIRST_ROWS, rest),
        lambda: jnp.zeros((chips, rest, up_weight.shape[1]), adapter_up.dtype),
    )
    return combine(base, code, begin, fullest, coeffs, incoming, extra)


def gathered(input_rows, up_weight, adapter_down, adapter_up, slot_row, row_rank):
    shards = lax.axis_size("tensor")
    position = lax.axis_index("tensor")
    total_rows = input_rows.shape[0] * shards
    stored, rank_width, hidden = adapter_up.shape
    width = hidden // shards
    slots = shards * stored
    outgoing = jnp.stack(
        [adapter_up[:, :, i * width : (i + 1) * width] for i in range(shards)], axis=0
    )
    incoming = lax.all_to_all(outgoing, "tensor", split_axis=0, concat_axis=0, tiled=True)
    rows = lax.all_gather(input_rows, "tensor", axis=0, tiled=True)
    shrink = jnp.einsum("gf,ojf->ogj", rows, adapter_down, preferred_element_type=jnp.float32)
    own = position * stored + jnp.arange(stored, dtype=jnp.int32)
    inside = jnp.arange(rank_width, dtype=jnp.int32)[None, :] < row_rank[:, None]
    keep = (slot_row[None, :] == own[:, None])[:, :, None] & inside[None]
    scale = ADAPTER_ALPHA / row_rank.astype(jnp.float32)
    own_coeff = jnp.where(keep, shrink * scale[None, :, None], 0.0).astype(jnp.bfloat16)
    base = jnp.dot(rows, up_weight, preferred_element_type=jnp.float32)
    own_coeff, base = lax.optimization_barrier((own_coeff, base))
    coeff = lax.all_gather(own_coeff, "tensor", axis=0, tiled=True)
    placed = coeff.transpose(1, 0, 2).reshape(total_rows, slots * rank_width)
    factors = incoming.reshape(slots * rank_width, width)
    term = jnp.dot(placed, factors, preferred_element_type=jnp.float32)
    return (base + term).astype(jnp.bfloat16)


def on_device(
    input_rows,
    up_weight,
    adapter_down,
    adapter_up,
    ranks,
    adapter_slot,
    segment_lengths,
    segment_adapter,
):
    shards = lax.axis_size("tensor")
    stored, rank_width, _ = adapter_up.shape
    tiled = up_weight.shape[1] % 128 == 0 and input_rows.shape[0] % 16 == 0 and rank_width == 64
    if shards == POOLED_SHARDS and stored == 1 and tiled:
        return pooled(
            input_rows,
            up_weight,
            adapter_down,
            adapter_up,
            ranks,
            adapter_slot,
            segment_lengths,
            segment_adapter,
        )
    slot_row, row_rank = row_tables(
        input_rows.shape[0] * shards, ranks, adapter_slot, segment_lengths, segment_adapter
    )
    return gathered(input_rows, up_weight, adapter_down, adapter_up, slot_row, row_rank)


def solution(mesh):
    placed = (
        P(("groups", "tensor"), None),
        P(None, "tensor"),
        P(("groups", "tensor"), None, None),
        P(("groups", "tensor"), None, None),
        P("groups"),
        P("groups"),
        P("groups"),
        P("groups"),
    )
    return jax.shard_map(
        on_device, mesh=mesh, in_specs=placed, out_specs=P("groups", "tensor"), check_vma=False
    )
```

profile of v0, /device:TPU:0, one launch (start us, length us, event | category | flops | bytes accessed | tf_op | source)
XLA Modules:
  0.0 145.6 jit_solution(12071783914653239354)
XLA Ops:
  0.0 3.0 %collective-permute-start.1 = (bf16[16,8192]{1,0:T(8,128)(2,1)}, bf16[16,8192]{1,0:T(8,128)(2,1)S(1)}, u32[]{:S(2)}, u32[]{:S(2)}) collective-permute-start(bf16[16,8192]{1,0:T(8,128)(2,1)} %refs_0_.1), channel_id=1, source_target_pairs={{0,4},{1,5},{4,8},{5,9},{8,12},{9,13},{12,14},{13,15},{14,10},{15,... | collective-permute-start | bytes 786440 | tf_op jit(solution)/shard_map/ppermute | solution.py:345
  3.0 6.5 %collective-permute-done.1.refs_2_ = bf16[16,8192]{1,0:T(8,128)(2,1)S(1)} collective-permute-done((bf16[16,8192]{1,0:T(8,128)(2,1)}, bf16[16,8192]{1,0:T(8,128)(2,1)S(1)}, u32[]{:S(2)}, u32[]{:S(2)}) %collective-permute-start.1) | collective-permute-done | bytes 262176 | tf_op jit(solution)/shard_map/ppermute | solution.py:345
  9.5 1.8 %collective-permute-start.5 = (bf16[16,8192]{1,0:T(8,128)(2,1)S(1)}, bf16[16,8192]{1,0:T(8,128)(2,1)S(1)}, u32[]{:S(2)}, u32[]{:S(2)}) collective-permute-start(bf16[16,8192]{1,0:T(8,128)(2,1)S(1)} %collective-permute-done.1.refs_2_), channel_id=1, source_target_pairs={{0,4},{1,5},{4,8},{5,9},{8,12},{9,13},{12,14},{13,15},{14,10},{15,... | collective-permute-start | bytes 786440 | tf_op jit(solution)/shard_map/ppermute | solution.py:345
  14.4 1.6 %shard_map.91 = (f32[256,128]{1,0:T(8,128)S(1)}, bf16[128,256]{1,0:T(8,128)(2,1)}, bf16[128,128]{1,0:T(8,128)(2,1)}, s32[256,128]{1,0:T(8,128)S(1)}, s32[16]{0:T(128)S(1)}, /*index=5*/s32[1]{0:T(128)}) custom-call(s32[16]{0:T(128)S(1)} %copy-done.8, s32[16]{0:T(128)S(1)} %copy-done.9, s32[16]{0:T(128)S(1)} %copy-done.10, s32[16]{0:T(128)S(1)} %copy-done.11, ...), custom_call_target="tpu_custom_call" | custom-call | flops 6553600 | bytes 524288 | tf_op jit(solution)/shard_map/pallas_call | solution.py:134
  16.6 1.5 %collective-permute-start.16 = (s32[1]{0:T(128)}, s32[1]{0:T(128)}, u32[]{:S(2)}, u32[]{:S(2)}) collective-permute-start(s32[1]{0:T(128)} %get-tuple-element.42), channel_id=1, source_target_pairs={{0,16},{16,0},{1,17},{17,1},{2,18},{18,2},{3,19},{19,3},{4,20},{20... | collective-permute-start | bytes 20 | tf_op jit(solution)/shard_map/ppermute | solution.py:363
  18.6 1.8 %collective-permute-done.16 = s32[1]{0:T(128)} collective-permute-done((s32[1]{0:T(128)}, s32[1]{0:T(128)}, u32[]{:S(2)}, u32[]{:S(2)}) %collective-permute-start.16) | collective-permute-done | bytes 36 | tf_op jit(solution)/shard_map/ppermute | solution.py:363
  20.3 1.6 %collective-permute-start.9 = (bf16[16,8192]{1,0:T(8,128)(2,1)S(1)}, bf16[16,8192]{1,0:T(8,128)(2,1)S(1)}, u32[]{:S(2)}, u32[]{:S(2)}) collective-permute-start(bf16[16,8192]{1,0:T(8,128)(2,1)S(1)} %collective-permute-done.5.refs_6_), channel_id=1, source_target_pairs={{0,4},{1,5},{4,8},{5,9},{8,12},{9,13},{12,14},{13,15},{14,10},{15,... | collective-permute-start | bytes 786440 | tf_op jit(solution)/shard_map/ppermute | solution.py:345
  22.1 3.9 %collective-permute-done.7.refs_8_ = bf16[16,8192]{1,0:T(8,128)(2,1)S(1)} collective-permute-done((bf16[16,8192]{1,0:T(8,128)(2,1)S(1)}, bf16[16,8192]{1,0:T(8,128)(2,1)S(1)}, u32[]{:S(2)}, u32[]{:S(2)}) %collective-permute-start.7) | collective-permute-done | bytes 262176 | tf_op jit(solution)/shard_map/ppermute | solution.py:347
  26.5 2.5 %collective-permute-done.9.refs_10_ = bf16[16,8192]{1,0:T(8,128)(2,1)S(1)} collective-permute-done((bf16[16,8192]{1,0:T(8,128)(2,1)S(1)}, bf16[16,8192]{1,0:T(8,128)(2,1)S(1)}, u32[]{:S(2)}, u32[]{:S(2)}) %collective-permute-start.9) | collective-permute-done | bytes 262176 | tf_op jit(solution)/shard_map/ppermute | solution.py:345
  29.0 1.6 %collective-permute-start.13 = (bf16[16,8192]{1,0:T(8,128)(2,1)S(1)}, bf16[16,8192]{1,0:T(8,128)(2,1)}, u32[]{:S(2)}, u32[]{:S(2)}) collective-permute-start(bf16[16,8192]{1,0:T(8,128)(2,1)S(1)} %collective-permute-done.9.refs_10_), channel_id=1, source_target_pairs={{0,4},{1,5},{4,8},{5,9},{8,12},{9,13},{12,14},{13,15},{14,10},{15,... | collective-permute-start | bytes 786440 | tf_op jit(solution)/shard_map/ppermute | solution.py:345
  30.6 2.5 %collective-permute-done.11.refs_12_ = bf16[16,8192]{1,0:T(8,128)(2,1)S(1)} collective-permute-done((bf16[16,8192]{1,0:T(8,128)(2,1)S(1)}, bf16[16,8192]{1,0:T(8,128)(2,1)S(1)}, u32[]{:S(2)}, u32[]{:S(2)}) %collective-permute-start.11) | collective-permute-done | bytes 262176 | tf_op jit(solution)/shard_map/ppermute | solution.py:347
  33.1 0.7 copy-done.4
  34.3 2.8 %collective-permute-done.13.refs_14_ = bf16[16,8192]{1,0:T(8,128)(2,1)} collective-permute-done((bf16[16,8192]{1,0:T(8,128)(2,1)S(1)}, bf16[16,8192]{1,0:T(8,128)(2,1)}, u32[]{:S(2)}, u32[]{:S(2)}) %collective-permute-start.13) | collective-permute-done | bytes 262176 | tf_op jit(solution)/shard_map/ppermute | solution.py:345
  37.1 0.7 dynamic-slice_bitcast_fusion.places_ref
  39.1 2.0 %copy-done = bf16[1,64,28672]{2,1,0:T(8,128)(2,1)S(1)} copy-done((bf16[1,64,28672]{2,1,0:T(8,128)(2,1)S(1)}, bf16[1,64,28672]{2,1,0:T(8,128)(2,1)}, u32[]{:S(2)}) %copy-start) | copy-done | bytes 3670040
  41.1 2.1 %shard_map.93 = (bf16[8,64,1792]{2,1,0:T(8,128)(2,1)}, bf16[8,64,1792]{2,1,0:T(8,128)(2,1)S(1)}) custom-call(s32[1]{0:T(128)} %bitcast.3.core_ref, bf16[64,28672]{1,0:T(8,128)(2,1)S(1)} %bitcast.9), custom_call_target="tpu_custom_call" | custom-call | bytes 7340032 | tf_op jit(solution)/shard_map/pallas_call | solution.py:56
  43.8 7.0 %shard_map.92 = (bf16[256,8192]{1,0:T(8,128)(2,1)S(1)}, bf16[256,128]{1,0:T(8,128)(2,1)}) custom-call(s32[16]{0:T(128)S(1)} %dynamic-slice_bitcast_fusion.places_ref, f32[256,128]{1,0:T(8,128)S(1)} %get-tuple-element.39.gain_ref, bf16[16,8192]{1,0:T(8,128)(2,1)S(1)} %copy-done.3, bf16[16,8192]{1,0:T(8,128)(2,1)S(1)} %collective-permute-done.refs_1_, ...), custom_call_target="tpu_custom_call" | custom-call | flops 536870912 | bytes 8388608 | tf_op jit(solution)/shard_map/pallas_call | solution.py:200
  50.9 14.7 %fusion.base_ref = f32[256,1792]{1,0:T(8,128)} fusion(bf16[256,8192]{1,0:T(8,128)(2,1)S(1)} %get-tuple-element.43, bf16[8192,1792]{1,0:T(8,128)(2,1)} %param.12), kind=kOutput, calls=%fused_computation.2 | convolution fusion | flops 7516192768 | bytes 35389440 | tf_op jit(solution)/shard_map/dot_general | solution.py:410
  65.7 1.2 copy-done.13
  67.0 5.4 %shard_map.94 = bf16[8,80,1792]{2,1,0:T(8,128)(2,1)} custom-call(bf16[128,256]{1,0:T(8,128)(2,1)S(1)} %copy-done.16, bf16[128,128]{1,0:T(8,128)(2,1)S(1)} %copy-done.17, bf16[256,128]{1,0:T(8,128)(2,1)S(1)} %copy-done.15, bf16[8,64,1792]{2,1,0:T(8,128)(2,1)S(1)} %copy-done.12, bf16[8,64,1792]{2,1,0:T(8,128)(2,1)} %copy-done.13), custom_call_target="tpu_custom_call" | custom-call | flops 293601280 | bytes 5963776 | tf_op jit(solution)/shard_map/pallas_call | solution.py:238
  72.5 5.0 %all-to-all-start.1 = ((bf16[8,80,1792]{2,1,0:T(8,128)(2,1)}), bf16[8,80,1792]{2,1,0:T(8,128)(2,1)S(1)}, u32[]{:S(2)}, u32[]{:S(2)}) async-start(bf16[8,80,1792]{2,1,0:T(8,128)(2,1)} %shard_map.94), calls=%async_computation.1 | async-start | bytes 4587520 | tf_op jit(solution)/shard_map/all_to_all | solution.py:400
  77.5 2.1 %collective-permute-start.17 = (bf16[256,64]{1,0:T(8,128)(2,1)S(1)}, bf16[256,64]{1,0:T(8,128)(2,1)S(1)}, u32[]{:S(2)}, u32[]{:S(2)}) collective-permute-start(bf16[256,64]{1,0:T(8,128)(2,1)S(1)} %slice_add_fusion.refs_0_), channel_id=1, source_target_pairs={{0,2},{1,3},{2,4},{3,5},{4,6},{5,7},{6,8},{7,9},{8,10},{9,11},{10,... | collective-permute-start | bytes 98312 | tf_op jit(solution)/shard_map/ppermute | solution.py:416
  79.6 1.5 %collective-permute-start.18 = (bf16[256,64]{1,0:T(8,128)(2,1)S(1)}, bf16[256,64]{1,0:T(8,128)(2,1)S(1)}, u32[]{:S(2)}, u32[]{:S(2)}) collective-permute-start(bf16[256,64]{1,0:T(8,128)(2,1)S(1)} %slice_add_fusion.refs_0_), channel_id=1, source_target_pairs={{0,4},{1,5},{2,6},{3,7},{4,8},{5,9},{6,10},{7,11},{8,12},{9,13},{1... | collective-permute-start | bytes 98312 | tf_op jit(solution)/shard_map/ppermute | solution.py:416
  81.0 2.4 %collective-permute-start.19 = (bf16[256,64]{1,0:T(8,128)(2,1)S(1)}, bf16[256,64]{1,0:T(8,128)(2,1)S(1)}, u32[]{:S(2)}, u32[]{:S(2)}) collective-permute-start(bf16[256,64]{1,0:T(8,128)(2,1)S(1)} %slice_add_fusion.refs_0_), channel_id=1, source_target_pairs={{0,6},{1,7},{2,8},{3,9},{4,10},{5,11},{6,12},{7,13},{8,14},{9,15},... | collective-permute-start | bytes 98312 | tf_op jit(solution)/shard_map/ppermute | solution.py:416
  83.4 1.5 %collective-permute-start.20 = (bf16[256,64]{1,0:T(8,128)(2,1)S(1)}, bf16[256,64]{1,0:T(8,128)(2,1)S(1)}, u32[]{:S(2)}, u32[]{:S(2)}) collective-permute-start(bf16[256,64]{1,0:T(8,128)(2,1)S(1)} %slice_add_fusion.refs_0_), channel_id=1, source_target_pairs={{0,8},{1,9},{2,10},{3,11},{4,12},{5,13},{6,14},{7,15},{8,0},{9,1},... | collective-permute-start | bytes 98312 | tf_op jit(solution)/shard_map/ppermute | solution.py:416
  84.9 2.4 %collective-permute-start.21 = (bf16[256,64]{1,0:T(8,128)(2,1)S(1)}, bf16[256,64]{1,0:T(8,128)(2,1)S(1)}, u32[]{:S(2)}, u32[]{:S(2)}) collective-permute-start(bf16[256,64]{1,0:T(8,128)(2,1)S(1)} %slice_add_fusion.refs_0_), channel_id=1, source_target_pairs={{0,10},{1,11},{2,12},{3,13},{4,14},{5,15},{6,0},{7,1},{8,2},{9,3},... | collective-permute-start | bytes 98312 | tf_op jit(solution)/shard_map/ppermute | solution.py:416
  87.2 35.1 %collective-permute-done.17.refs_1_ = bf16[256,64]{1,0:T(8,128)(2,1)S(1)} collective-permute-done((bf16[256,64]{1,0:T(8,128)(2,1)S(1)}, bf16[256,64]{1,0:T(8,128)(2,1)S(1)}, u32[]{:S(2)}, u32[]{:S(2)}) %collective-permute-start.17) | collective-permute-done | bytes 32800 | tf_op jit(solution)/shard_map/ppermute | solution.py:416
  122.3 0.9 collective-permute-start.23
  123.2 15.8 %collective-permute-done.19.refs_3_ = bf16[256,64]{1,0:T(8,128)(2,1)S(1)} collective-permute-done((bf16[256,64]{1,0:T(8,128)(2,1)S(1)}, bf16[256,64]{1,0:T(8,128)(2,1)S(1)}, u32[]{:S(2)}, u32[]{:S(2)}) %collective-permute-start.19) | collective-permute-done | bytes 32800 | tf_op jit(solution)/shard_map/ppermute | solution.py:416
  139.0 0.8 collective-permute-done.22.refs_6_
  139.8 1.5 %copy-done.1 = f32[256,1792]{1,0:T(8,128)S(1)} copy-done((f32[256,1792]{1,0:T(8,128)S(1)}, f32[256,1792]{1,0:T(8,128)}, u32[]{:S(2)}) %copy-start.1) | copy-done | bytes 1835032
  141.3 4.3 %shard_map.95 = bf16[256,1792]{1,0:T(8,128)(2,1)} custom-call(s32[16]{0:T(128)S(1)} %get-tuple-element.38.begin_ref, s32[1]{0:T(128)S(6)} %max.3.more_ref, f32[256,1792]{1,0:T(8,128)S(1)} %copy-done.1, s32[256,128]{1,0:T(8,128)S(1)} %copy-done.7, bf16[256,64]{1,0:T(8,128)(2,1)S(1)} %slice_add_fusion.refs_0_, ...), custom_call_target="tpu_custom_call" | custom-call | flops 1879048192 | bytes 6422528 | tf_op jit(solution)/shard_map/pallas_call | solution.py:317
  (66 shorter events, 6.4 us)
Async XLA Ops:
  0.0 9.5 %collective-permute-start.1 = (bf16[16,8192]{1,0:T(8,128)(2,1)}, bf16[16,8192]{1,0:T(8,128)(2,1)S(1)}, u32[]{:S(2)}, u32[]{:S(2)}) collective-permute-start(bf16[16,8192]{1,0:T(8,128)(2,1)} %refs_0_.1), channel_id=1, source_target_pairs={{0,4},{1,5},{4,8},{5,9},{8,12},{9,13},{12,14},{13,15},{14,10},{15,... | collective-permute-start | bytes 786440 | tf_op jit(solution)/shard_map/ppermute | solution.py:345
  3.0 15.1 %collective-permute-start.3 = (bf16[16,8192]{1,0:T(8,128)(2,1)}, bf16[16,8192]{1,0:T(8,128)(2,1)S(1)}, u32[]{:S(2)}, u32[]{:S(2)}) collective-permute-start(bf16[16,8192]{1,0:T(8,128)(2,1)} %refs_0_.1), channel_id=1, source_target_pairs={{4,0},{5,1},{8,4},{9,5},{12,8},{13,9},{14,12},{15,13},{10,14},{11,... | collective-permute-start | bytes 786440 | tf_op jit(solution)/shard_map/ppermute | solution.py:347
  9.5 10.8 %collective-permute-start.5 = (bf16[16,8192]{1,0:T(8,128)(2,1)S(1)}, bf16[16,8192]{1,0:T(8,128)(2,1)S(1)}, u32[]{:S(2)}, u32[]{:S(2)}) collective-permute-start(bf16[16,8192]{1,0:T(8,128)(2,1)S(1)} %collective-permute-done.1.refs_2_), channel_id=1, source_target_pairs={{0,4},{1,5},{4,8},{5,9},{8,12},{9,13},{12,14},{13,15},{14,10},{15,... | collective-permute-start | bytes 786440 | tf_op jit(solution)/shard_map/ppermute | solution.py:345
  11.3 32.5 %collective-permute-start.15 = (bf16[64,8192]{1,0:T(8,128)(2,1)}, bf16[64,8192]{1,0:T(8,128)(2,1)S(1)}, u32[]{:S(2)}, u32[]{:S(2)}) collective-permute-start(bf16[64,8192]{1,0:T(8,128)(2,1)} %bitcast.10), channel_id=1, source_target_pairs={{0,1},{1,0},{2,3},{3,2},{4,5},{5,4},{6,7},{7,6},{8,9},{9,8},{10,11... | collective-permute-start | bytes 3145736 | tf_op jit(solution)/shard_map/ppermute | solution.py:391
  11.3 10.6 %collective-permute-start = (bf16[16,8192]{1,0:T(8,128)(2,1)}, bf16[16,8192]{1,0:T(8,128)(2,1)S(1)}, u32[]{:S(2)}, u32[]{:S(2)}) collective-permute-start(bf16[16,8192]{1,0:T(8,128)(2,1)} %refs_0_.1), channel_id=1, source_target_pairs={{0,1},{1,0},{2,3},{3,2},{4,5},{5,4},{6,7},{7,6},{8,9},{9,8},{10,11... | collective-permute-start | bytes 786440 | tf_op jit(solution)/shard_map/ppermute | solution.py:350
  16.6 3.7 %collective-permute-start.16 = (s32[1]{0:T(128)}, s32[1]{0:T(128)}, u32[]{:S(2)}, u32[]{:S(2)}) collective-permute-start(s32[1]{0:T(128)} %get-tuple-element.42), channel_id=1, source_target_pairs={{0,16},{16,0},{1,17},{17,1},{2,18},{18,2},{3,19},{19,3},{4,20},{20... | collective-permute-start | bytes 20 | tf_op jit(solution)/shard_map/ppermute | solution.py:363
  18.1 7.9 %collective-permute-start.7 = (bf16[16,8192]{1,0:T(8,128)(2,1)S(1)}, bf16[16,8192]{1,0:T(8,128)(2,1)S(1)}, u32[]{:S(2)}, u32[]{:S(2)}) collective-permute-start(bf16[16,8192]{1,0:T(8,128)(2,1)S(1)} %collective-permute-done.3.refs_4_), channel_id=1, source_target_pairs={{4,0},{5,1},{8,4},{9,5},{12,8},{13,9},{14,12},{15,13},{10,14},{11,... | collective-permute-start | bytes 786440 | tf_op jit(solution)/shard_map/ppermute | solution.py:347
  20.3 6.2 %collective-permute-start.2 = (bf16[16,8192]{1,0:T(8,128)(2,1)S(1)}, bf16[16,8192]{1,0:T(8,128)(2,1)S(1)}, u32[]{:S(2)}, u32[]{:S(2)}) collective-permute-start(bf16[16,8192]{1,0:T(8,128)(2,1)S(1)} %collective-permute-done.1.refs_2_), channel_id=1, source_target_pairs={{0,1},{1,0},{2,3},{3,2},{4,5},{5,4},{6,7},{7,6},{8,9},{9,8},{10,11... | collective-permute-start | bytes 786440 | tf_op jit(solution)/shard_map/ppermute | solution.py:350
  20.3 8.7 %collective-permute-start.9 = (bf16[16,8192]{1,0:T(8,128)(2,1)S(1)}, bf16[16,8192]{1,0:T(8,128)(2,1)S(1)}, u32[]{:S(2)}, u32[]{:S(2)}) collective-permute-start(bf16[16,8192]{1,0:T(8,128)(2,1)S(1)} %collective-permute-done.5.refs_6_), channel_id=1, source_target_pairs={{0,4},{1,5},{4,8},{5,9},{8,12},{9,13},{12,14},{13,15},{14,10},{15,... | collective-permute-start | bytes 786440 | tf_op jit(solution)/shard_map/ppermute | solution.py:345
  21.9 8.7 %collective-permute-start.4 = (bf16[16,8192]{1,0:T(8,128)(2,1)S(1)}, bf16[16,8192]{1,0:T(8,128)(2,1)S(1)}, u32[]{:S(2)}, u32[]{:S(2)}) collective-permute-start(bf16[16,8192]{1,0:T(8,128)(2,1)S(1)} %collective-permute-done.3.refs_4_), channel_id=1, source_target_pairs={{0,1},{1,0},{2,3},{3,2},{4,5},{5,4},{6,7},{7,6},{8,9},{9,8},{10,11... | collective-permute-start | bytes 786440 | tf_op jit(solution)/shard_map/ppermute | solution.py:350
  26.0 7.0 %collective-permute-start.11 = (bf16[16,8192]{1,0:T(8,128)(2,1)S(1)}, bf16[16,8192]{1,0:T(8,128)(2,1)S(1)}, u32[]{:S(2)}, u32[]{:S(2)}) collective-permute-start(bf16[16,8192]{1,0:T(8,128)(2,1)S(1)} %collective-permute-done.7.refs_8_), channel_id=1, source_target_pairs={{4,0},{5,1},{8,4},{9,5},{12,8},{13,9},{14,12},{15,13},{10,14},{11,... | collective-permute-start | bytes 786440 | tf_op jit(solution)/shard_map/ppermute | solution.py:347
  26.5 6.6 %collective-permute-start.6 = (bf16[16,8192]{1,0:T(8,128)(2,1)S(1)}, bf16[16,8192]{1,0:T(8,128)(2,1)S(1)}, u32[]{:S(2)}, u32[]{:S(2)}) collective-permute-start(bf16[16,8192]{1,0:T(8,128)(2,1)S(1)} %collective-permute-done.5.refs_6_), channel_id=1, source_target_pairs={{0,1},{1,0},{2,3},{3,2},{4,5},{5,4},{6,7},{7,6},{8,9},{9,8},{10,11... | collective-permute-start | bytes 786440 | tf_op jit(solution)/shard_map/ppermute | solution.py:350
  29.0 8.0 %collective-permute-start.13 = (bf16[16,8192]{1,0:T(8,128)(2,1)S(1)}, bf16[16,8192]{1,0:T(8,128)(2,1)}, u32[]{:S(2)}, u32[]{:S(2)}) collective-permute-start(bf16[16,8192]{1,0:T(8,128)(2,1)S(1)} %collective-permute-done.9.refs_10_), channel_id=1, source_target_pairs={{0,4},{1,5},{4,8},{5,9},{8,12},{9,13},{12,14},{13,15},{14,10},{15,... | collective-permute-start | bytes 786440 | tf_op jit(solution)/shard_map/ppermute | solution.py:345
  30.6 12.6 %collective-permute-start.8 = (bf16[16,8192]{1,0:T(8,128)(2,1)S(1)}, bf16[16,8192]{1,0:T(8,128)(2,1)}, u32[]{:S(2)}, u32[]{:S(2)}) collective-permute-start(bf16[16,8192]{1,0:T(8,128)(2,1)S(1)} %collective-permute-done.7.refs_8_), channel_id=1, source_target_pairs={{0,1},{1,0},{2,3},{3,2},{4,5},{5,4},{6,7},{7,6},{8,9},{9,8},{10,11... | collective-permute-start | bytes 786440 | tf_op jit(solution)/shard_map/ppermute | solution.py:350
  33.1 10.7 %collective-permute-start.10 = (bf16[16,8192]{1,0:T(8,128)(2,1)S(1)}, bf16[16,8192]{1,0:T(8,128)(2,1)}, u32[]{:S(2)}, u32[]{:S(2)}) collective-permute-start(bf16[16,8192]{1,0:T(8,128)(2,1)S(1)} %collective-permute-done.9.refs_10_), channel_id=1, source_target_pairs={{0,1},{1,0},{2,3},{3,2},{4,5},{5,4},{6,7},{7,6},{8,9},{9,8},{10,11... | collective-permute-start | bytes 786440 | tf_op jit(solution)/shard_map/ppermute | solution.py:350
  33.8 10.0 %collective-permute-start.12 = (bf16[16,8192]{1,0:T(8,128)(2,1)S(1)}, bf16[16,8192]{1,0:T(8,128)(2,1)}, u32[]{:S(2)}, u32[]{:S(2)}) collective-permute-start(bf16[16,8192]{1,0:T(8,128)(2,1)S(1)} %collective-permute-done.11.refs_12_), channel_id=1, source_target_pairs={{0,1},{1,0},{2,3},{3,2},{4,5},{5,4},{6,7},{7,6},{8,9},{9,8},{10,11... | collective-permute-start | bytes 786440 | tf_op jit(solution)/shard_map/ppermute | solution.py:350
  37.1 6.7 %collective-permute-start.14 = (bf16[16,8192]{1,0:T(8,128)(2,1)}, bf16[16,8192]{1,0:T(8,128)(2,1)}, u32[]{:S(2)}, u32[]{:S(2)}) collective-permute-start(bf16[16,8192]{1,0:T(8,128)(2,1)} %collective-permute-done.13.refs_14_), channel_id=1, source_target_pairs={{0,1},{1,0},{2,3},{3,2},{4,5},{5,4},{6,7},{7,6},{8,9},{9,8},{10,11... | collective-permute-start | bytes 786440 | tf_op jit(solution)/shard_map/ppermute | solution.py:350
  43.2 22.4 %collective-permute-start.24 = (bf16[8,64,1792]{2,1,0:T(8,128)(2,1)S(1)}, bf16[8,64,1792]{2,1,0:T(8,128)(2,1)S(1)}, u32[]{:S(2)}, u32[]{:S(2)}) collective-permute-start(bf16[8,64,1792]{2,1,0:T(8,128)(2,1)S(1)} %get-tuple-element.52), channel_id=1, source_target_pairs={{0,1},{1,0},{2,3},{3,2},{4,5},{5,4},{6,7},{7,6},{8,9},{9,8},{10,11... | collective-permute-start | bytes 5505032 | tf_op jit(solution)/shard_map/ppermute | solution.py:390
  50.9 14.8 %copy-start.12 = (bf16[8,64,1792]{2,1,0:T(8,128)(2,1)S(1)}, bf16[8,64,1792]{2,1,0:T(8,128)(2,1)}, u32[]{:S(2)}) copy-start(bf16[8,64,1792]{2,1,0:T(8,128)(2,1)} %get-tuple-element.51.mine_ref) | copy-start | bytes 5505028
  50.9 14.7 %copy-start.15 = (bf16[256,128]{1,0:T(8,128)(2,1)S(1)}, bf16[256,128]{1,0:T(8,128)(2,1)}, u32[]{:S(2)}) copy-start(bf16[256,128]{1,0:T(8,128)(2,1)} %get-tuple-element.47.coeff_ref) | copy-start | bytes 196612
  50.9 14.7 %copy-start.16 = (bf16[128,256]{1,0:T(8,128)(2,1)S(1)}, bf16[128,256]{1,0:T(8,128)(2,1)}, u32[]{:S(2)}) copy-start(bf16[128,256]{1,0:T(8,128)(2,1)} %get-tuple-element.48.choose_ref) | copy-start | bytes 196612
  50.9 14.7 %copy-start.17 = (bf16[128,128]{1,0:T(8,128)(2,1)S(1)}, bf16[128,128]{1,0:T(8,128)(2,1)}, u32[]{:S(2)}) copy-start(bf16[128,128]{1,0:T(8,128)(2,1)} %get-tuple-element.49.fixed_ref) | copy-start | bytes 98308
  67.0 5.4 %copy-start.14 = (bf16[8,48,1792]{2,1,0:T(8,128)(2,1)}, bf16[8,48,1792]{2,1,0:T(8,128)(2,1)S(1)}, u32[]{:S(2)}) copy-start(bf16[8,48,1792]{2,1,0:T(8,128)(2,1)S(1)} %get-tuple-element.53.refs_9_) | copy-start | bytes 4128772
  72.5 67.3 %copy-start.7 = (s32[256,128]{1,0:T(8,128)S(1)}, s32[256,128]{1,0:T(8,128)}, u32[]{:S(2)}) copy-start(s32[256,128]{1,0:T(8,128)} %copy-done.6) | copy-start | bytes 393220
  72.5 67.3 %all-to-all-start.1 = ((bf16[8,80,1792]{2,1,0:T(8,128)(2,1)}), bf16[8,80,1792]{2,1,0:T(8,128)(2,1)S(1)}, u32[]{:S(2)}, u32[]{:S(2)}) async-start(bf16[8,80,1792]{2,1,0:T(8,128)(2,1)} %shard_map.94), calls=%async_computation.1 | async-start | bytes 4587520 | tf_op jit(solution)/shard_map/all_to_all | solution.py:400
  77.5 44.8 %collective-permute-start.17 = (bf16[256,64]{1,0:T(8,128)(2,1)S(1)}, bf16[256,64]{1,0:T(8,128)(2,1)S(1)}, u32[]{:S(2)}, u32[]{:S(2)}) collective-permute-start(bf16[256,64]{1,0:T(8,128)(2,1)S(1)} %slice_add_fusion.refs_0_), channel_id=1, source_target_pairs={{0,2},{1,3},{2,4},{3,5},{4,6},{5,7},{6,8},{7,9},{8,10},{9,11},{10,... | collective-permute-start | bytes 98312 | tf_op jit(solution)/shard_map/ppermute | solution.py:416
  79.6 42.7 %collective-permute-start.18 = (bf16[256,64]{1,0:T(8,128)(2,1)S(1)}, bf16[256,64]{1,0:T(8,128)(2,1)S(1)}, u32[]{:S(2)}, u32[]{:S(2)}) collective-permute-start(bf16[256,64]{1,0:T(8,128)(2,1)S(1)} %slice_add_fusion.refs_0_), channel_id=1, source_target_pairs={{0,4},{1,5},{2,6},{3,7},{4,8},{5,9},{6,10},{7,11},{8,12},{9,13},{1... | collective-permute-start | bytes 98312 | tf_op jit(solution)/shard_map/ppermute | solution.py:416
  81.0 58.0 %collective-permute-start.19 = (bf16[256,64]{1,0:T(8,128)(2,1)S(1)}, bf16[256,64]{1,0:T(8,128)(2,1)S(1)}, u32[]{:S(2)}, u32[]{:S(2)}) collective-permute-start(bf16[256,64]{1,0:T(8,128)(2,1)S(1)} %slice_add_fusion.refs_0_), channel_id=1, source_target_pairs={{0,6},{1,7},{2,8},{3,9},{4,10},{5,11},{6,12},{7,13},{8,14},{9,15},... | collective-permute-start | bytes 98312 | tf_op jit(solution)/shard_map/ppermute | solution.py:416
  83.4 55.6 %collective-permute-start.20 = (bf16[256,64]{1,0:T(8,128)(2,1)S(1)}, bf16[256,64]{1,0:T(8,128)(2,1)S(1)}, u32[]{:S(2)}, u32[]{:S(2)}) collective-permute-start(bf16[256,64]{1,0:T(8,128)(2,1)S(1)} %slice_add_fusion.refs_0_), channel_id=1, source_target_pairs={{0,8},{1,9},{2,10},{3,11},{4,12},{5,13},{6,14},{7,15},{8,0},{9,1},... | collective-permute-start | bytes 98312 | tf_op jit(solution)/shard_map/ppermute | solution.py:416
  84.9 54.1 %collective-permute-start.21 = (bf16[256,64]{1,0:T(8,128)(2,1)S(1)}, bf16[256,64]{1,0:T(8,128)(2,1)S(1)}, u32[]{:S(2)}, u32[]{:S(2)}) collective-permute-start(bf16[256,64]{1,0:T(8,128)(2,1)S(1)} %slice_add_fusion.refs_0_), channel_id=1, source_target_pairs={{0,10},{1,11},{2,12},{3,13},{4,14},{5,15},{6,0},{7,1},{8,2},{9,3},... | collective-permute-start | bytes 98312 | tf_op jit(solution)/shard_map/ppermute | solution.py:416
  122.3 17.5 %collective-permute-start.22 = (bf16[256,64]{1,0:T(8,128)(2,1)S(1)}, bf16[256,64]{1,0:T(8,128)(2,1)S(1)}, u32[]{:S(2)}, u32[]{:S(2)}) collective-permute-start(bf16[256,64]{1,0:T(8,128)(2,1)S(1)} %slice_add_fusion.refs_0_), channel_id=1, source_target_pairs={{0,12},{1,13},{2,14},{3,15},{4,0},{5,1},{6,2},{7,3},{8,4},{9,5},{1... | collective-permute-start | bytes 98312 | tf_op jit(solution)/shard_map/ppermute | solution.py:416
  122.3 17.5 %collective-permute-start.23 = (bf16[256,64]{1,0:T(8,128)(2,1)S(1)}, bf16[256,64]{1,0:T(8,128)(2,1)S(1)}, u32[]{:S(2)}, u32[]{:S(2)}) collective-permute-start(bf16[256,64]{1,0:T(8,128)(2,1)S(1)} %slice_add_fusion.refs_0_), channel_id=1, source_target_pairs={{0,14},{1,15},{2,0},{3,1},{4,2},{5,3},{6,4},{7,5},{8,6},{9,7},{10,... | collective-permute-start | bytes 98312 | tf_op jit(solution)/shard_map/ppermute | solution.py:416
  (12 other events, 16.9 us)
where the time goes:
time: 146 us
  waiting for transfers between devices  71.6 us (49%)
  starting transfers between devices  27.8 us (19%)
  Pallas kernels  20.4 us (14%)
  matrix products  14.7 us (10%)
  local copies, waits for them, and re-layouts  9.56 us (7%)
  between operations  1.51 us (1%)
    ppermute x7, waiting for transfers between devices, pooled(): coeffs.append(lax.ppermute(own, 'tensor', hop))  51.7 us
    dot_general x1, matrix products, pooled(): base = jnp.dot(rows, up_weight, preferred_element_type=jnp.float32)  14.7 us
    ppermute x4, waiting for transfers between devices, ring_gather(): held[-step] = lax.ppermute(held[1 - step], 'tensor', ahead)  11.8 us
    ppermute x7, starting transfers between devices, pooled(): coeffs.append(lax.ppermute(own, 'tensor', hop))  10.6 us
    unnamed x36, local copies, waits for them, and re-layouts  8.77 us
    ppermute x4, starting transfers between devices, ring_gather(): held[-step] = lax.ppermute(held[1 - step], 'tensor', ahead)  7.98 us
    pallas_call x1, Pallas kernels, collect_rows(): pl.pallas_call(kernel, in_specs=[pl.BlockSpec(memory_space=pltpu.SMEM), p...  7.04 us
    ppermute x3, waiting for transfers between devices, ring_gather(): held[step] = lax.ppermute(held[step - 1], 'tensor', back)  6.37 us
  transfers between devices with their start and end apart: 26, of which 9 were waited for; matrix products, arithmetic and copies ran while one was open for 11% of the time, Pallas kernels for 7%

commit v1 on v0

--- a/solution.py
+++ b/solution.py
@@ -1,5 +1,3 @@
-import functools
-
 import jax
 import jax.numpy as jnp
 import numpy as np
@@ -73,7 +71,7 @@
 
     def kernel(
         ranks_ref, home_ref, length_ref, adapter_ref, position_ref,
-        gain_ref, choose_ref, fixed_ref, code_ref, begin_ref, full_ref,
+        gain_ref, own_ref, choose_ref, live_ref, fixed_ref, code_ref, begin_ref, full_ref,
         rank_of, rows_of, used, factor, order,
     ):
         for a in range(slots):
@@ -104,14 +102,16 @@
             return spot, code & 31, (code >> 5) & 1, code >> 6
 
         here = position_ref[0]
-        spot, slot, by_factor, rank = tables(
-            lax.broadcasted_iota(jnp.int32, (total_rows, limit), 0)
-        )
+        spot, slot, by_factor, _ = tables(lax.broadcasted_iota(jnp.int32, (total_rows, limit), 0))
         code_ref[...] = slot + 32 * by_factor + 64 * spot
-        lane = lax.broadcasted_iota(jnp.int32, (total_rows, limit), 1)
-        half, column = lane >> shift, lane & (rank_width - 1)
+
+        lane = lax.broadcasted_iota(jnp.int32, (total_rows // 2, limit), 1)
+        row = lax.broadcasted_iota(jnp.int32, (total_rows // 2, limit), 0)
+        _, slot, _, rank = tables(row + (lane >> shift) * (total_rows // 2))
+        own_ref[...] = jnp.where(slot == here, 1.0, 0.0)
         scale = ADAPTER_ALPHA / rank.astype(jnp.float32)
-        gain_ref[...] = jnp.where((slot == (here ^ half)) & (column < rank), scale, 0.0)
+        inside = ((slot >> 1) == (here >> 1)) & ((lane & (rank_width - 1)) < rank)
+        gain_ref[...] = jnp.where(inside, scale, 0.0)
 
         spot, slot, by_factor, _ = tables(lax.broadcasted_iota(jnp.int32, (8, total_rows), 1))
         mine = ((slot >> 1) == (here >> 1)) & (by_factor == 0)
@@ -124,20 +124,23 @@
         half, column = lane >> shift, lane & (rank_width - 1)
         other = here ^ 1
         begin = jnp.where(half == 0, begin_ref[here], begin_ref[other])
-        bound = jnp.where(
-            half == 0, used[here] * factor[here], used[other] * factor[other]
-        )
-        held = (line == begin + column) & (column < bound)
+        many = jnp.where(half == 0, used[here], used[other])
+        kind = jnp.where(half == 0, factor[here], factor[other])
+        held = (line == begin + column) & (column < many) & (kind == 1)
         fixed_ref[...] = jnp.where(held, 1.0, 0.0).astype(jnp.bfloat16)
+        live = (line >= begin) & (line < begin + many) & (kind == 0)
+        live_ref[...] = jnp.where(live, 1.0, 0.0)
 
     smem, whole = pl.BlockSpec(memory_space=pltpu.SMEM), pl.BlockSpec(memory_space=pltpu.VMEM)
     return pl.pallas_call(
         kernel,
         in_specs=[smem] * 5,
-        out_specs=[whole] * 4 + [smem] * 2,
+        out_specs=[whole] * 6 + [smem] * 2,
         out_shape=[
-            jax.ShapeDtypeStruct((total_rows, limit), jnp.float32),
+            jax.ShapeDtypeStruct((total_rows // 2, limit), jnp.float32),
+            jax.ShapeDtypeStruct((total_rows // 2, limit), jnp.float32),
             jax.ShapeDtypeStruct((limit, total_rows), jnp.bfloat16),
+            jax.ShapeDtypeStruct((limit, limit), jnp.float32),
             jax.ShapeDtypeStruct((limit, limit), jnp.bfloat16),
             jax.ShapeDtypeStruct((total_rows, limit), jnp.int32),
             jax.ShapeDtypeStruct((slots,), jnp.int32),
@@ -151,41 +154,49 @@
     )(ranks, adapter_slot, segment_lengths, segment_adapter, position)
 
 
-def collect_rows(blocks, places, down_pair, gain):
+def collect_rows(blocks, places, core, own_down, other_down, own):
     count = len(blocks)
     height, features = blocks[0].shape
-    rank_width = down_pair[0].shape[0]
-    chunk = 2048 if features % 2048 == 0 else features
+    height = height // 2
+    rank_width = other_down.shape[0]
+    half_rows = own.shape[0]
+    chunk = 1024 if features % 1024 == 0 else features
     chunks = features // chunk
 
-    def kernel(places_ref, gain_ref, *refs):
-        sources, down_refs = refs[:count], refs[count : count + 2]
-        rows_ref, coeff_ref, downs, sems = refs[count + 2 :]
-        copies = []
+    def kernel(places_ref, core_ref, own_ref, *refs):
+        sources, own_down_ref, other_down_ref = refs[:count], refs[count], refs[count + 1]
+        rows_ref, shrink_ref, downs, sems = refs[count + 2 :]
+        groups = []
         for k in range(chunks):
             columns = pl.ds(k * chunk, chunk)
-            for i in range(2):
-                copies.append(
-                    pltpu.make_async_copy(
-                        down_refs[i].at[:, columns],
-                        downs.at[pl.ds(i * rank_width, rank_width), columns],
-                        sems.at[k, count + i],
-                    )
-                )
-            for i in range(count):
+            offset = pl.multiple_of(core_ref[0] * features + k * chunk, chunk)
+            copies = [
+                pltpu.make_async_copy(
+                    own_down_ref.at[:, pl.ds(offset, chunk)],
+                    downs.at[pl.ds(0, rank_width), columns],
+                    sems.at[k, 2 * count],
+                ),
+                pltpu.make_async_copy(
+                    other_down_ref.at[:, columns],
+                    downs.at[pl.ds(rank_width, rank_width), columns],
+                    sems.at[k, 2 * count + 1],
+                ),
+            ]
+            for i in range(2 * count):
                 start = pl.multiple_of(places_ref[i] * height, height)
                 copies.append(
                     pltpu.make_async_copy(
-                        sources[i].at[:, columns],
+                        sources[i // 2].at[pl.ds(i % 2 * height, height), columns],
                         rows_ref.at[pl.ds(start, height), columns],
                         sems.at[k, i],
                     )
                 )
-        for copy in copies:
-            copy.start()
-        shrink = jnp.zeros(gain_ref.shape, jnp.float32)
+            groups.append(copies)
+            for copy in copies:
+                copy.start()
+        shrink = jnp.zeros((2 * half_rows, 2 * rank_width), jnp.float32)
         for k in range(chunks):
-            for copy in copies[k * (count + 2) : (k + 1) * (count + 2)]:
+            for copy in groups[k]:
                 copy.wait()
             columns = pl.ds(k * chunk, chunk)
             shrink = shrink + lax.dot_general(
@@ -194,21 +205,24 @@
                 (((1,), (1,)), ((), ())),
                 preferred_element_type=jnp.float32,
             )
-        coeff_ref[...] = (shrink * gain_ref[...]).astype(jnp.bfloat16)
-
-    rows = count * height
+        top, bottom = shrink[:half_rows], shrink[half_rows:]
+        first = jnp.concatenate([top[:, :rank_width], bottom[:, :rank_width]], axis=1)
+        second = jnp.concatenate([top[:, rank_width:], bottom[:, rank_width:]], axis=1)
+        shrink_ref[...] = jnp.where(own_ref[...] > 0.5, first, second)
+
+    smem, whole = pl.BlockSpec(memory_space=pltpu.SMEM), pl.BlockSpec(memory_space=pltpu.VMEM)
+    rows = 2 * count * height
     return pl.pallas_call(
         kernel,
-        in_specs=[pl.BlockSpec(memory_space=pltpu.SMEM), pl.BlockSpec(memory_space=pltpu.VMEM)]
-        + [pl.BlockSpec(memory_space=pl.ANY)] * (count + 2),
-        out_specs=[pl.BlockSpec(memory_space=pltpu.VMEM)] * 2,
+        in_specs=[smem, smem, whole] + [pl.BlockSpec(memory_space=pl.ANY)] * (count + 2),
+        out_specs=[whole] * 2,
         out_shape=[
             jax.ShapeDtypeStruct((rows, features), blocks[0].dtype),
-            jax.ShapeDtypeStruct((rows, 2 * rank_width), jnp.bfloat16),
+            jax.ShapeDtypeStruct(own.shape, jnp.float32),
         ],
         scratch_shapes=[
-            pltpu.VMEM((2 * rank_width, features), down_pair[0].dtype),
-            pltpu.SemaphoreType.DMA((chunks, count + 2)),
+            pltpu.VMEM((2 * rank_width, features), own_down.dtype),
+            pltpu.SemaphoreType.DMA((chunks, 2 * count + 2)),
         ],
         compiler_params=vmem(4 * rows * features),
         cost_estimate=pl.CostEstimate(
@@ -216,15 +230,21 @@
             bytes_accessed=4 * rows * features,
             transcendentals=0,
         ),
-    )(places, gain, *blocks, *down_pair)
-
-
-def build_payload(choose, fixed, coeff, mine, other, first, count):
+    )(places, core, own, *blocks, own_down, other_down)
+
+
+def build_payload(choose, live, fixed, coeff, mine, other, first, count):
     chips, rank_width, width = mine.shape
 
-    def kernel(choose_ref, fixed_ref, coeff_ref, mine_ref, other_ref, out_ref):
+    half_rows = coeff.shape[0]
+
+    def kernel(choose_ref, live_ref, fixed_ref, coeff_ref, mine_ref, other_ref, out_ref):
         lines = pl.ds(first, count)
-        select = jnp.dot(choose_ref[lines], coeff_ref[...], preferred_element_type=jnp.float32)
+        folded = coeff_ref[...]
+        top = jnp.dot(choose_ref[lines, :half_rows], folded, preferred_element_type=jnp.float32)
+        low = jnp.dot(choose_ref[lines, half_rows:], folded, preferred_element_type=jnp.float32)
+        chosen = top[:, :rank_width] + low[:, rank_width:]
+        select = jnp.concatenate([chosen, chosen], axis=1) * live_ref[lines]
         select = (select + fixed_ref[lines].astype(jnp.float32)).astype(jnp.bfloat16)
 
         @pl.loop(0, chips)
@@ -237,7 +257,7 @@
 
     return pl.pallas_call(
         kernel,
-        in_specs=[pl.BlockSpec(memory_space=pltpu.VMEM)] * 5,
+        in_specs=[pl.BlockSpec(memory_space=pltpu.VMEM)] * 6,
         out_specs=pl.BlockSpec(memory_space=pltpu.VMEM),
         out_shape=jax.ShapeDtypeStruct((chips, count, width), mine.dtype),
         compiler_params=vmem(4 * chips * width * (2 * rank_width + count)),
@@ -246,10 +266,10 @@
             bytes_accessed=2 * chips * width * (2 * rank_width + count),
             transcendentals=0,
         ),
-    )(choose, fixed, coeff, mine, other)
-
-
-def combine(base, code, begin, more, coeffs, incoming, extra):
+    )(choose, live, fixed, coeff, mine, other)
+
+
+def combine(base, code, begin, more, coeff, incoming, extra):
     total_rows, width = base.shape
     chips, first, _ = incoming.shape
     second = extra.shape[1]
@@ -258,12 +278,19 @@
     shift = rank_width.bit_length() - 1
     tile = 256 if width % 256 == 0 else 128
 
-    def kernel(begin_ref, more_ref, base_ref, code_ref, *refs):
-        coeff_refs, incoming_ref = refs[: len(coeffs)], refs[len(coeffs)]
-        extra_ref, out_ref, late, sem = refs[len(coeffs) + 1 :]
+    def kernel(
+        begin_ref, more_ref, base_ref, code_ref, coeff_ref, incoming_ref, extra_ref,
+        out_ref, late, sem,
+    ):
         fetch = pltpu.make_async_copy(extra_ref, late, sem)
-        half = functools.reduce(jnp.add, [ref[...].astype(jnp.float32) for ref in coeff_refs])
-        both = jnp.concatenate([half, half], axis=1)
+        folded = coeff_ref[...].astype(jnp.float32)
+        both = jnp.concatenate(
+            [
+                jnp.concatenate([part, part], axis=1)
+                for part in (folded[:, :rank_width], folded[:, rank_width:])
+            ],
+            axis=0,
+        )
         code_value = code_ref[...]
         slot, by_factor, spot = code_value & 31, (code_value >> 5) & 1, code_value >> 6
         lane = lax.broadcasted_iota(jnp.int32, (total_rows, limit), 1)
@@ -317,7 +344,7 @@
     return pl.pallas_call(
         kernel,
         in_specs=[smem] * 2
-        + [whole] * (len(coeffs) + 3)
+        + [whole] * 4
         + [pl.BlockSpec(memory_space=pl.ANY)],
         out_specs=whole,
         out_shape=jax.ShapeDtypeStruct((total_rows, width), jnp.bfloat16),
@@ -328,10 +355,10 @@
             bytes_accessed=6 * total_rows * width + 2 * chips * limit * width,
             transcendentals=0,
         ),
-    )(begin, more, base, code, *coeffs, incoming, extra)
-
-
-def ring_gather(block, shards):
+    )(begin, more, base, code, coeff, incoming, extra)
+
+
+def ring_gather(block, shards, halfway):
     chips = shards // 2
     depth = chips // 2
     cycle = list(range(0, chips, 2)) + list(range(chips - 1, 0, -2))
@@ -339,22 +366,19 @@
         (2 * cycle[p] + c, 2 * cycle[(p + 1) % chips] + c) for p in range(chips) for c in range(2)
     ]
     back = [(b, a) for a, b in ahead]
-    sibling = [(t, t ^ 1) for t in range(shards)]
     held = {0: block}
     for step in range(1, depth + 1):
         held[-step] = lax.ppermute(held[1 - step], "tensor", ahead)
         if step < chips - depth:
             held[step] = lax.ppermute(held[step - 1], "tensor", back)
-    blocks = []
-    for piece in held.values():
-        blocks += [piece, lax.ppermute(piece, "tensor", sibling)]
+        held[-step] = halfway(step, held[-step])
     table = np.zeros((shards, shards), np.int32)
     for t in range(shards):
         for i, offset in enumerate(held):
             chip = cycle[(cycle.index(t // 2) + offset) % chips]
             table[t, 2 * i], table[t, 2 * i + 1] = 2 * chip + t % 2, 2 * chip + 1 - t % 2
     places = lax.dynamic_index_in_dim(table, lax.axis_index("tensor"), keepdims=False)
-    return blocks, places, held[-1]
+    return list(held.values()), places
 
 
 def largest_over_groups(value):
@@ -384,21 +408,54 @@
     sibling = [(t, t ^ 1) for t in range(shards)]
     same_core = [list(range(c, shards, 2)) for c in range(2)]
 
-    blocks, places, first = ring_gather(input_rows, shards)
-    adapter_up, adapter_down, first = lax.optimization_barrier((adapter_up, adapter_down, first))
-    mine, other = split_for_pair(adapter_up[0], (position & 1)[None], chips)
+    core = position & 1
+    features = input_rows.shape[1] // 2
+
+    def swap(value):
+        keep = lax.dynamic_slice_in_dim(value, core * features, features, 1)
+        send = lax.dynamic_slice_in_dim(value, (1 - core) * features, features, 1)
+        return keep, lax.ppermute(send, "tensor", sibling)
+
+    block = jnp.concatenate(swap(input_rows), axis=0)
+    side = {}
+
+    def halfway(step, piece):
+        if step == 1:
+            up, down, piece = lax.optimization_barrier((adapter_up[0], adapter_down[0], piece))
+            side["up"] = split_for_pair(up, core[None], chips)
+            side["down"] = swap(down)[1]
+            side["tables"] = describe(
+                ranks, adapter_slot, segment_lengths, segment_adapter, position[None],
+                total_rows, limit,
+            )
+        if step == 2:
+            piece, side["up"], side["tables"] = lax.optimization_barrier(
+                (piece, side["up"], side["tables"])
+            )
+        return piece
+
+    blocks, places = ring_gather(block, shards, halfway)
+    mine, other = side["up"]
     other = lax.ppermute(other, "tensor", sibling)
-    down_pair = (adapter_down[0], lax.ppermute(adapter_down[0], "tensor", sibling))
-    gain, choose, fixed, code, begin, full = describe(
-        ranks, adapter_slot, segment_lengths, segment_adapter, position[None], total_rows, limit
-    )
+    gain, own, choose, live, fixed, code, begin, full = side["tables"]
     fullest = largest_over_groups(full)
-    rows, coeff = collect_rows(blocks, places, down_pair, gain)
-
-    def exchange(low, count):
-        payload = build_payload(choose, fixed, coeff, mine, other, low, count)
+    rows, shrink = collect_rows(
+        blocks, places, core[None], adapter_down[0], side["down"], own
+    )
+    shrink = shrink + lax.ppermute(shrink, "tensor", sibling)
+    rows_other = lax.ppermute(rows, "tensor", sibling)
+    coeff = (shrink * gain).astype(jnp.bfloat16)
+    every, bit = coeff, 2
+    while bit < shards:
+        every = every + lax.ppermute(every, "tensor", [(t, t ^ bit) for t in range(shards)])
+        bit *= 2
+
+    def payload(low, count):
+        return build_payload(choose, live, fixed, coeff, mine, other, low, count)
+
+    def exchange(value):
         return lax.all_to_all(
-            payload,
+            value,
             "tensor",
             split_axis=0,
             concat_axis=0,
@@ -406,21 +463,21 @@
             tiled=True,
         )
 
-    incoming = exchange(0, FIRST_ROWS)
-    base = jnp.dot(rows, up_weight, preferred_element_type=jnp.float32)
-    coeff, fullest, base = lax.optimization_barrier((coeff, fullest, base))
-    own = coeff[:, :rank_width] + coeff[:, rank_width:]
-    coeffs = [own]
-    for step in range(1, chips):
-        hop = [(t, (t + 2 * step) % shards) for t in range(shards)]
-        coeffs.append(lax.ppermute(own, "tensor", hop))
+    near = payload(0, FIRST_ROWS)
+    near, every, rows, rows_other = lax.optimization_barrier((near, every, rows, rows_other))
+    incoming = exchange(near)
+    halves = [jnp.where(core == c, rows, rows_other) for c in range(2)]
+    base = jnp.dot(
+        jnp.concatenate(halves, axis=1), up_weight, preferred_element_type=jnp.float32
+    )
+    fullest, base = lax.optimization_barrier((fullest, base))
     rest = limit - FIRST_ROWS
     extra = lax.cond(
         fullest[0] > FIRST_ROWS,
-        lambda: exchange(FIRST_ROWS, rest),
+        lambda: exchange(payload(FIRST_ROWS, rest)),
         lambda: jnp.zeros((chips, rest, up_weight.shape[1]), adapter_up.dtype),
     )
-    return combine(base, code, begin, fullest, coeffs, incoming, extra)
+    return combine(base, code, begin, fullest, every, incoming, extra)
 
 
 def gathered(input_rows, up_weight, adapter_down, adapter_up, slot_row, row_rank):
@@ -463,6 +520,7 @@
     shards = lax.axis_size("tensor")
     stored, rank_width, _ = adapter_up.shape
     tiled = up_weight.shape[1] % 128 == 0 and input_rows.shape[0] % 16 == 0 and rank_width == 64
+    tiled = tiled and input_rows.shape[1] % 256 == 0 and input_rows.shape[0] * shards <= 256
     if shards == POOLED_SHARDS and stored == 1 and tiled:
         return pooled(
             input_rows,

time: 146 us -> 147 us (level)
  blocking collectives: 0 us -> 52.7 us
  waiting for transfers between devices: 71.6 us -> 27.2 us
  starting transfers between devices: 27.8 us -> 17.7 us
  other arithmetic: 0.09 us -> 2.57 us
  local copies, waits for them, and re-layouts: 9.56 us -> 11.4 us
  Pallas kernels: 20.4 us -> 18.6 us
    all_to_all x0 -> x1, blocking collectives: none -> 52.7 us  [exchange(): lax.all_to_all(value, 'tensor', split_axis=0, concat_axis=0, axis_index_g...]
    ppermute x16 -> x7, waiting for transfers between devices: 51.7 us -> 11.5 us  [the longest x1 5.95 us: pooled(): shrink = shrink + lax.ppermute(shrink, 'tensor', sibling)]
    ppermute x4, waiting for transfers between devices: 11.8 us -> 1.42 us  [ring_gather(): held[-step] = lax.ppermute(held[1 - step], 'tensor', ahead)]
    ppermute x3, waiting for transfers between devices: 6.37 us -> 11.9 us  [ring_gather(): held[step] = lax.ppermute(held[step - 1], 'tensor', back)]
    ppermute x16 -> x7, starting transfers between devices: 11.9 us -> 6.84 us  [the longest x3 6.17 us: pooled(): lax.ppermute(every, 'tensor', [(t, t ^ bit) for t in range(shards)])]
    all_to_all x1 -> x0, starting transfers between devices: 4.96 us -> none  [exchange(): lax.all_to_all(payload, 'tensor', split_axis=0, concat_axis=0, axis_index...]
    dynamic_slice x0 -> x2, local copies, waits for them, and re-layouts: none -> 2.94 us  [the longest x1 1.96 us: swap(): send = lax.dynamic_slice_in_dim(value, (1 - core) * features, features, 1)]
    select_n x0 -> x1, other arithmetic: none -> 2.5 us  [pooled(): halves = [jnp.where(core == c, rows, rows_other) for c in range(2)]]
  transfers between devices with their start and end apart: 26 -> 16, of which waited for: 9 -> 9; matrix products, arithmetic and copies ran while one was open for 11% -> 2% of each run, Pallas kernels for 7% -> 6%
where the time goes in v1:
time: 147 us; the launch traced here: 146 us
  blocking collectives  52.7 us (36%)
  waiting for transfers between devices  27.2 us (19%)
  Pallas kernels  18.6 us (13%)
  starting transfers between devices  17.7 us (12%)
  matrix products  14.7 us (10%)
  local copies, waits for them, and re-layouts  11.4 us (8%)
  other arithmetic  2.57 us (2%)
    all_to_all x1, blocking collectives, exchange(): lax.all_to_all(value, 'tensor', split_axis=0, concat_axis=0, axis_index_g...  52.7 us
    dot_general x1, matrix products, pooled(): jnp.dot(jnp.concatenate(halves, axis=1), up_weight, preferred_element_typ...  14.7 us
    ppermute x3, waiting for transfers between devices, ring_gather(): held[step] = lax.ppermute(held[step - 1], 'tensor', back)  11.9 us
    ppermute x4, starting transfers between devices, ring_gather(): held[-step] = lax.ppermute(held[1 - step], 'tensor', ahead)  8.32 us
    unnamed x28, local copies, waits for them, and re-layouts  6.57 us
    ppermute x3, starting transfers between devices, pooled(): lax.ppermute(every, 'tensor', [(t, t ^ bit) for t in range(shards)])  6.17 us
    ppermute x1, waiting for transfers between devices, pooled(): shrink = shrink + lax.ppermute(shrink, 'tensor', sibling)  5.95 us
    pallas_call x1, Pallas kernels, collect_rows(): pl.pallas_call(kernel, in_specs=[smem, smem, whole] + [pl.BlockSpec(memor...  5.4 us
  transfers between devices with their start and end apart: 16, of which 9 were waited for; matrix products, arithmetic and copies ran while one was open for 2% of the time, Pallas kernels for 6%

profile of v1, /device:TPU:0, one launch (start us, length us, event | category | flops | bytes accessed | tf_op | source)
XLA Modules:
  0.0 146.3 jit_solution(14910324810833052465)
XLA Ops:
  0.0 1.0 constant_dynamic-slice_fusion.3
  1.5 1.0 collective-permute-done
  2.5 3.0 %collective-permute-start.1 = (bf16[32,4096]{1,0:T(8,128)(2,1)S(1)}, bf16[32,4096]{1,0:T(8,128)(2,1)S(1)}, u32[]{:S(2)}, u32[]{:S(2)}) collective-permute-start(bf16[32,4096]{1,0:T(8,128)(2,1)S(1)} %pad_maximum_fusion.refs_0_), channel_id=1, source_target_pairs={{0,4},{1,5},{4,8},{5,9},{8,12},{9,13},{12,14},{13,15},{14,10},{15,... | collective-permute-start | bytes 786440 | tf_op jit(solution)/shard_map/ppermute | solution.py:371
  6.2 0.7 copy-done.3
  8.1 2.0 %shard_map.92 = (f32[128,128]{1,0:T(8,128)S(1)}, f32[128,128]{1,0:T(8,128)S(1)}, bf16[128,256]{1,0:T(8,128)(2,1)}, f32[128,128]{1,0:T(8,128)}, bf16[128,128]{1,0...) custom-call(s32[16]{0:T(128)S(1)} %copy-done.2, s32[16]{0:T(128)S(1)} %copy-done.3, ...), custom_call_target="tpu_custom_call" | custom-call | flops 6553600 | bytes 524288 | tf_op jit(solution)/shard_map/pallas_call | solution.py:135
  10.8 1.2 collective-permute-done.1.refs_1_
  12.1 1.8 %collective-permute-start.2 = (bf16[32,4096]{1,0:T(8,128)(2,1)S(1)}, bf16[32,4096]{1,0:T(8,128)(2,1)S(1)}, u32[]{:S(2)}, u32[]{:S(2)}) collective-permute-start(bf16[32,4096]{1,0:T(8,128)(2,1)S(1)} %collective-permute-done.1.refs_1_), channel_id=1, source_target_pairs={{0,4},{1,5},{4,8},{5,9},{8,12},{9,13},{12,14},{13,15},{14,10},{15,... | collective-permute-start | bytes 786440 | tf_op jit(solution)/shard_map/ppermute | solution.py:371
  13.9 2.0 %constant_dynamic-slice_fusion = bf16[64,4096]{1,0:T(8,128)(2,1)} fusion(bf16[64,8192]{1,0:T(8,128)(2,1)} %bitcast.9, s32[]{:T(128)S(6)} %select_n.26), kind=kLoop, calls=%fused_computation.8 | loop fusion | bytes 1048580 | tf_op jit(solution)/shard_map/dynamic_slice | solution.py:416
  15.8 2.0 %copy-done = bf16[1,64,28672]{2,1,0:T(8,128)(2,1)S(1)} copy-done((bf16[1,64,28672]{2,1,0:T(8,128)(2,1)S(1)}, bf16[1,64,28672]{2,1,0:T(8,128)(2,1)}, u32[]{:S(2)}) %copy-start) | copy-done | bytes 3670040
  17.9 2.6 %shard_map.91 = (bf16[8,64,1792]{2,1,0:T(8,128)(2,1)}, bf16[8,64,1792]{2,1,0:T(8,128)(2,1)}) custom-call(s32[1]{0:T(128)} %bitcast.2.core_ref, bf16[64,28672]{1,0:T(8,128)(2,1)S(1)} %bitcast.8), custom_call_target="tpu_custom_call" | custom-call | bytes 7340032 | tf_op jit(solution)/shard_map/pallas_call | solution.py:54
  20.8 1.8 %collective-permute-start.6 = (bf16[32,4096]{1,0:T(8,128)(2,1)S(1)}, bf16[32,4096]{1,0:T(8,128)(2,1)S(1)}, u32[]{:S(2)}, u32[]{:S(2)}) collective-permute-start(bf16[32,4096]{1,0:T(8,128)(2,1)S(1)} %collective-permute-done.2.refs_3_), channel_id=1, source_target_pairs={{0,4},{1,5},{4,8},{5,9},{8,12},{9,13},{12,14},{13,15},{14,10},{15,... | collective-permute-start | bytes 786440 | tf_op jit(solution)/shard_map/ppermute | solution.py:371
  22.6 6.7 %collective-permute-done.5.refs_4_ = bf16[32,4096]{1,0:T(8,128)(2,1)S(1)} collective-permute-done((bf16[32,4096]{1,0:T(8,128)(2,1)S(1)}, bf16[32,4096]{1,0:T(8,128)(2,1)S(1)}, u32[]{:S(2)}, u32[]{:S(2)}) %collective-permute-start.5) | collective-permute-done | bytes 262176 | tf_op jit(solution)/shard_map/ppermute | solution.py:373
  29.5 1.7 %collective-permute-start.8 = (bf16[32,4096]{1,0:T(8,128)(2,1)S(1)}, bf16[32,4096]{1,0:T(8,128)(2,1)}, u32[]{:S(2)}, u32[]{:S(2)}) collective-permute-start(bf16[32,4096]{1,0:T(8,128)(2,1)S(1)} %collective-permute-done.6.refs_5_), channel_id=1, source_target_pairs={{0,4},{1,5},{4,8},{5,9},{8,12},{9,13},{12,14},{13,15},{14,10},{15,... | collective-permute-start | bytes 786440 | tf_op jit(solution)/shard_map/ppermute | solution.py:371
  31.3 0.7 fusion.4.places_ref
  32.0 5.2 %collective-permute-done.7.refs_6_ = bf16[32,4096]{1,0:T(8,128)(2,1)S(1)} collective-permute-done((bf16[32,4096]{1,0:T(8,128)(2,1)S(1)}, bf16[32,4096]{1,0:T(8,128)(2,1)S(1)}, u32[]{:S(2)}, u32[]{:S(2)}) %collective-permute-start.7) | collective-permute-done | bytes 262176 | tf_op jit(solution)/shard_map/ppermute | solution.py:373
  37.4 5.4 %shard_map.93 = (bf16[256,4096]{1,0:T(8,128)(2,1)}, f32[128,128]{1,0:T(8,128)S(1)}) custom-call(s32[16]{0:T(128)S(1)} %fusion.4.places_ref, s32[1]{0:T(128)} %bitcast.2.core_ref, f32[128,128]{1,0:T(8,128)S(1)} %get-tuple-element.75.own_ref, bf16[32,4096]{1,0:T(8,128)(2,1)S(1)} %pad_maximum_fusion.refs_0_, ...), custom_call_target="tpu_custom_call" | custom-call | flops 268435456 | bytes 4194304 | tf_op jit(solution)/shard_map/pallas_call | solution.py:215
  43.4 6.0 %collective-permute-done.10 = f32[128,128]{1,0:T(8,128)S(1)} collective-permute-done((f32[128,128]{1,0:T(8,128)S(1)}, f32[128,128]{1,0:T(8,128)S(1)}, u32[]{:S(2)}, u32[]{:S(2)}) %collective-permute-start.10) | collective-permute-done | bytes 65568 | tf_op jit(solution)/shard_map/ppermute | solution.py:445
  49.4 1.7 %collective-permute-start.12 = (bf16[128,128]{1,0:T(8,128)(2,1)S(1)}, bf16[128,128]{1,0:T(8,128)(2,1)S(1)}, u32[]{:S(2)}, u32[]{:S(2)}) collective-permute-start(bf16[128,128]{1,0:T(8,128)(2,1)S(1)} %multiply_convert_fusion.coeff_ref), channel_id=1, source_target_pairs={{0,2},{1,3},{2,0},{3,1},{4,6},{5,7},{6,4},{7,5},{8,10},{9,11},{10,... | collective-permute-start | bytes 98312 | tf_op jit(solution)/shard_map/ppermute | solution.py:450
  51.1 2.3 %collective-permute-done.12 = bf16[128,128]{1,0:T(8,128)(2,1)S(1)} collective-permute-done((bf16[128,128]{1,0:T(8,128)(2,1)S(1)}, bf16[128,128]{1,0:T(8,128)(2,1)S(1)}, u32[]{:S(2)}, u32[]{:S(2)}) %collective-permute-start.12) | collective-permute-done | bytes 32800 | tf_op jit(solution)/shard_map/ppermute | solution.py:450
  53.4 1.7 %collective-permute-start.13 = (bf16[128,128]{1,0:T(8,128)(2,1)S(1)}, bf16[128,128]{1,0:T(8,128)(2,1)S(1)}, u32[]{:S(2)}, u32[]{:S(2)}) collective-permute-start(bf16[128,128]{1,0:T(8,128)(2,1)S(1)} %add.27), channel_id=1, source_target_pairs={{0,4},{1,5},{2,6},{3,7},{4,0},{5,1},{6,2},{7,3},{8,12},{9,13},{10,... | collective-permute-start | bytes 98312 | tf_op jit(solution)/shard_map/ppermute | solution.py:450
  55.1 2.2 %collective-permute-done.13 = bf16[128,128]{1,0:T(8,128)(2,1)S(1)} collective-permute-done((bf16[128,128]{1,0:T(8,128)(2,1)S(1)}, bf16[128,128]{1,0:T(8,128)(2,1)S(1)}, u32[]{:S(2)}, u32[]{:S(2)}) %collective-permute-start.13) | collective-permute-done | bytes 32800 | tf_op jit(solution)/shard_map/ppermute | solution.py:450
  57.4 2.8 %collective-permute-start.14 = (bf16[128,128]{1,0:T(8,128)(2,1)S(1)}, bf16[128,128]{1,0:T(8,128)(2,1)S(1)}, u32[]{:S(2)}, u32[]{:S(2)}) collective-permute-start(bf16[128,128]{1,0:T(8,128)(2,1)S(1)} %add.28), channel_id=1, source_target_pairs={{0,8},{1,9},{2,10},{3,11},{4,12},{5,13},{6,14},{7,15},{8,0},{9,1},... | collective-permute-start | bytes 98312 | tf_op jit(solution)/shard_map/ppermute | solution.py:450
  60.1 1.5 %collective-permute-start.3 = (s32[1]{0:T(128)}, s32[1]{0:T(128)}, u32[]{:S(2)}, u32[]{:S(2)}) collective-permute-start(s32[1]{0:T(128)} %get-tuple-element.71), channel_id=1, source_target_pairs={{0,16},{16,0},{1,17},{17,1},{2,18},{18,2},{3,19},{19,3},{4,20},{20... | collective-permute-start | bytes 20 | tf_op jit(solution)/shard_map/ppermute | solution.py:387
  61.6 2.4 %collective-permute-done.3 = s32[1]{0:T(128)} collective-permute-done((s32[1]{0:T(128)}, s32[1]{0:T(128)}, u32[]{:S(2)}, u32[]{:S(2)}) %collective-permute-start.3) | collective-permute-done | bytes 36 | tf_op jit(solution)/shard_map/ppermute | solution.py:387
  65.3 1.2 copy-done.9
  66.5 4.3 %shard_map.94 = bf16[8,80,1792]{2,1,0:T(8,128)(2,1)S(1)} custom-call(bf16[128,256]{1,0:T(8,128)(2,1)} %get-tuple-element.72.choose_ref, f32[128,128]{1,0:T(8,128)} %get-tuple-element.73.live_ref, bf16[128,128]{1,0:T(8,128)(2,1)} %get-tuple-element.74.fixed_ref, bf16[128,128]{1,0:T(8,128)(2,1)S(1)} %multiply_convert_fusion.coeff_ref, ...), custom_call_target="tpu_custom_call" | custom-call | flops 293601280 | bytes 5963776 | tf_op jit(solution)/shard_map/pallas_call | solution.py:258
  70.8 2.5 %broadcast_select_fusion.1 = (bf16[256,4096]{1,0:T(8,128)(2,1)S(1)}, bf16[256,4096]{1,0:T(8,128)(2,1)S(1)}) fusion(bf16[256,4096]{1,0:T(8,128)(2,1)} %get-tuple-element.83, bf16[256,4096]{1,0:T(8,128)(2,1)} %collective-permute-done.15, pred[]{:T(512)S(6)} %eq.6, pred[]{:T(512)S(6)} %eq.7), kind=kLoop, calls=%fused_computation.5 | loop fusion | flops 2097152 | bytes 8388610 | tf_op jit(solution)/shard_map/jit(_where)/select_n | solution.py:469
  73.3 14.7 %fusion.base_ref = f32[256,1792]{1,0:T(8,128)} fusion(bf16[8192,1792]{1,0:T(8,128)(2,1)} %param.12, bf16[256,4096]{1,0:T(8,128)(2,1)S(1)} %get-tuple-element.91, bf16[256,4096]{1,0:T(8,128)(2,1)S(1)} %get-tuple-element.90), kind=kOutput, calls=%fused_computation | convolution fusion | flops 7524581376 | bytes 35389440 | tf_op jit(solution)/shard_map/dot_general | solution.py:470
  88.1 1.2 conditional.1
  88.1 1.2 broadcast.2
  89.2 52.7 %all_to_all.10.incoming_ref = bf16[8,80,1792]{2,1,0:T(8,128)(2,1)S(1)} all-to-all(bf16[8,80,1792]{2,1,0:T(8,128)(2,1)S(1)} %shard_map.94), channel_id=1, replica_groups={{0,2,4,6,8,10,12,14},{1,3,5,7,9,11,13,15},{16,18,20,22,24,26,28,30},{17..., dimensions={0} | all-to-all | bytes 4587520 | tf_op jit(solution)/shard_map/all_to_all | solution.py:457
  141.9 4.3 %shard_map.95 = bf16[256,1792]{1,0:T(8,128)(2,1)} custom-call(s32[16]{0:T(128)S(1)} %get-tuple-element.70.begin_ref, s32[1]{0:T(128)S(6)} %max.3.more_ref, f32[256,1792]{1,0:T(8,128)S(1)} %copy-done.8, s32[256,128]{1,0:T(8,128)S(1)} %copy-done.7, bf16[128,128]{1,0:T(8,128)(2,1)S(1)} %add.29.coeff_ref, bf16[8,80,1792]{2,1,0:T(8,128)(2,1)S(1)} %all_to_all.10.incoming_ref, ...), custom_call_target="tpu_custom_call" | custom-call | flops 1879048192 | bytes 6422528 | tf_op jit(solution)/shard_map/pallas_call | solution.py:344
  (46 shorter events, 4.6 us)
Async XLA Ops:
  1.0 1.5 %collective-permute-start = (bf16[16,4096]{1,0:T(8,128)(2,1)S(1)}, bf16[16,4096]{1,0:T(8,128)(2,1)S(1)}, u32[]{:S(2)}, u32[]{:S(2)}) collective-permute-start(bf16[16,4096]{1,0:T(8,128)(2,1)S(1)} %get-tuple-element.93), channel_id=1, source_target_pairs={{0,1},{1,0},{2,3},{3,2},{4,5},{5,4},{6,7},{7,6},{8,9},{9,8},{10,11... | collective-permute-start | bytes 393224 | tf_op jit(solution)/shard_map/ppermute | solution.py:417
  2.5 9.5 %collective-permute-start.1 = (bf16[32,4096]{1,0:T(8,128)(2,1)S(1)}, bf16[32,4096]{1,0:T(8,128)(2,1)S(1)}, u32[]{:S(2)}, u32[]{:S(2)}) collective-permute-start(bf16[32,4096]{1,0:T(8,128)(2,1)S(1)} %pad_maximum_fusion.refs_0_), channel_id=1, source_target_pairs={{0,4},{1,5},{4,8},{5,9},{8,12},{9,13},{12,14},{13,15},{14,10},{15,... | collective-permute-start | bytes 786440 | tf_op jit(solution)/shard_map/ppermute | solution.py:371
  5.5 0.7 copy-start.2
  6.2 0.7 copy-start.3
  6.8 0.7 copy-start.4
  7.5 0.7 copy-start.5
  10.2 0.7 copy-start.6
  10.8 9.6 %collective-permute-start.4 = (bf16[32,4096]{1,0:T(8,128)(2,1)S(1)}, bf16[32,4096]{1,0:T(8,128)(2,1)S(1)}, u32[]{:S(2)}, u32[]{:S(2)}) collective-permute-start(bf16[32,4096]{1,0:T(8,128)(2,1)S(1)} %pad_maximum_fusion.refs_0_), channel_id=1, source_target_pairs={{4,0},{5,1},{8,4},{9,5},{12,8},{13,9},{14,12},{15,13},{10,14},{11,... | collective-permute-start | bytes 786440 | tf_op jit(solution)/shard_map/ppermute | solution.py:373
  12.1 8.7 %collective-permute-start.2 = (bf16[32,4096]{1,0:T(8,128)(2,1)S(1)}, bf16[32,4096]{1,0:T(8,128)(2,1)S(1)}, u32[]{:S(2)}, u32[]{:S(2)}) collective-permute-start(bf16[32,4096]{1,0:T(8,128)(2,1)S(1)} %collective-permute-done.1.refs_1_), channel_id=1, source_target_pairs={{0,4},{1,5},{4,8},{5,9},{8,12},{9,13},{12,14},{13,15},{14,10},{15,... | collective-permute-start | bytes 786440 | tf_op jit(solution)/shard_map/ppermute | solution.py:371
  13.9 23.5 %copy-start.1 = (bf16[1,64,8192]{2,1,0:T(8,128)(2,1)S(1)}, bf16[1,64,8192]{2,1,0:T(8,128)(2,1)}, u32[]{:S(2)}) copy-start(bf16[1,64,8192]{2,1,0:T(8,128)(2,1)} %param.13) | copy-start | bytes 3145732
  15.8 21.4 %collective-permute-start.9 = (bf16[64,4096]{1,0:T(8,128)(2,1)}, bf16[64,4096]{1,0:T(8,128)(2,1)S(1)}, u32[]{:S(2)}, u32[]{:S(2)}) collective-permute-start(bf16[64,4096]{1,0:T(8,128)(2,1)} %constant_dynamic-slice_fusion), channel_id=1, source_target_pairs={{0,1},{1,0},{2,3},{3,2},{4,5},{5,4},{6,7},{7,6},{8,9},{9,8},{10,11... | collective-permute-start | bytes 1572872 | tf_op jit(solution)/shard_map/ppermute | solution.py:417
  15.8 2.0 %copy-start = (bf16[1,64,28672]{2,1,0:T(8,128)(2,1)S(1)}, bf16[1,64,28672]{2,1,0:T(8,128)(2,1)}, u32[]{:S(2)}) copy-start(bf16[1,64,28672]{2,1,0:T(8,128)(2,1)} %param.14) | copy-start | bytes 11010052
  20.5 8.8 %collective-permute-start.5 = (bf16[32,4096]{1,0:T(8,128)(2,1)S(1)}, bf16[32,4096]{1,0:T(8,128)(2,1)S(1)}, u32[]{:S(2)}, u32[]{:S(2)}) collective-permute-start(bf16[32,4096]{1,0:T(8,128)(2,1)S(1)} %collective-permute-done.4.refs_2_), channel_id=1, source_target_pairs={{4,0},{5,1},{8,4},{9,5},{12,8},{13,9},{14,12},{15,13},{10,14},{11,... | collective-permute-start | bytes 786440 | tf_op jit(solution)/shard_map/ppermute | solution.py:373
  20.8 8.8 %collective-permute-start.6 = (bf16[32,4096]{1,0:T(8,128)(2,1)S(1)}, bf16[32,4096]{1,0:T(8,128)(2,1)S(1)}, u32[]{:S(2)}, u32[]{:S(2)}) collective-permute-start(bf16[32,4096]{1,0:T(8,128)(2,1)S(1)} %collective-permute-done.2.refs_3_), channel_id=1, source_target_pairs={{0,4},{1,5},{4,8},{5,9},{8,12},{9,13},{12,14},{13,15},{14,10},{15,... | collective-permute-start | bytes 786440 | tf_op jit(solution)/shard_map/ppermute | solution.py:371
  29.2 7.9 %collective-permute-start.7 = (bf16[32,4096]{1,0:T(8,128)(2,1)S(1)}, bf16[32,4096]{1,0:T(8,128)(2,1)S(1)}, u32[]{:S(2)}, u32[]{:S(2)}) collective-permute-start(bf16[32,4096]{1,0:T(8,128)(2,1)S(1)} %collective-permute-done.5.refs_4_), channel_id=1, source_target_pairs={{4,0},{5,1},{8,4},{9,5},{12,8},{13,9},{14,12},{15,13},{10,14},{11,... | collective-permute-start | bytes 786440 | tf_op jit(solution)/shard_map/ppermute | solution.py:373
  29.5 7.8 %collective-permute-start.8 = (bf16[32,4096]{1,0:T(8,128)(2,1)S(1)}, bf16[32,4096]{1,0:T(8,128)(2,1)}, u32[]{:S(2)}, u32[]{:S(2)}) collective-permute-start(bf16[32,4096]{1,0:T(8,128)(2,1)S(1)} %collective-permute-done.6.refs_5_), channel_id=1, source_target_pairs={{0,4},{1,5},{4,8},{5,9},{8,12},{9,13},{12,14},{13,15},{14,10},{15,... | collective-permute-start | bytes 786440 | tf_op jit(solution)/shard_map/ppermute | solution.py:371
  42.8 28.0 %collective-permute-start.15 = (bf16[256,4096]{1,0:T(8,128)(2,1)}, bf16[256,4096]{1,0:T(8,128)(2,1)}, u32[]{:S(2)}, u32[]{:S(2)}) collective-permute-start(bf16[256,4096]{1,0:T(8,128)(2,1)} %get-tuple-element.83), channel_id=1, source_target_pairs={{0,1},{1,0},{2,3},{3,2},{4,5},{5,4},{6,7},{7,6},{8,9},{9,8},{10,11... | collective-permute-start | bytes 6291464 | tf_op jit(solution)/shard_map/ppermute | solution.py:446
  42.9 22.4 %collective-permute-start.11 = (bf16[8,64,1792]{2,1,0:T(8,128)(2,1)}, bf16[8,64,1792]{2,1,0:T(8,128)(2,1)S(1)}, u32[]{:S(2)}, u32[]{:S(2)}) collective-permute-start(bf16[8,64,1792]{2,1,0:T(8,128)(2,1)} %get-tuple-element.81), channel_id=1, source_target_pairs={{0,1},{1,0},{2,3},{3,2},{4,5},{5,4},{6,7},{7,6},{8,9},{9,8},{10,11... | collective-permute-start | bytes 5505032 | tf_op jit(solution)/shard_map/ppermute | solution.py:439
  43.4 6.0 %collective-permute-start.10 = (f32[128,128]{1,0:T(8,128)S(1)}, f32[128,128]{1,0:T(8,128)S(1)}, u32[]{:S(2)}, u32[]{:S(2)}) collective-permute-start(f32[128,128]{1,0:T(8,128)S(1)} %get-tuple-element.78), channel_id=1, source_target_pairs={{0,1},{1,0},{2,3},{3,2},{4,5},{5,4},{6,7},{7,6},{8,9},{9,8},{10,11... | collective-permute-start | bytes 196616 | tf_op jit(solution)/shard_map/ppermute | solution.py:445
  49.4 4.0 %collective-permute-start.12 = (bf16[128,128]{1,0:T(8,128)(2,1)S(1)}, bf16[128,128]{1,0:T(8,128)(2,1)S(1)}, u32[]{:S(2)}, u32[]{:S(2)}) collective-permute-start(bf16[128,128]{1,0:T(8,128)(2,1)S(1)} %multiply_convert_fusion.coeff_ref), channel_id=1, source_target_pairs={{0,2},{1,3},{2,0},{3,1},{4,6},{5,7},{6,4},{7,5},{8,10},{9,11},{10,... | collective-permute-start | bytes 98312 | tf_op jit(solution)/shard_map/ppermute | solution.py:450
  53.4 4.0 %collective-permute-start.13 = (bf16[128,128]{1,0:T(8,128)(2,1)S(1)}, bf16[128,128]{1,0:T(8,128)(2,1)S(1)}, u32[]{:S(2)}, u32[]{:S(2)}) collective-permute-start(bf16[128,128]{1,0:T(8,128)(2,1)S(1)} %add.27), channel_id=1, source_target_pairs={{0,4},{1,5},{2,6},{3,7},{4,0},{5,1},{6,2},{7,3},{8,12},{9,13},{10,... | collective-permute-start | bytes 98312 | tf_op jit(solution)/shard_map/ppermute | solution.py:450
  57.4 7.8 %collective-permute-start.14 = (bf16[128,128]{1,0:T(8,128)(2,1)S(1)}, bf16[128,128]{1,0:T(8,128)(2,1)S(1)}, u32[]{:S(2)}, u32[]{:S(2)}) collective-permute-start(bf16[128,128]{1,0:T(8,128)(2,1)S(1)} %add.28), channel_id=1, source_target_pairs={{0,8},{1,9},{2,10},{3,11},{4,12},{5,13},{6,14},{7,15},{8,0},{9,1},... | collective-permute-start | bytes 98312 | tf_op jit(solution)/shard_map/ppermute | solution.py:450
  60.1 3.9 %collective-permute-start.3 = (s32[1]{0:T(128)}, s32[1]{0:T(128)}, u32[]{:S(2)}, u32[]{:S(2)}) collective-permute-start(s32[1]{0:T(128)} %get-tuple-element.71), channel_id=1, source_target_pairs={{0,16},{16,0},{1,17},{17,1},{2,18},{18,2},{3,19},{19,3},{4,20},{20... | collective-permute-start | bytes 20 | tf_op jit(solution)/shard_map/ppermute | solution.py:387
  65.2 1.2 copy-start.9
  73.3 14.8 %copy-start.11 = (bf16[128,256]{1,0:T(8,128)(2,1)S(1)}, bf16[128,256]{1,0:T(8,128)(2,1)}, u32[]{:S(2)}) copy-start(bf16[128,256]{1,0:T(8,128)(2,1)} %get-tuple-element.72.choose_ref) | copy-start | bytes 196612
  73.3 14.7 %copy-start.12 = (f32[128,128]{1,0:T(8,128)S(1)}, f32[128,128]{1,0:T(8,128)}, u32[]{:S(2)}) copy-start(f32[128,128]{1,0:T(8,128)} %get-tuple-element.73.live_ref) | copy-start | bytes 196612
  73.3 14.7 %copy-start.13 = (bf16[128,128]{1,0:T(8,128)(2,1)S(1)}, bf16[128,128]{1,0:T(8,128)(2,1)}, u32[]{:S(2)}) copy-start(bf16[128,128]{1,0:T(8,128)(2,1)} %get-tuple-element.74.fixed_ref) | copy-start | bytes 98308
  89.2 52.7 %copy-start.7 = (s32[256,128]{1,0:T(8,128)S(1)}, s32[256,128]{1,0:T(8,128)}, u32[]{:S(2)}) copy-start(s32[256,128]{1,0:T(8,128)} %copy-done.6) | copy-start | bytes 393220
  89.2 52.7 %copy-start.8 = (f32[256,1792]{1,0:T(8,128)S(1)}, f32[256,1792]{1,0:T(8,128)}, u32[]{:S(2)}) copy-start(f32[256,1792]{1,0:T(8,128)} %fusion.base_ref) | copy-start | bytes 5505028
  89.2 52.7 %copy-start.10 = (bf16[8,48,1792]{2,1,0:T(8,128)(2,1)S(1)}, bf16[8,48,1792]{2,1,0:T(8,128)(2,1)}, u32[]{:S(2)}) copy-start(bf16[8,48,1792]{2,1,0:T(8,128)(2,1)} %get-tuple-element.94.extra_ref) | copy-start | bytes 4128772

commit v2 on v1

--- a/solution.py
+++ b/solution.py
@@ -31,18 +31,25 @@
     return pltpu.CompilerParams(vmem_limit_bytes=buffers + (8 << 20))
 
 
-def split_for_pair(up_factor, core, chips):
+def split_for_pair(up_factor, down_factor, core, chips):
     rank_width, hidden = up_factor.shape
     width = hidden // (2 * chips)
-
-    def kernel(core_ref, source, mine, other, sems):
-        copies = []
+    features = down_factor.shape[1] // 2
+
+    def kernel(core_ref, source, down, mine, other, half_down, sems):
+        core = core_ref[0]
+        start = pl.multiple_of((1 - core) * features, features)
+        copies = [
+            pltpu.make_async_copy(
+                down.at[:, pl.ds(start, features)], half_down, sems.at[2 * chips]
+            )
+        ]
         for q in range(chips):
-            for target, half in ((mine, core_ref[0]), (other, 1 - core_ref[0])):
+            for i, (target, half) in enumerate(((other, 1 - core), (mine, core))):
                 start = pl.multiple_of((2 * q + half) * width, width)
                 copies.append(
                     pltpu.make_async_copy(
-                        source.at[:, pl.ds(start, width)], target.at[q], sems.at[len(copies)]
+                        source.at[:, pl.ds(start, width)], target.at[q], sems.at[2 * q + i]
                     )
                 )
         for copy in copies:
@@ -53,15 +60,18 @@
     block = jax.ShapeDtypeStruct((chips, rank_width, width), up_factor.dtype)
     return pl.pallas_call(
         kernel,
-        in_specs=[pl.BlockSpec(memory_space=pltpu.SMEM), pl.BlockSpec(memory_space=pl.ANY)],
-        out_specs=[pl.BlockSpec(memory_space=pltpu.VMEM)] * 2,
-        out_shape=[block, block],
-        scratch_shapes=[pltpu.SemaphoreType.DMA((2 * chips,))],
-        compiler_params=vmem(2 * rank_width * hidden),
+        in_specs=[pl.BlockSpec(memory_space=pltpu.SMEM)]
+        + [pl.BlockSpec(memory_space=pltpu.HBM)] * 2,
+        out_specs=[pl.BlockSpec(memory_space=pltpu.VMEM)] * 3,
+        out_shape=[
+            block, block, jax.ShapeDtypeStruct((rank_width, features), down_factor.dtype)
+        ],
+        scratch_shapes=[pltpu.SemaphoreType.DMA((2 * chips + 1,))],
+        compiler_params=vmem(2 * rank_width * (hidden + features)),
         cost_estimate=pl.CostEstimate(
             flops=0, bytes_accessed=4 * rank_width * hidden, transcendentals=0
         ),
-    )(core, up_factor)
+    )(core, up_factor, down_factor)
 
 
 def describe(ranks, adapter_slot, segment_lengths, segment_adapter, position, total_rows, limit):
@@ -70,10 +80,22 @@
     shift = rank_width.bit_length() - 1
 
     def kernel(
-        ranks_ref, home_ref, length_ref, adapter_ref, position_ref,
+        ranks_in, home_in, length_in, adapter_in, position_ref,
         gain_ref, own_ref, choose_ref, live_ref, fixed_ref, code_ref, begin_ref, full_ref,
-        rank_of, rows_of, used, factor, order,
+        rank_of, rows_of, used, factor, order, ranks_ref, home_ref, length_ref, adapter_ref, sems,
     ):
+        pairs = zip(
+            (ranks_in, home_in, length_in, adapter_in),
+            (ranks_ref, home_ref, length_ref, adapter_ref),
+        )
+        copies = [
+            pltpu.make_async_copy(source, target, sems.at[i])
+            for i, (source, target) in enumerate(pairs)
+        ]
+        for copy in copies:
+            copy.start()
+        for copy in copies:
+            copy.wait()
         for a in range(slots):
             rows_of[a] = 0
             rank_of[home_ref[a]] = ranks_ref[a]
@@ -134,7 +156,7 @@
     smem, whole = pl.BlockSpec(memory_space=pltpu.SMEM), pl.BlockSpec(memory_space=pltpu.VMEM)
     return pl.pallas_call(
         kernel,
-        in_specs=[smem] * 5,
+        in_specs=[pl.BlockSpec(memory_space=pltpu.HBM)] * 4 + [smem],
         out_specs=[whole] * 6 + [smem] * 2,
         out_shape=[
             jax.ShapeDtypeStruct((total_rows // 2, limit), jnp.float32),
@@ -146,7 +168,11 @@
             jax.ShapeDtypeStruct((slots,), jnp.int32),
             jax.ShapeDtypeStruct((1,), jnp.int32),
         ],
-        scratch_shapes=[pltpu.SMEM((slots,), jnp.int32)] * 4 + [pltpu.SMEM((segments,), jnp.int32)],
+        scratch_shapes=[pltpu.SMEM((slots,), jnp.int32)] * 4
+        + [pltpu.SMEM((segments,), jnp.int32)]
+        + [pltpu.SMEM((slots,), jnp.int32)] * 2
+        + [pltpu.SMEM((segments,), jnp.int32)] * 2
+        + [pltpu.SemaphoreType.DMA((4,))],
         compiler_params=vmem(16 * total_rows * limit),
         cost_estimate=pl.CostEstimate(
             flops=200 * total_rows * limit, bytes_accessed=16 * total_rows * limit, transcendentals=0
@@ -416,39 +442,29 @@
         send = lax.dynamic_slice_in_dim(value, (1 - core) * features, features, 1)
         return keep, lax.ppermute(send, "tensor", sibling)
 
+    mine, other, down_half = split_for_pair(adapter_up[0], adapter_down[0], core[None], chips)
     block = jnp.concatenate(swap(input_rows), axis=0)
-    side = {}
+    block, mine, other, down_half = lax.optimization_barrier((block, mine, other, down_half))
+    other = lax.ppermute(other, "tensor", sibling)
+    down_half = lax.ppermute(down_half, "tensor", sibling)
+    gain, own, choose, live, fixed, code, begin, full = describe(
+        ranks, adapter_slot, segment_lengths, segment_adapter, position[None], total_rows, limit
+    )
+    fullest = largest_over_groups(full)
+    pending = [(own, choose), (fullest, other, down_half)]
 
     def halfway(step, piece):
-        if step == 1:
-            up, down, piece = lax.optimization_barrier((adapter_up[0], adapter_down[0], piece))
-            side["up"] = split_for_pair(up, core[None], chips)
-            side["down"] = swap(down)[1]
-            side["tables"] = describe(
-                ranks, adapter_slot, segment_lengths, segment_adapter, position[None],
-                total_rows, limit,
-            )
-        if step == 2:
-            piece, side["up"], side["tables"] = lax.optimization_barrier(
-                (piece, side["up"], side["tables"])
-            )
+        nonlocal pending
+        if step <= len(pending):
+            piece, pending[step - 1] = lax.optimization_barrier((piece, pending[step - 1]))
         return piece
 
     blocks, places = ring_gather(block, shards, halfway)
-    mine, other = side["up"]
-    other = lax.ppermute(other, "tensor", sibling)
-    gain, own, choose, live, fixed, code, begin, full = side["tables"]
-    fullest = largest_over_groups(full)
-    rows, shrink = collect_rows(
-        blocks, places, core[None], adapter_down[0], side["down"], own
-    )
+    (own, choose), (fullest, other, down_half) = pending
+    rows, shrink = collect_rows(blocks, places, core[None], adapter_down[0], down_half, own)
     shrink = shrink + lax.ppermute(shrink, "tensor", sibling)
-    rows_other = lax.ppermute(rows, "tensor", sibling)
     coeff = (shrink * gain).astype(jnp.bfloat16)
-    every, bit = coeff, 2
-    while bit < shards:
-        every = every + lax.ppermute(every, "tensor", [(t, t ^ bit) for t in range(shards)])
-        bit *= 2
+    coeff, rows = lax.optimization_barrier((coeff, rows))
 
     def payload(low, count):
         return build_payload(choose, live, fixed, coeff, mine, other, low, count)
@@ -464,13 +480,20 @@
         )
 
     near = payload(0, FIRST_ROWS)
+    rows_other = lax.ppermute(rows, "tensor", sibling)
+    every, bit = coeff, 2
+    while bit < shards:
+        every = every + lax.ppermute(every, "tensor", [(t, t ^ bit) for t in range(shards)])
+        if bit == 2:
+            every, near = lax.optimization_barrier((every, near))
+        bit *= 2
     near, every, rows, rows_other = lax.optimization_barrier((near, every, rows, rows_other))
     incoming = exchange(near)
     halves = [jnp.where(core == c, rows, rows_other) for c in range(2)]
     base = jnp.dot(
         jnp.concatenate(halves, axis=1), up_weight, preferred_element_type=jnp.float32
     )
-    fullest, base = lax.optimization_barrier((fullest, base))
+    fullest, base, incoming = lax.optimization_barrier((fullest, base, incoming))
     rest = limit - FIRST_ROWS
     extra = lax.cond(
         fullest[0] > FIRST_ROWS,

time: 147 us -> 121 us (0.82)
  blocking collectives: 52.7 us -> 0 us
  waiting for transfers between devices: 27.2 us -> 55.4 us
  starting transfers between devices: 17.7 us -> 20.8 us
  local copies, waits for them, and re-layouts: 11.4 us -> 8.53 us
  Pallas kernels: 18.6 us -> 16.8 us
    all_to_all x1 -> x0, blocking collectives: 52.7 us -> none  [exchange(): lax.all_to_all(value, 'tensor', split_axis=0, concat_axis=0, axis_index_g...]
    all_to_all x0 -> x1, waiting for transfers between devices: none -> 33.3 us  [exchange(): lax.all_to_all(value, 'tensor', split_axis=0, concat_axis=0, axis_index_g...]
    all_to_all x0 -> x1, starting transfers between devices: none -> 5.13 us  [exchange(): lax.all_to_all(value, 'tensor', split_axis=0, concat_axis=0, axis_index_g...]
    ppermute x4, waiting for transfers between devices: 1.42 us -> 6.24 us  [ring_gather(): held[-step] = lax.ppermute(held[1 - step], 'tensor', ahead)]
    ppermute x1, waiting for transfers between devices: 5.95 us -> 1.24 us  [pooled(): shrink = shrink + lax.ppermute(shrink, 'tensor', sibling)]
    ppermute x3, waiting for transfers between devices: 11.9 us -> 7.85 us  [ring_gather(): held[step] = lax.ppermute(held[step - 1], 'tensor', back)]
    dynamic_slice x1 -> x0, local copies, waits for them, and re-layouts: 1.96 us -> none  [swap(): send = lax.dynamic_slice_in_dim(value, (1 - core) * features, features, 1)]
    unnamed x28 -> x40, local copies, waits for them, and re-layouts: 6.57 us -> 5.48 us
  transfers between devices with their start and end apart: 16 -> 17, of which waited for: 9 -> 11; matrix products, arithmetic and copies ran while one was open for 2% -> 15% of each run, Pallas kernels for 6% -> 7%
where the time goes in v2:
time: 121 us; the launch traced here: 120 us
  waiting for transfers between devices  55.4 us (46%)
  starting transfers between devices  20.8 us (17%)
  Pallas kernels  16.8 us (14%)
  matrix products  14.7 us (12%)
  local copies, waits for them, and re-layouts  8.53 us (7%)
  other arithmetic  2.57 us (2%)
  between operations  1.52 us (1%)
    all_to_all x1, waiting for transfers between devices, exchange(): lax.all_to_all(value, 'tensor', split_axis=0, concat_axis=0, axis_index_g...  33.3 us
    dot_general x1, matrix products, pooled(): jnp.dot(jnp.concatenate(halves, axis=1), up_weight, preferred_element_typ...  14.7 us
    ppermute x3, waiting for transfers between devices, ring_gather(): held[step] = lax.ppermute(held[step - 1], 'tensor', back)  7.85 us
    ppermute x4, starting transfers between devices, ring_gather(): held[-step] = lax.ppermute(held[1 - step], 'tensor', ahead)  7.5 us
    ppermute x4, waiting for transfers between devices, ring_gather(): held[-step] = lax.ppermute(held[1 - step], 'tensor', ahead)  6.24 us
    unnamed x40, local copies, waits for them, and re-layouts  5.48 us
    ppermute x3, starting transfers between devices, pooled(): lax.ppermute(every, 'tensor', [(t, t ^ bit) for t in range(shards)])  5.39 us
    all_to_all x1, starting transfers between devices, exchange(): lax.all_to_all(value, 'tensor', split_axis=0, concat_axis=0, axis_index_g...  5.13 us
  transfers between devices with their start and end apart: 17, of which 11 were waited for; matrix products, arithmetic and copies ran while one was open for 15% of the time, Pallas kernels for 7%

profile of v2, /device:TPU:0, one launch (start us, length us, event | category | flops | bytes accessed | tf_op | source)
XLA Modules:
  0.0 120.4 jit_solution(4674290288741677699)
XLA Ops:
  0.0 1.0 constant_dynamic-slice_fusion.2
  1.5 1.2 %copy-done = bf16[1,64,8192]{2,1,0:T(8,128)(2,1)S(1)} copy-done((bf16[1,64,8192]{2,1,0:T(8,128)(2,1)S(1)}, bf16[1,64,8192]{2,1,0:T(8,128)(2,1)}, u32[]{:S(2)}) %copy-start) | copy-done | bytes 1048600
  2.7 2.0 %copy-done.2 = bf16[1,64,28672]{2,1,0:T(8,128)(2,1)S(1)} copy-done((bf16[1,64,28672]{2,1,0:T(8,128)(2,1)S(1)}, bf16[1,64,28672]{2,1,0:T(8,128)(2,1)}, u32[]{:S(2)}) %copy-start.2) | copy-done | bytes 3670040
  4.8 2.2 %shard_map.92 = (bf16[8,64,1792]{2,1,0:T(8,128)(2,1)}, bf16[8,64,1792]{2,1,0:T(8,128)(2,1)S(1)}, bf16[64,4096]{1,0:T(8,128)(2,1)S(1)}) custom-call(s32[1]{0:T(128)} %bitcast.1.core_ref, bf16[64,28672]{1,0:T(8,128)(2,1)S(1)} %bitcast.10, bf16[64,8192]{1,0:T(8,128)(2,1)S(1)} %bitcast.8), custom_call_target="tpu_custom_call" | custom-call | bytes 7340032 | tf_op jit(solution)/shard_map/pallas_call | solution.py:61
  7.1 3.0 %collective-permute-start.1 = (bf16[32,4096]{1,0:T(8,128)(2,1)S(1)}, bf16[32,4096]{1,0:T(8,128)(2,1)S(1)}, u32[]{:S(2)}, u32[]{:S(2)}) collective-permute-start(bf16[32,4096]{1,0:T(8,128)(2,1)S(1)} %pad_maximum_fusion.refs_0_), channel_id=1, source_target_pairs={{0,4},{1,5},{4,8},{5,9},{8,12},{9,13},{12,14},{13,15},{14,10},{15,... | collective-permute-start | bytes 786440 | tf_op jit(solution)/shard_map/ppermute | solution.py:397
  10.2 2.1 %shard_map.91 = (f32[128,128]{1,0:T(8,128)S(1)}, f32[128,128]{1,0:T(8,128)S(1)}, bf16[128,256]{1,0:T(8,128)(2,1)}, f32[128,128]{1,0:T(8,128)}, bf16[128,128]{1,0...) custom-call(s32[16]{0:T(128)S(1)} %copy-done.4, s32[16]{0:T(128)S(1)} %copy-done.5, ...), custom_call_target="tpu_custom_call" | custom-call | flops 6553600 | bytes 524288 | tf_op jit(solution)/shard_map/pallas_call | solution.py:157
  13.0 3.6 %collective-permute-done.1.refs_1_ = bf16[32,4096]{1,0:T(8,128)(2,1)S(1)} collective-permute-done((bf16[32,4096]{1,0:T(8,128)(2,1)S(1)}, bf16[32,4096]{1,0:T(8,128)(2,1)S(1)}, u32[]{:S(2)}, u32[]{:S(2)}) %collective-permute-start.1) | collective-permute-done | bytes 262176 | tf_op jit(solution)/shard_map/ppermute | solution.py:397
  16.7 1.8 %collective-permute-start.2 = (bf16[32,4096]{1,0:T(8,128)(2,1)S(1)}, bf16[32,4096]{1,0:T(8,128)(2,1)S(1)}, u32[]{:S(2)}, u32[]{:S(2)}) collective-permute-start(bf16[32,4096]{1,0:T(8,128)(2,1)S(1)} %collective-permute-done.1.refs_1_), channel_id=1, source_target_pairs={{0,4},{1,5},{4,8},{5,9},{8,12},{9,13},{12,14},{13,15},{14,10},{15,... | collective-permute-start | bytes 786440 | tf_op jit(solution)/shard_map/ppermute | solution.py:397
  18.4 1.5 %collective-permute-start.3 = (s32[1]{0:T(128)}, s32[1]{0:T(128)}, u32[]{:S(2)}, u32[]{:S(2)}) collective-permute-start(s32[1]{0:T(128)} %get-tuple-element.69), channel_id=1, source_target_pairs={{0,16},{16,0},{1,17},{17,1},{2,18},{18,2},{3,19},{19,3},{4,20},{20... | collective-permute-start | bytes 20 | tf_op jit(solution)/shard_map/ppermute | solution.py:413
  19.9 2.2 %collective-permute-done.3 = s32[1]{0:T(128)} collective-permute-done((s32[1]{0:T(128)}, s32[1]{0:T(128)}, u32[]{:S(2)}, u32[]{:S(2)}) %collective-permute-start.3) | collective-permute-done | bytes 36 | tf_op jit(solution)/shard_map/ppermute | solution.py:413
  24.4 1.5 %collective-permute-start.8 = (bf16[32,4096]{1,0:T(8,128)(2,1)S(1)}, bf16[32,4096]{1,0:T(8,128)(2,1)S(1)}, u32[]{:S(2)}, u32[]{:S(2)}) collective-permute-start(bf16[32,4096]{1,0:T(8,128)(2,1)S(1)} %collective-permute-done.2.refs_3_), channel_id=1, source_target_pairs={{0,4},{1,5},{4,8},{5,9},{8,12},{9,13},{12,14},{13,15},{14,10},{15,... | collective-permute-start | bytes 786440 | tf_op jit(solution)/shard_map/ppermute | solution.py:397
  25.9 4.4 %collective-permute-done.7.refs_4_ = bf16[32,4096]{1,0:T(8,128)(2,1)S(1)} collective-permute-done((bf16[32,4096]{1,0:T(8,128)(2,1)S(1)}, bf16[32,4096]{1,0:T(8,128)(2,1)S(1)}, u32[]{:S(2)}, u32[]{:S(2)}) %collective-permute-start.7) | collective-permute-done | bytes 262176 | tf_op jit(solution)/shard_map/ppermute | solution.py:399
  30.4 0.9 collective-permute-done.8.refs_5_
  31.3 1.1 collective-permute-start.10
  33.3 3.4 %collective-permute-done.9.refs_6_ = bf16[32,4096]{1,0:T(8,128)(2,1)S(1)} collective-permute-done((bf16[32,4096]{1,0:T(8,128)(2,1)S(1)}, bf16[32,4096]{1,0:T(8,128)(2,1)S(1)}, u32[]{:S(2)}, u32[]{:S(2)}) %collective-permute-start.9) | collective-permute-done | bytes 262176 | tf_op jit(solution)/shard_map/ppermute | solution.py:399
  36.8 1.0 collective-permute-done.10.refs_7_
  37.8 4.6 %shard_map.93 = (bf16[256,4096]{1,0:T(8,128)(2,1)S(1)}, f32[128,128]{1,0:T(8,128)S(1)}) custom-call(s32[16]{0:T(128)S(1)} %fusion.4.places_ref, s32[1]{0:T(128)} %bitcast.1.core_ref, f32[128,128]{1,0:T(8,128)S(1)} %get-tuple-element.73.own_ref, bf16[32,4096]{1,0:T(8,128)(2,1)S(1)} %pad_maximum_fusion.refs_0_, ...), custom_call_target="tpu_custom_call" | custom-call | flops 268435456 | bytes 4194304 | tf_op jit(solution)/shard_map/pallas_call | solution.py:241
  42.5 1.2 %collective-permute-done.11 = f32[128,128]{1,0:T(8,128)S(1)} collective-permute-done((f32[128,128]{1,0:T(8,128)S(1)}, f32[128,128]{1,0:T(8,128)S(1)}, u32[]{:S(2)}, u32[]{:S(2)}) %collective-permute-start.11) | collective-permute-done | bytes 65568 | tf_op jit(solution)/shard_map/ppermute | solution.py:465
  44.0 1.1 collective-permute-start.12
  45.1 3.6 %shard_map.94 = bf16[8,80,1792]{2,1,0:T(8,128)(2,1)} custom-call(bf16[128,256]{1,0:T(8,128)(2,1)S(1)} %copy-done.14, f32[128,128]{1,0:T(8,128)S(1)} %copy-done.16, bf16[128,128]{1,0:T(8,128)(2,1)S(1)} %copy-done.18, bf16[128,128]{1,0:T(8,128)(2,1)S(1)} %multiply_convert_fusion.coeff_ref, bf16[8,64,1792]{2,1,0:T(8,128)(2,1)S(1)} %copy-done.11, ...), custom_call_target="tpu_custom_call" | custom-call | flops 293601280 | bytes 5963776 | tf_op jit(solution)/shard_map/pallas_call | solution.py:284
  48.7 1.6 %collective-permute-start.13 = (bf16[128,128]{1,0:T(8,128)(2,1)S(1)}, bf16[128,128]{1,0:T(8,128)(2,1)S(1)}, u32[]{:S(2)}, u32[]{:S(2)}) collective-permute-start(bf16[128,128]{1,0:T(8,128)(2,1)S(1)} %add.26), channel_id=1, source_target_pairs={{0,4},{1,5},{2,6},{3,7},{4,0},{5,1},{6,2},{7,3},{8,12},{9,13},{10,... | collective-permute-start | bytes 98312 | tf_op jit(solution)/shard_map/ppermute | solution.py:486
  50.3 2.3 %collective-permute-done.13 = bf16[128,128]{1,0:T(8,128)(2,1)S(1)} collective-permute-done((bf16[128,128]{1,0:T(8,128)(2,1)S(1)}, bf16[128,128]{1,0:T(8,128)(2,1)S(1)}, u32[]{:S(2)}, u32[]{:S(2)}) %collective-permute-start.13) | collective-permute-done | bytes 32800 | tf_op jit(solution)/shard_map/ppermute | solution.py:486
  52.7 2.7 %collective-permute-start.14 = (bf16[128,128]{1,0:T(8,128)(2,1)S(1)}, bf16[128,128]{1,0:T(8,128)(2,1)S(1)}, u32[]{:S(2)}, u32[]{:S(2)}) collective-permute-start(bf16[128,128]{1,0:T(8,128)(2,1)S(1)} %add.27), channel_id=1, source_target_pairs={{0,8},{1,9},{2,10},{3,11},{4,12},{5,13},{6,14},{7,15},{8,0},{9,1},... | collective-permute-start | bytes 98312 | tf_op jit(solution)/shard_map/ppermute | solution.py:486
  55.4 2.2 %collective-permute-done.14 = bf16[128,128]{1,0:T(8,128)(2,1)S(1)} collective-permute-done((bf16[128,128]{1,0:T(8,128)(2,1)S(1)}, bf16[128,128]{1,0:T(8,128)(2,1)S(1)}, u32[]{:S(2)}, u32[]{:S(2)}) %collective-permute-start.14) | collective-permute-done | bytes 32800 | tf_op jit(solution)/shard_map/ppermute | solution.py:486
  57.6 5.1 %all-to-all-start.1 = ((bf16[8,80,1792]{2,1,0:T(8,128)(2,1)}), bf16[8,80,1792]{2,1,0:T(8,128)(2,1)S(1)}, u32[]{:S(2)}, u32[]{:S(2)}) async-start(bf16[8,80,1792]{2,1,0:T(8,128)(2,1)} %shard_map.94), calls=%async_computation.1 | async-start | bytes 4587520 | tf_op jit(solution)/shard_map/all_to_all | solution.py:473
  62.7 2.5 %broadcast_select_fusion.1 = (bf16[256,4096]{1,0:T(8,128)(2,1)S(1)}, bf16[256,4096]{1,0:T(8,128)(2,1)S(1)}) fusion(bf16[256,4096]{1,0:T(8,128)(2,1)} %copy-done.3, bf16[256,4096]{1,0:T(8,128)(2,1)} %collective-permute-done.15, pred[]{:T(512)S(6)} %eq.6, pred[]{:T(512)S(6)} %eq.7), kind=kLoop, calls=%fused_computation.5 | loop fusion | flops 2097152 | bytes 8388610 | tf_op jit(solution)/shard_map/jit(_where)/select_n | solution.py:492
  65.3 14.7 %fusion.base_ref = f32[256,1792]{1,0:T(8,128)} fusion(bf16[8192,1792]{1,0:T(8,128)(2,1)} %param.12, bf16[256,4096]{1,0:T(8,128)(2,1)S(1)} %get-tuple-element.97, bf16[256,4096]{1,0:T(8,128)(2,1)S(1)} %get-tuple-element.96), kind=kOutput, calls=%fused_computation | convolution fusion | flops 7524581376 | bytes 35389440 | tf_op jit(solution)/shard_map/dot_general | solution.py:493
  80.0 33.3 %all-to-all-done.1.incoming_ref = bf16[8,80,1792]{2,1,0:T(8,128)(2,1)S(1)} async-done(((bf16[8,80,1792]{2,1,0:T(8,128)(2,1)}), bf16[8,80,1792]{2,1,0:T(8,128)(2,1)S(1)}, u32[]{:S(2)}, u32[]{:S(2)}) %all-to-all-start.1) | async-done | bytes 2293792 | tf_op jit(solution)/shard_map/all_to_all | solution.py:473
  113.3 1.2 %conditional.1 = (bf16[8,48,1792]{2,1,0:T(8,128)(2,1)}) conditional(s32[]{:T(128)} %bitcast.5, () %tuple.25, (bf16[128,256]{1,0:T(8,128)(2,1)S(1)}, f32[128,128]{1,0:T(8,128)S(1)}, bf16[128,128]{1,0:T(8,128)(2,1)S(1)}, bf16[128,128]{1,0:T(8,128)(2,1)S(1)}, bf16[8,64,1792]{2,1,0:T(8,128)(2,1)}, /*index=5*/bf16[8,64,1792]{2,1,0:T(8,128)(2,1)}) %tuple.34), branch_computations={%region_0.1_spmd, %region_1.2_spmd} | conditional | flops 176160768 | bytes 7798792 | solution.py:498
  113.3 1.2 %broadcast.2 = bf16[8,48,1792]{2,1,0:T(8,128)(2,1)} broadcast(bf16[]{:T(256)} %constant.9.clone), dimensions={} | broadcast | bytes 1376258 | tf_op jit(solution)/shard_map/broadcast.1
  114.6 1.5 %copy-done.10 = f32[256,1792]{1,0:T(8,128)S(1)} copy-done((f32[256,1792]{1,0:T(8,128)S(1)}, f32[256,1792]{1,0:T(8,128)}, u32[]{:S(2)}) %copy-start.10) | copy-done | bytes 1835032
  116.1 4.3 %shard_map.95 = bf16[256,1792]{1,0:T(8,128)(2,1)} custom-call(s32[16]{0:T(128)S(1)} %get-tuple-element.61.begin_ref, s32[1]{0:T(128)S(6)} %max.3.more_ref, f32[256,1792]{1,0:T(8,128)S(1)} %copy-done.10, s32[256,128]{1,0:T(8,128)S(1)} %copy-done.9, bf16[128,128]{1,0:T(8,128)(2,1)S(1)} %add.28.coeff_ref, bf16[8,80,1792]{2,1,0:T(8,128)(2,1)S(1)} %all-to-all-done.1.incoming_ref, ...), custom_call_target="tpu_custom_call" | custom-call | flops 1879048192 | bytes 6422528 | tf_op jit(solution)/shard_map/pallas_call | solution.py:370
  (58 shorter events, 3.6 us)
Async XLA Ops:
  1.0 6.0 %collective-permute-start = (bf16[16,4096]{1,0:T(8,128)(2,1)S(1)}, bf16[16,4096]{1,0:T(8,128)(2,1)S(1)}, u32[]{:S(2)}, u32[]{:S(2)}) collective-permute-start(bf16[16,4096]{1,0:T(8,128)(2,1)S(1)} %get-tuple-element.99), channel_id=1, source_target_pairs={{0,1},{1,0},{2,3},{3,2},{4,5},{5,4},{6,7},{7,6},{8,9},{9,8},{10,11... | collective-permute-start | bytes 393224 | tf_op jit(solution)/shard_map/ppermute | solution.py:443
  4.8 5.4 %copy-start.4 = (s32[16]{0:T(128)S(1)}, s32[16]{0:T(128)}, u32[]{:S(2)}) copy-start(s32[16]{0:T(128)} %ranks_in.1) | copy-start | bytes 196
  4.8 5.4 %copy-start.5 = (s32[16]{0:T(128)S(1)}, s32[16]{0:T(128)}, u32[]{:S(2)}) copy-start(s32[16]{0:T(128)} %home_in.1) | copy-start | bytes 196
  4.8 5.4 %copy-start.6 = (s32[16]{0:T(128)S(1)}, s32[16]{0:T(128)}, u32[]{:S(2)}) copy-start(s32[16]{0:T(128)} %length_in.1) | copy-start | bytes 196
  4.8 5.4 %copy-start.7 = (s32[16]{0:T(128)S(1)}, s32[16]{0:T(128)}, u32[]{:S(2)}) copy-start(s32[16]{0:T(128)} %adapter_in.1) | copy-start | bytes 196
  4.8 33.0 %copy-start.1 = (bf16[1,64,8192]{2,1,0:T(8,128)(2,1)S(1)}, bf16[1,64,8192]{2,1,0:T(8,128)(2,1)}, u32[]{:S(2)}) copy-start(bf16[1,64,8192]{2,1,0:T(8,128)(2,1)} %param.13) | copy-start | bytes 3145732
  7.0 17.4 %collective-permute-start.4 = (bf16[8,64,1792]{2,1,0:T(8,128)(2,1)S(1)}, bf16[8,64,1792]{2,1,0:T(8,128)(2,1)S(1)}, u32[]{:S(2)}, u32[]{:S(2)}) collective-permute-start(bf16[8,64,1792]{2,1,0:T(8,128)(2,1)S(1)} %get-tuple-element.70), channel_id=1, source_target_pairs={{0,1},{1,0},{2,3},{3,2},{4,5},{5,4},{6,7},{7,6},{8,9},{9,8},{10,11... | collective-permute-start | bytes 5505032 | tf_op jit(solution)/shard_map/ppermute | solution.py:448
  7.1 9.5 %collective-permute-start.1 = (bf16[32,4096]{1,0:T(8,128)(2,1)S(1)}, bf16[32,4096]{1,0:T(8,128)(2,1)S(1)}, u32[]{:S(2)}, u32[]{:S(2)}) collective-permute-start(bf16[32,4096]{1,0:T(8,128)(2,1)S(1)} %pad_maximum_fusion.refs_0_), channel_id=1, source_target_pairs={{0,4},{1,5},{4,8},{5,9},{8,12},{9,13},{12,14},{13,15},{14,10},{15,... | collective-permute-start | bytes 786440 | tf_op jit(solution)/shard_map/ppermute | solution.py:397
  10.2 14.2 %collective-permute-start.5 = (bf16[64,4096]{1,0:T(8,128)(2,1)S(1)}, bf16[64,4096]{1,0:T(8,128)(2,1)S(1)}, u32[]{:S(2)}, u32[]{:S(2)}) collective-permute-start(bf16[64,4096]{1,0:T(8,128)(2,1)S(1)} %get-tuple-element.71), channel_id=1, source_target_pairs={{0,1},{1,0},{2,3},{3,2},{4,5},{5,4},{6,7},{7,6},{8,9},{9,8},{10,11... | collective-permute-start | bytes 1572872 | tf_op jit(solution)/shard_map/ppermute | solution.py:449
  13.0 10.5 %collective-permute-start.6 = (bf16[32,4096]{1,0:T(8,128)(2,1)S(1)}, bf16[32,4096]{1,0:T(8,128)(2,1)S(1)}, u32[]{:S(2)}, u32[]{:S(2)}) collective-permute-start(bf16[32,4096]{1,0:T(8,128)(2,1)S(1)} %pad_maximum_fusion.refs_0_), channel_id=1, source_target_pairs={{4,0},{5,1},{8,4},{9,5},{12,8},{13,9},{14,12},{15,13},{10,14},{11,... | collective-permute-start | bytes 786440 | tf_op jit(solution)/shard_map/ppermute | solution.py:399
  16.7 7.8 %collective-permute-start.2 = (bf16[32,4096]{1,0:T(8,128)(2,1)S(1)}, bf16[32,4096]{1,0:T(8,128)(2,1)S(1)}, u32[]{:S(2)}, u32[]{:S(2)}) collective-permute-start(bf16[32,4096]{1,0:T(8,128)(2,1)S(1)} %collective-permute-done.1.refs_1_), channel_id=1, source_target_pairs={{0,4},{1,5},{4,8},{5,9},{8,12},{9,13},{12,14},{13,15},{14,10},{15,... | collective-permute-start | bytes 786440 | tf_op jit(solution)/shard_map/ppermute | solution.py:397
  18.4 3.7 %collective-permute-start.3 = (s32[1]{0:T(128)}, s32[1]{0:T(128)}, u32[]{:S(2)}, u32[]{:S(2)}) collective-permute-start(s32[1]{0:T(128)} %get-tuple-element.69), channel_id=1, source_target_pairs={{0,16},{16,0},{1,17},{17,1},{2,18},{18,2},{3,19},{19,3},{4,20},{20... | collective-permute-start | bytes 20 | tf_op jit(solution)/shard_map/ppermute | solution.py:413
  23.5 6.9 %collective-permute-start.7 = (bf16[32,4096]{1,0:T(8,128)(2,1)S(1)}, bf16[32,4096]{1,0:T(8,128)(2,1)S(1)}, u32[]{:S(2)}, u32[]{:S(2)}) collective-permute-start(bf16[32,4096]{1,0:T(8,128)(2,1)S(1)} %collective-permute-done.6.refs_2_), channel_id=1, source_target_pairs={{4,0},{5,1},{8,4},{9,5},{12,8},{13,9},{14,12},{15,13},{10,14},{11,... | collective-permute-start | bytes 786440 | tf_op jit(solution)/shard_map/ppermute | solution.py:399
  24.4 6.9 %copy-start.12 = (bf16[8,64,1792]{2,1,0:T(8,128)(2,1)}, bf16[8,64,1792]{2,1,0:T(8,128)(2,1)S(1)}, u32[]{:S(2)}) copy-start(bf16[8,64,1792]{2,1,0:T(8,128)(2,1)S(1)} %collective-permute-done.4.other_ref) | copy-start | bytes 5505028
  24.4 6.9 %collective-permute-start.8 = (bf16[32,4096]{1,0:T(8,128)(2,1)S(1)}, bf16[32,4096]{1,0:T(8,128)(2,1)S(1)}, u32[]{:S(2)}, u32[]{:S(2)}) collective-permute-start(bf16[32,4096]{1,0:T(8,128)(2,1)S(1)} %collective-permute-done.2.refs_3_), channel_id=1, source_target_pairs={{0,4},{1,5},{4,8},{5,9},{8,12},{9,13},{12,14},{13,15},{14,10},{15,... | collective-permute-start | bytes 786440 | tf_op jit(solution)/shard_map/ppermute | solution.py:397
  30.4 6.4 %collective-permute-start.9 = (bf16[32,4096]{1,0:T(8,128)(2,1)S(1)}, bf16[32,4096]{1,0:T(8,128)(2,1)S(1)}, u32[]{:S(2)}, u32[]{:S(2)}) collective-permute-start(bf16[32,4096]{1,0:T(8,128)(2,1)S(1)} %collective-permute-done.7.refs_4_), channel_id=1, source_target_pairs={{4,0},{5,1},{8,4},{9,5},{12,8},{13,9},{14,12},{15,13},{10,14},{11,... | collective-permute-start | bytes 786440 | tf_op jit(solution)/shard_map/ppermute | solution.py:399
  31.3 6.5 %collective-permute-start.10 = (bf16[32,4096]{1,0:T(8,128)(2,1)S(1)}, bf16[32,4096]{1,0:T(8,128)(2,1)}, u32[]{:S(2)}, u32[]{:S(2)}) collective-permute-start(bf16[32,4096]{1,0:T(8,128)(2,1)S(1)} %collective-permute-done.8.refs_5_), channel_id=1, source_target_pairs={{0,4},{1,5},{4,8},{5,9},{8,12},{9,13},{12,14},{13,15},{14,10},{15,... | collective-permute-start | bytes 786440 | tf_op jit(solution)/shard_map/ppermute | solution.py:397
  32.5 12.6 %copy-start.11 = (bf16[8,64,1792]{2,1,0:T(8,128)(2,1)S(1)}, bf16[8,64,1792]{2,1,0:T(8,128)(2,1)}, u32[]{:S(2)}) copy-start(bf16[8,64,1792]{2,1,0:T(8,128)(2,1)} %get-tuple-element.83.mine_ref) | copy-start | bytes 5505028
  32.5 12.6 %copy-start.13 = (bf16[8,64,1792]{2,1,0:T(8,128)(2,1)S(1)}, bf16[8,64,1792]{2,1,0:T(8,128)(2,1)}, u32[]{:S(2)}) copy-start(bf16[8,64,1792]{2,1,0:T(8,128)(2,1)} %copy-done.12) | copy-start | bytes 5505028
  32.5 12.6 %copy-start.14 = (bf16[128,256]{1,0:T(8,128)(2,1)S(1)}, bf16[128,256]{1,0:T(8,128)(2,1)}, u32[]{:S(2)}) copy-start(bf16[128,256]{1,0:T(8,128)(2,1)} %get-tuple-element.80.choose_ref) | copy-start | bytes 196612
  32.5 12.6 %copy-start.16 = (f32[128,128]{1,0:T(8,128)S(1)}, f32[128,128]{1,0:T(8,128)}, u32[]{:S(2)}) copy-start(f32[128,128]{1,0:T(8,128)} %get-tuple-element.81.live_ref) | copy-start | bytes 196612
  32.5 12.6 %copy-start.18 = (bf16[128,128]{1,0:T(8,128)(2,1)S(1)}, bf16[128,128]{1,0:T(8,128)(2,1)}, u32[]{:S(2)}) copy-start(bf16[128,128]{1,0:T(8,128)(2,1)} %get-tuple-element.82.fixed_ref) | copy-start | bytes 98308
  42.4 6.3 %copy-start.3 = (bf16[256,4096]{1,0:T(8,128)(2,1)}, bf16[256,4096]{1,0:T(8,128)(2,1)S(1)}, u32[]{:S(2)}) copy-start(bf16[256,4096]{1,0:T(8,128)(2,1)S(1)} %get-tuple-element.88) | copy-start | bytes 6291460
  42.4 1.3 %collective-permute-start.11 = (f32[128,128]{1,0:T(8,128)S(1)}, f32[128,128]{1,0:T(8,128)S(1)}, u32[]{:S(2)}, u32[]{:S(2)}) collective-permute-start(f32[128,128]{1,0:T(8,128)S(1)} %get-tuple-element.76), channel_id=1, source_target_pairs={{0,1},{1,0},{2,3},{3,2},{4,5},{5,4},{6,7},{7,6},{8,9},{9,8},{10,11... | collective-permute-start | bytes 196616 | tf_op jit(solution)/shard_map/ppermute | solution.py:465
  43.8 13.8 %collective-permute-start.15 = (bf16[256,4096]{1,0:T(8,128)(2,1)S(1)}, bf16[256,4096]{1,0:T(8,128)(2,1)}, u32[]{:S(2)}, u32[]{:S(2)}) collective-permute-start(bf16[256,4096]{1,0:T(8,128)(2,1)S(1)} %get-tuple-element.88), channel_id=1, source_target_pairs={{0,1},{1,0},{2,3},{3,2},{4,5},{5,4},{6,7},{7,6},{8,9},{9,8},{10,11... | collective-permute-start | bytes 6291464 | tf_op jit(solution)/shard_map/ppermute | solution.py:483
  44.0 4.7 %collective-permute-start.12 = (bf16[128,128]{1,0:T(8,128)(2,1)S(1)}, bf16[128,128]{1,0:T(8,128)(2,1)S(1)}, u32[]{:S(2)}, u32[]{:S(2)}) collective-permute-start(bf16[128,128]{1,0:T(8,128)(2,1)S(1)} %multiply_convert_fusion.coeff_ref), channel_id=1, source_target_pairs={{0,2},{1,3},{2,0},{3,1},{4,6},{5,7},{6,4},{7,5},{8,10},{9,11},{10,... | collective-permute-start | bytes 98312 | tf_op jit(solution)/shard_map/ppermute | solution.py:486
  48.7 4.0 %collective-permute-start.13 = (bf16[128,128]{1,0:T(8,128)(2,1)S(1)}, bf16[128,128]{1,0:T(8,128)(2,1)S(1)}, u32[]{:S(2)}, u32[]{:S(2)}) collective-permute-start(bf16[128,128]{1,0:T(8,128)(2,1)S(1)} %add.26), channel_id=1, source_target_pairs={{0,4},{1,5},{2,6},{3,7},{4,0},{5,1},{6,2},{7,3},{8,12},{9,13},{10,... | collective-permute-start | bytes 98312 | tf_op jit(solution)/shard_map/ppermute | solution.py:486
  52.7 4.9 %collective-permute-start.14 = (bf16[128,128]{1,0:T(8,128)(2,1)S(1)}, bf16[128,128]{1,0:T(8,128)(2,1)S(1)}, u32[]{:S(2)}, u32[]{:S(2)}) collective-permute-start(bf16[128,128]{1,0:T(8,128)(2,1)S(1)} %add.27), channel_id=1, source_target_pairs={{0,8},{1,9},{2,10},{3,11},{4,12},{5,13},{6,14},{7,15},{8,0},{9,1},... | collective-permute-start | bytes 98312 | tf_op jit(solution)/shard_map/ppermute | solution.py:486
  57.6 55.7 %all-to-all-start.1 = ((bf16[8,80,1792]{2,1,0:T(8,128)(2,1)}), bf16[8,80,1792]{2,1,0:T(8,128)(2,1)S(1)}, u32[]{:S(2)}, u32[]{:S(2)}) async-start(bf16[8,80,1792]{2,1,0:T(8,128)(2,1)} %shard_map.94), calls=%async_computation.1 | async-start | bytes 4587520 | tf_op jit(solution)/shard_map/all_to_all | solution.py:473
  65.2 48.1 %copy-start.15 = (bf16[128,256]{1,0:T(8,128)(2,1)S(1)}, bf16[128,256]{1,0:T(8,128)(2,1)}, u32[]{:S(2)}) copy-start(bf16[128,256]{1,0:T(8,128)(2,1)} %get-tuple-element.80.choose_ref) | copy-start | bytes 196612
  65.2 48.1 %copy-start.17 = (f32[128,128]{1,0:T(8,128)S(1)}, f32[128,128]{1,0:T(8,128)}, u32[]{:S(2)}) copy-start(f32[128,128]{1,0:T(8,128)} %get-tuple-element.81.live_ref) | copy-start | bytes 196612
  65.3 48.1 %copy-start.19 = (bf16[128,128]{1,0:T(8,128)(2,1)S(1)}, bf16[128,128]{1,0:T(8,128)(2,1)}, u32[]{:S(2)}) copy-start(bf16[128,128]{1,0:T(8,128)(2,1)} %get-tuple-element.82.fixed_ref) | copy-start | bytes 98308
  (5 other events, 6.7 us)

commit v3 on v2

--- a/solution.py
+++ b/solution.py
@@ -8,7 +8,8 @@
 
 ADAPTER_ALPHA = 32.0
 POOLED_SHARDS = 16
-FIRST_ROWS = 80
+FIRST_ROWS = 64
+MORE_ROWS = (16, 32)
 
 
 def row_tables(row_count, ranks, adapter_slot, segment_lengths, segment_adapter):
@@ -306,9 +307,13 @@
 
     def kernel(
         begin_ref, more_ref, base_ref, code_ref, coeff_ref, incoming_ref, extra_ref,
-        out_ref, late, sem,
+        out_ref, late, base_part, near_rows, sems,
     ):
-        fetch = pltpu.make_async_copy(extra_ref, late, sem)
+        fetch = pltpu.make_async_copy(extra_ref, late, sems.at[0])
+        get_base = pltpu.make_async_copy(base_ref, base_part, sems.at[1])
+        get_near = pltpu.make_async_copy(incoming_ref, near_rows, sems.at[2])
+        get_near.start()
+        get_base.start()
         folded = coeff_ref[...].astype(jnp.float32)
         both = jnp.concatenate(
             [
@@ -342,14 +347,16 @@
             return total.astype(jnp.bfloat16)
 
         near = weights(0, first)
+        get_near.wait()
+        get_base.wait()
 
         def write(far):
             @pl.loop(0, width // tile)
             def _(i):
                 columns = pl.ds(pl.multiple_of(i * tile, tile), tile)
-                block = incoming_ref[:, :, columns].reshape(chips * first, tile)
+                block = near_rows[:, :, columns].reshape(chips * first, tile)
                 total = jnp.dot(near, block, preferred_element_type=jnp.float32)
-                total += base_ref[:, columns]
+                total += base_part[:, columns]
                 if far is not None:
                     block = late[:, :, columns].reshape(chips * second, tile)
                     total += jnp.dot(far, block, preferred_element_type=jnp.float32)
@@ -370,11 +377,17 @@
     return pl.pallas_call(
         kernel,
         in_specs=[smem] * 2
-        + [whole] * 4
-        + [pl.BlockSpec(memory_space=pl.ANY)],
+        + [pl.BlockSpec(memory_space=pl.ANY)]
+        + [whole] * 2
+        + [pl.BlockSpec(memory_space=pl.ANY)] * 2,
         out_specs=whole,
         out_shape=jax.ShapeDtypeStruct((total_rows, width), jnp.bfloat16),
-        scratch_shapes=[pltpu.VMEM(extra.shape, extra.dtype), pltpu.SemaphoreType.DMA(())],
+        scratch_shapes=[
+            pltpu.VMEM(extra.shape, extra.dtype),
+            pltpu.VMEM(base.shape, base.dtype),
+            pltpu.VMEM(incoming.shape, incoming.dtype),
+            pltpu.SemaphoreType.DMA((3,)),
+        ],
         compiler_params=vmem(8 * total_rows * width + 2 * chips * limit * width),
         cost_estimate=pl.CostEstimate(
             flops=4 * total_rows * chips * limit * width,
@@ -442,29 +455,32 @@
         send = lax.dynamic_slice_in_dim(value, (1 - core) * features, features, 1)
         return keep, lax.ppermute(send, "tensor", sibling)
 
-    mine, other, down_half = split_for_pair(adapter_up[0], adapter_down[0], core[None], chips)
     block = jnp.concatenate(swap(input_rows), axis=0)
-    block, mine, other, down_half = lax.optimization_barrier((block, mine, other, down_half))
-    other = lax.ppermute(other, "tensor", sibling)
-    down_half = lax.ppermute(down_half, "tensor", sibling)
-    gain, own, choose, live, fixed, code, begin, full = describe(
+    tables = describe(
         ranks, adapter_slot, segment_lengths, segment_adapter, position[None], total_rows, limit
     )
+    gain, own, choose, live, fixed, code, begin, full = tables
     fullest = largest_over_groups(full)
-    pending = [(own, choose), (fullest, other, down_half)]
+    packed = ()
 
     def halfway(step, piece):
-        nonlocal pending
-        if step <= len(pending):
-            piece, pending[step - 1] = lax.optimization_barrier((piece, pending[step - 1]))
+        nonlocal packed, own
+        if step == 1:
+            piece, own, which = lax.optimization_barrier((piece, own, core[None]))
+            packed = split_for_pair(adapter_up[0], adapter_down[0], which, chips)
+        if step == 2:
+            piece, packed = lax.optimization_barrier((piece, packed))
         return piece
 
     blocks, places = ring_gather(block, shards, halfway)
-    (own, choose), (fullest, other, down_half) = pending
+    mine, other, down_half = packed
+    down_half = lax.ppermute(down_half, "tensor", sibling)
+    blocks, other, down_half = lax.optimization_barrier((blocks, other, down_half))
+    other = lax.ppermute(other, "tensor", sibling)
     rows, shrink = collect_rows(blocks, places, core[None], adapter_down[0], down_half, own)
     shrink = shrink + lax.ppermute(shrink, "tensor", sibling)
     coeff = (shrink * gain).astype(jnp.bfloat16)
-    coeff, rows = lax.optimization_barrier((coeff, rows))
+    coeff, rows, fullest = lax.optimization_barrier((coeff, rows, fullest))
 
     def payload(low, count):
         return build_payload(choose, live, fixed, coeff, mine, other, low, count)
@@ -481,12 +497,12 @@
 
     near = payload(0, FIRST_ROWS)
     rows_other = lax.ppermute(rows, "tensor", sibling)
-    every, bit = coeff, 2
-    while bit < shards:
-        every = every + lax.ppermute(every, "tensor", [(t, t ^ bit) for t in range(shards)])
-        if bit == 2:
-            every, near = lax.optimization_barrier((every, near))
-        bit *= 2
+    every = coeff + lax.ppermute(coeff, "tensor", [(t, t ^ 2) for t in range(shards)])
+    every, near = lax.optimization_barrier((every, near))
+    shifts = [[(t, (t + 4 * k) % shards) for t in range(shards)] for k in range(1, shards // 4)]
+    others = [lax.ppermute(every, "tensor", hop) for hop in shifts]
+    for value in others:
+        every = every + value
     near, every, rows, rows_other = lax.optimization_barrier((near, every, rows, rows_other))
     incoming = exchange(near)
     halves = [jnp.where(core == c, rows, rows_other) for c in range(2)]
@@ -495,11 +511,20 @@
     )
     fullest, base, incoming = lax.optimization_barrier((fullest, base, incoming))
     rest = limit - FIRST_ROWS
-    extra = lax.cond(
-        fullest[0] > FIRST_ROWS,
-        lambda: exchange(payload(FIRST_ROWS, rest)),
-        lambda: jnp.zeros((chips, rest, up_weight.shape[1]), adapter_up.dtype),
-    )
+
+    def later(count):
+        def run():
+            value = jnp.zeros((chips, rest - count, up_weight.shape[1]), adapter_up.dtype)
+            if count:
+                late = exchange(payload(FIRST_ROWS, count))
+                value = jnp.concatenate([late, value], axis=1)
+            return value
+
+        return run
+
+    sizes = (0,) + tuple(size for size in MORE_ROWS if size < rest) + (rest,)
+    which = sum((fullest[0] > FIRST_ROWS + size).astype(jnp.int32) for size in sizes[:-1])
+    extra = lax.switch(which, [later(size) for size in sizes])
     return combine(base, code, begin, fullest, every, incoming, extra)
 
 

time: 121 us -> 125 us (1.033)
  local copies, waits for them, and re-layouts: 8.53 us -> 23.7 us
  waiting for transfers between devices: 55.4 us -> 44.2 us
    unnamed x40 -> x70, local copies, waits for them, and re-layouts: 5.48 us -> 20.6 us
    all_to_all x1, waiting for transfers between devices: 33.3 us -> 25.5 us  [exchange(): lax.all_to_all(value, 'tensor', split_axis=0, concat_axis=0, axis_index_g...]
    ppermute x4, waiting for transfers between devices: 6.24 us -> 1.2 us  [ring_gather(): held[-step] = lax.ppermute(held[1 - step], 'tensor', ahead)]
    ppermute x3 -> x4, waiting for transfers between devices: 4.56 us -> 7.38 us  [the longest x3 4.64 us: pooled(): others = [lax.ppermute(every, 'tensor', hop) for hop in shifts]]
    ppermute x3, waiting for transfers between devices: 7.85 us -> 6 us  [ring_gather(): held[step] = lax.ppermute(held[step - 1], 'tensor', back)]
    ppermute x3 -> x4, starting transfers between devices: 5.39 us -> 5.8 us  [the longest x3 4.62 us: pooled(): others = [lax.ppermute(every, 'tensor', hop) for hop in shifts]]
  transfers between devices with their start and end apart: 17 -> 18, of which waited for: 11 -> 11; matrix products, arithmetic and copies ran while one was open for 15% -> 14% of each run, Pallas kernels for 7% -> 6%
where the time goes in v3:
time: 125 us; the launch traced here: 124 us
  waiting for transfers between devices  44.2 us (35%)
  local copies, waits for them, and re-layouts  23.7 us (19%)
  starting transfers between devices  21.8 us (17%)
  Pallas kernels  16.9 us (14%)
  matrix products  14.3 us (11%)
  other arithmetic  1.93 us (2%)
  between operations  1.49 us (1%)
    all_to_all x1, waiting for transfers between devices, exchange(): lax.all_to_all(value, 'tensor', split_axis=0, concat_axis=0, axis_index_g...  25.5 us
    unnamed x70, local copies, waits for them, and re-layouts  20.6 us
    dot_general x1, matrix products, pooled(): jnp.dot(jnp.concatenate(halves, axis=1), up_weight, preferred_element_typ...  14.3 us
    ppermute x4, starting transfers between devices, ring_gather(): held[-step] = lax.ppermute(held[1 - step], 'tensor', ahead)  8.06 us
    ppermute x3, waiting for transfers between devices, ring_gather(): held[step] = lax.ppermute(held[step - 1], 'tensor', back)  6 us
    pallas_call x1, Pallas kernels, collect_rows(): pl.pallas_call(kernel, in_specs=[smem, smem, whole] + [pl.BlockSpec(memor...  4.83 us
    ppermute x3, waiting for transfers between devices, pooled(): others = [lax.ppermute(every, 'tensor', hop) for hop in shifts]  4.64 us
    pallas_call x1, Pallas kernels, combine(): pl.pallas_call(kernel, in_specs=[smem] * 2 + [pl.BlockSpec(memory_space=p...  4.62 us
  transfers between devices with their start and end apart: 18, of which 11 were waited for; matrix products, arithmetic and copies ran while one was open for 14% of the time, Pallas kernels for 6%

profile of v3, /device:TPU:0, one launch (start us, length us, event | category | flops | bytes accessed | tf_op | source)
XLA Modules:
  0.0 124.3 jit_solution(14404807394342805020)
XLA Ops:
  0.0 1.0 constant_dynamic-slice_fusion.1
  1.5 1.0 collective-permute-done
  2.5 3.0 %collective-permute-start.1 = (bf16[32,4096]{1,0:T(8,128)(2,1)S(1)}, bf16[32,4096]{1,0:T(8,128)(2,1)S(1)}, u32[]{:S(2)}, u32[]{:S(2)}) collective-permute-start(bf16[32,4096]{1,0:T(8,128)(2,1)S(1)} %pad_maximum_fusion.refs_0_), channel_id=1, source_target_pairs={{0,4},{1,5},{4,8},{5,9},{8,12},{9,13},{12,14},{13,15},{14,10},{15,... | collective-permute-start | bytes 786440 | tf_op jit(solution)/shard_map/ppermute | solution.py:410
  8.1 2.1 %shard_map.91 = (f32[128,128]{1,0:T(8,128)S(1)}, f32[128,128]{1,0:T(8,128)S(1)}, bf16[128,256]{1,0:T(8,128)(2,1)}, f32[128,128]{1,0:T(8,128)}, bf16[128,128]{1,0...) custom-call(s32[16]{0:T(128)S(1)} %copy-done.21, s32[16]{0:T(128)S(1)} %copy-done.22, ...), custom_call_target="tpu_custom_call" | custom-call | flops 6553600 | bytes 524288 | tf_op jit(solution)/shard_map/pallas_call | solution.py:158
  10.9 1.2 collective-permute-done.1.refs_1_
  12.1 1.8 %collective-permute-start.3 = (bf16[32,4096]{1,0:T(8,128)(2,1)S(1)}, bf16[32,4096]{1,0:T(8,128)(2,1)S(1)}, u32[]{:S(2)}, u32[]{:S(2)}) collective-permute-start(bf16[32,4096]{1,0:T(8,128)(2,1)S(1)} %collective-permute-done.1.refs_1_), channel_id=1, source_target_pairs={{0,4},{1,5},{4,8},{5,9},{8,12},{9,13},{12,14},{13,15},{14,10},{15,... | collective-permute-start | bytes 786440 | tf_op jit(solution)/shard_map/ppermute | solution.py:410
  13.9 1.2 copy-done
  15.1 2.0 %copy-done.2 = bf16[1,64,28672]{2,1,0:T(8,128)(2,1)S(1)} copy-done((bf16[1,64,28672]{2,1,0:T(8,128)(2,1)S(1)}, bf16[1,64,28672]{2,1,0:T(8,128)(2,1)}, u32[]{:S(2)}) %copy-start.2) | copy-done | bytes 3670040
  17.1 2.1 %shard_map.92 = (bf16[8,64,1792]{2,1,0:T(8,128)(2,1)}, bf16[8,64,1792]{2,1,0:T(8,128)(2,1)S(1)}, bf16[64,4096]{1,0:T(8,128)(2,1)S(1)}) custom-call(s32[1]{0:T(128)} %bitcast.2.core_ref, bf16[64,28672]{1,0:T(8,128)(2,1)S(1)} %bitcast.10, bf16[64,8192]{1,0:T(8,128)(2,1)S(1)} %bitcast.8), custom_call_target="tpu_custom_call" | custom-call | bytes 7340032 | tf_op jit(solution)/shard_map/pallas_call | solution.py:62
  19.2 1.2 %copy-done.19 = bf16[8,64,1792]{2,1,0:T(8,128)(2,1)} copy-done((bf16[8,64,1792]{2,1,0:T(8,128)(2,1)}, bf16[8,64,1792]{2,1,0:T(8,128)(2,1)S(1)}, u32[]{:S(2)}) %copy-start.19) | copy-done | bytes 1835032
  21.5 1.8 %collective-permute-start.5 = (bf16[32,4096]{1,0:T(8,128)(2,1)S(1)}, bf16[32,4096]{1,0:T(8,128)(2,1)S(1)}, u32[]{:S(2)}, u32[]{:S(2)}) collective-permute-start(bf16[32,4096]{1,0:T(8,128)(2,1)S(1)} %collective-permute-done.3.refs_3_), channel_id=1, source_target_pairs={{0,4},{1,5},{4,8},{5,9},{8,12},{9,13},{12,14},{13,15},{14,10},{15,... | collective-permute-start | bytes 786440 | tf_op jit(solution)/shard_map/ppermute | solution.py:410
  24.0 3.8 %collective-permute-done.4.refs_4_ = bf16[32,4096]{1,0:T(8,128)(2,1)S(1)} collective-permute-done((bf16[32,4096]{1,0:T(8,128)(2,1)S(1)}, bf16[32,4096]{1,0:T(8,128)(2,1)S(1)}, u32[]{:S(2)}, u32[]{:S(2)}) %collective-permute-start.4) | collective-permute-done | bytes 262176 | tf_op jit(solution)/shard_map/ppermute | solution.py:412
  29.0 1.5 %collective-permute-start.7 = (bf16[32,4096]{1,0:T(8,128)(2,1)S(1)}, bf16[32,4096]{1,0:T(8,128)(2,1)S(1)}, u32[]{:S(2)}, u32[]{:S(2)}) collective-permute-start(bf16[32,4096]{1,0:T(8,128)(2,1)S(1)} %collective-permute-done.5.refs_5_), channel_id=1, source_target_pairs={{0,4},{1,5},{4,8},{5,9},{8,12},{9,13},{12,14},{13,15},{14,10},{15,... | collective-permute-start | bytes 786440 | tf_op jit(solution)/shard_map/ppermute | solution.py:410
  31.9 2.2 %collective-permute-done.6.refs_6_ = bf16[32,4096]{1,0:T(8,128)(2,1)S(1)} collective-permute-done((bf16[32,4096]{1,0:T(8,128)(2,1)S(1)}, bf16[32,4096]{1,0:T(8,128)(2,1)S(1)}, u32[]{:S(2)}, u32[]{:S(2)}) %collective-permute-start.6) | collective-permute-done | bytes 262176 | tf_op jit(solution)/shard_map/ppermute | solution.py:412
  36.4 1.0 copy-done.4
  37.4 0.9 copy-done.6
  44.1 4.8 %shard_map.93 = (bf16[256,4096]{1,0:T(8,128)(2,1)S(1)}, f32[128,128]{1,0:T(8,128)S(1)}) custom-call(s32[16]{0:T(128)S(1)} %fusion.4.places_ref, s32[1]{0:T(128)} %bitcast.2.core_ref, f32[128,128]{1,0:T(8,128)S(1)} %get-tuple-element.108.own_ref, bf16[32,4096]{1,0:T(8,128)(2,1)S(1)} %pad_maximum_fusion.refs_0_, bf16[32,4096]{1,0:T(8,128)(2,1)S(1)} %copy-done.6, ...), custom_call_target="tpu_custom_call" | custom-call | flops 268435456 | bytes 4194304 | tf_op jit(solution)/shard_map/pallas_call | solution.py:242
  49.0 1.6 %collective-permute-start.10 = (s32[1]{0:T(128)}, s32[1]{0:T(128)}, u32[]{:S(2)}, u32[]{:S(2)}) collective-permute-start(s32[1]{0:T(128)} %get-tuple-element.129), channel_id=1, source_target_pairs={{0,16},{16,0},{1,17},{17,1},{2,18},{18,2},{3,19},{19,3},{4,20},{20... | collective-permute-start | bytes 20 | tf_op jit(solution)/shard_map/ppermute | solution.py:426
  50.5 2.4 %collective-permute-done.10 = s32[1]{0:T(128)} collective-permute-done((s32[1]{0:T(128)}, s32[1]{0:T(128)}, u32[]{:S(2)}, u32[]{:S(2)}) %collective-permute-start.10) | collective-permute-done | bytes 36 | tf_op jit(solution)/shard_map/ppermute | solution.py:426
  54.8 1.2 collective-permute-start.11
  56.0 2.7 %collective-permute-done.11 = bf16[128,128]{1,0:T(8,128)(2,1)S(1)} collective-permute-done((bf16[128,128]{1,0:T(8,128)(2,1)S(1)}, bf16[128,128]{1,0:T(8,128)(2,1)S(1)}, u32[]{:S(2)}, u32[]{:S(2)}) %collective-permute-start.11) | collective-permute-done | bytes 32800 | tf_op jit(solution)/shard_map/ppermute | solution.py:500
  59.6 3.3 %shard_map.94 = bf16[8,64,1792]{2,1,0:T(8,128)(2,1)} custom-call(bf16[128,256]{1,0:T(8,128)(2,1)S(1)} %copy-done.29, f32[128,128]{1,0:T(8,128)S(1)} %copy-done.31, bf16[128,128]{1,0:T(8,128)(2,1)S(1)} %copy-done.33, bf16[128,128]{1,0:T(8,128)(2,1)S(1)} %multiply_convert_fusion.coeff_ref, bf16[8,64,1792]{2,1,0:T(8,128)(2,1)S(1)} %copy-done.27, ...), custom_call_target="tpu_custom_call" | custom-call | flops 234881024 | bytes 5505024 | tf_op jit(solution)/shard_map/pallas_call | solution.py:285
  62.8 3.5 %collective-permute-start.15 = (bf16[128,128]{1,0:T(8,128)(2,1)S(1)}, bf16[128,128]{1,0:T(8,128)(2,1)S(1)}, u32[]{:S(2)}, u32[]{:S(2)}) collective-permute-start(bf16[128,128]{1,0:T(8,128)(2,1)S(1)} %add.43), channel_id=1, source_target_pairs={{0,12},{1,13},{2,14},{3,15},{4,0},{5,1},{6,2},{7,3},{8,4},{9,5},{1... | collective-permute-start | bytes 98312 | tf_op jit(solution)/shard_map/ppermute | solution.py:503
  66.4 1.1 collective-permute-start.13
  68.0 3.3 %collective-permute-done.14 = bf16[128,128]{1,0:T(8,128)(2,1)S(1)} collective-permute-done((bf16[128,128]{1,0:T(8,128)(2,1)S(1)}, bf16[128,128]{1,0:T(8,128)(2,1)S(1)}, u32[]{:S(2)}, u32[]{:S(2)}) %collective-permute-start.14) | collective-permute-done | bytes 32800 | tf_op jit(solution)/shard_map/ppermute | solution.py:503
  72.1 4.3 %all-to-all-start.3 = ((bf16[8,64,1792]{2,1,0:T(8,128)(2,1)}), bf16[8,64,1792]{2,1,0:T(8,128)(2,1)}, u32[]{:S(2)}, u32[]{:S(2)}) async-start(bf16[8,64,1792]{2,1,0:T(8,128)(2,1)} %shard_map.94), calls=%async_computation.3 | async-start | bytes 3670016 | tf_op jit(solution)/shard_map/all_to_all | solution.py:489
  76.5 1.9 %broadcast_select_fusion.1 = (bf16[256,4096]{1,0:T(8,128)(2,1)S(1)}, bf16[256,4096]{1,0:T(8,128)(2,1)S(1)}) fusion(bf16[256,4096]{1,0:T(8,128)(2,1)S(1)} %get-tuple-element.140, bf16[256,4096]{1,0:T(8,128)(2,1)} %collective-permute-done.16, pred[]{:T(512)S(6)} %eq.6, pred[]{:T(512)S(6)} %eq.7), kind=kLoop, calls=%fused_computation.5 | loop fusion | flops 2097152 | bytes 8388610 | tf_op jit(solution)/shard_map/jit(_where)/select_n | solution.py:508
  78.4 14.3 %fusion.base_ref = f32[256,1792]{1,0:T(8,128)S(1)} fusion(bf16[8192,1792]{1,0:T(8,128)(2,1)} %param.14, bf16[256,4096]{1,0:T(8,128)(2,1)S(1)} %get-tuple-element.149, bf16[256,4096]{1,0:T(8,128)(2,1)S(1)} %get-tuple-element.148), kind=kOutput, calls=%fused_computation | convolution fusion | flops 7524581376 | bytes 35389440 | tf_op jit(solution)/shard_map/dot_general | solution.py:509
  92.7 25.5 %all-to-all-done.3.incoming_ref = bf16[8,64,1792]{2,1,0:T(8,128)(2,1)} async-done(((bf16[8,64,1792]{2,1,0:T(8,128)(2,1)}), bf16[8,64,1792]{2,1,0:T(8,128)(2,1)}, u32[]{:S(2)}, u32[]{:S(2)}) %all-to-all-start.3) | async-done | bytes 1835040 | tf_op jit(solution)/shard_map/all_to_all | solution.py:489
  118.3 1.4 %conditional.1 = (bf16[8,64,1792]{2,1,0:T(8,128)(2,1)}) conditional(s32[]{:T(128)} %bitcast.5, () %tuple.31, (bf16[128,256]{1,0:T(8,128)(2,1)S(1)}, f32[128,128]{1,0:T(8,128)S(1)}, bf16[128,128]{1,0:T(8,128)(2,1)S(1)}, bf16[128,128]{1,0:T(8,128)(2,1)S(1)}, bf16[8,64,1792]{2,1,0:T(8,128)(2,1)}, ...), branch_computations={%region_0.1_spmd, %region_1.2_spmd, %region_2.3_spmd, %region_3.4_... | conditional | flops 234881024 | bytes 9175050 | solution.py:527
  118.3 1.4 %broadcast.2 = bf16[8,64,1792]{2,1,0:T(8,128)(2,1)} broadcast(bf16[]{:T(256)} %constant.12.clone), dimensions={} | broadcast | bytes 1835010 | tf_op jit(solution)/shard_map/broadcast.1
  119.7 4.6 %shard_map.95 = bf16[256,1792]{1,0:T(8,128)(2,1)} custom-call(s32[16]{0:T(128)S(1)} %get-tuple-element.106.begin_ref, s32[1]{0:T(128)S(6)} %max.3.more_ref, f32[256,1792]{1,0:T(8,128)S(1)} %fusion.base_ref, s32[256,128]{1,0:T(8,128)S(1)} %copy-done.26, bf16[128,128]{1,0:T(8,128)(2,1)S(1)} %add_add_fusion.coeff_ref, ...), custom_call_target="tpu_custom_call" | custom-call | flops 1879048192 | bytes 6422528 | tf_op jit(solution)/shard_map/pallas_call | solution.py:377
  (89 shorter events, 19.0 us)
Async XLA Ops:
  1.0 1.5 %collective-permute-start = (bf16[16,4096]{1,0:T(8,128)(2,1)S(1)}, bf16[16,4096]{1,0:T(8,128)(2,1)S(1)}, u32[]{:S(2)}, u32[]{:S(2)}) collective-permute-start(bf16[16,4096]{1,0:T(8,128)(2,1)S(1)} %get-tuple-element.151), channel_id=1, source_target_pairs={{0,1},{1,0},{2,3},{3,2},{4,5},{5,4},{6,7},{7,6},{8,9},{9,8},{10,11... | collective-permute-start | bytes 393224 | tf_op jit(solution)/shard_map/ppermute | solution.py:456
  2.5 9.5 %collective-permute-start.1 = (bf16[32,4096]{1,0:T(8,128)(2,1)S(1)}, bf16[32,4096]{1,0:T(8,128)(2,1)S(1)}, u32[]{:S(2)}, u32[]{:S(2)}) collective-permute-start(bf16[32,4096]{1,0:T(8,128)(2,1)S(1)} %pad_maximum_fusion.refs_0_), channel_id=1, source_target_pairs={{0,4},{1,5},{4,8},{5,9},{8,12},{9,13},{12,14},{13,15},{14,10},{15,... | collective-permute-start | bytes 786440 | tf_op jit(solution)/shard_map/ppermute | solution.py:410
  10.9 9.6 %collective-permute-start.2 = (bf16[32,4096]{1,0:T(8,128)(2,1)S(1)}, bf16[32,4096]{1,0:T(8,128)(2,1)S(1)}, u32[]{:S(2)}, u32[]{:S(2)}) collective-permute-start(bf16[32,4096]{1,0:T(8,128)(2,1)S(1)} %pad_maximum_fusion.refs_0_), channel_id=1, source_target_pairs={{4,0},{5,1},{8,4},{9,5},{12,8},{13,9},{14,12},{15,13},{10,14},{11,... | collective-permute-start | bytes 786440 | tf_op jit(solution)/shard_map/ppermute | solution.py:412
  12.1 7.2 %copy-start.5 = (bf16[32,4096]{1,0:T(8,128)(2,1)}, bf16[32,4096]{1,0:T(8,128)(2,1)S(1)}, u32[]{:S(2)}) copy-start(bf16[32,4096]{1,0:T(8,128)(2,1)S(1)} %collective-permute-done.1.refs_1_) | copy-start | bytes 786436
  12.1 9.4 %collective-permute-start.3 = (bf16[32,4096]{1,0:T(8,128)(2,1)S(1)}, bf16[32,4096]{1,0:T(8,128)(2,1)S(1)}, u32[]{:S(2)}, u32[]{:S(2)}) collective-permute-start(bf16[32,4096]{1,0:T(8,128)(2,1)S(1)} %collective-permute-done.1.refs_1_), channel_id=1, source_target_pairs={{0,4},{1,5},{4,8},{5,9},{8,12},{9,13},{12,14},{13,15},{14,10},{15,... | collective-permute-start | bytes 786440 | tf_op jit(solution)/shard_map/ppermute | solution.py:410
  15.1 2.0 %copy-start.2 = (bf16[1,64,28672]{2,1,0:T(8,128)(2,1)S(1)}, bf16[1,64,28672]{2,1,0:T(8,128)(2,1)}, u32[]{:S(2)}) copy-start(bf16[1,64,28672]{2,1,0:T(8,128)(2,1)} %param.16) | copy-start | bytes 11010052
  17.1 19.2 %copy-start.1 = (bf16[1,64,8192]{2,1,0:T(8,128)(2,1)S(1)}, bf16[1,64,8192]{2,1,0:T(8,128)(2,1)}, u32[]{:S(2)}) copy-start(bf16[1,64,8192]{2,1,0:T(8,128)(2,1)} %param.15) | copy-start | bytes 3145732
  19.2 1.3 %copy-start.19 = (bf16[8,64,1792]{2,1,0:T(8,128)(2,1)}, bf16[8,64,1792]{2,1,0:T(8,128)(2,1)S(1)}, u32[]{:S(2)}) copy-start(bf16[8,64,1792]{2,1,0:T(8,128)(2,1)S(1)} %get-tuple-element.136) | copy-start | bytes 5505028
  20.5 7.3 %collective-permute-start.4 = (bf16[32,4096]{1,0:T(8,128)(2,1)S(1)}, bf16[32,4096]{1,0:T(8,128)(2,1)S(1)}, u32[]{:S(2)}, u32[]{:S(2)}) collective-permute-start(bf16[32,4096]{1,0:T(8,128)(2,1)S(1)} %collective-permute-done.2.refs_2_), channel_id=1, source_target_pairs={{4,0},{5,1},{8,4},{9,5},{12,8},{13,9},{14,12},{15,13},{10,14},{11,... | collective-permute-start | bytes 786440 | tf_op jit(solution)/shard_map/ppermute | solution.py:412
  21.5 7.6 %collective-permute-start.5 = (bf16[32,4096]{1,0:T(8,128)(2,1)S(1)}, bf16[32,4096]{1,0:T(8,128)(2,1)S(1)}, u32[]{:S(2)}, u32[]{:S(2)}) collective-permute-start(bf16[32,4096]{1,0:T(8,128)(2,1)S(1)} %collective-permute-done.3.refs_3_), channel_id=1, source_target_pairs={{0,4},{1,5},{4,8},{5,9},{8,12},{9,13},{12,14},{13,15},{14,10},{15,... | collective-permute-start | bytes 786440 | tf_op jit(solution)/shard_map/ppermute | solution.py:410
  24.0 10.9 %collective-permute-start.8 = (bf16[64,4096]{1,0:T(8,128)(2,1)S(1)}, bf16[64,4096]{1,0:T(8,128)(2,1)S(1)}, u32[]{:S(2)}, u32[]{:S(2)}) collective-permute-start(bf16[64,4096]{1,0:T(8,128)(2,1)S(1)} %get-tuple-element.116), channel_id=1, source_target_pairs={{0,1},{1,0},{2,3},{3,2},{4,5},{5,4},{6,7},{7,6},{8,9},{9,8},{10,11... | collective-permute-start | bytes 1572872 | tf_op jit(solution)/shard_map/ppermute | solution.py:477
  27.8 6.4 %collective-permute-start.6 = (bf16[32,4096]{1,0:T(8,128)(2,1)S(1)}, bf16[32,4096]{1,0:T(8,128)(2,1)S(1)}, u32[]{:S(2)}, u32[]{:S(2)}) collective-permute-start(bf16[32,4096]{1,0:T(8,128)(2,1)S(1)} %collective-permute-done.4.refs_4_), channel_id=1, source_target_pairs={{4,0},{5,1},{8,4},{9,5},{12,8},{13,9},{14,12},{15,13},{10,14},{11,... | collective-permute-start | bytes 786440 | tf_op jit(solution)/shard_map/ppermute | solution.py:412
  29.0 6.6 %collective-permute-start.7 = (bf16[32,4096]{1,0:T(8,128)(2,1)S(1)}, bf16[32,4096]{1,0:T(8,128)(2,1)S(1)}, u32[]{:S(2)}, u32[]{:S(2)}) collective-permute-start(bf16[32,4096]{1,0:T(8,128)(2,1)S(1)} %collective-permute-done.5.refs_5_), channel_id=1, source_target_pairs={{0,4},{1,5},{4,8},{5,9},{8,12},{9,13},{12,14},{13,15},{14,10},{15,... | collective-permute-start | bytes 786440 | tf_op jit(solution)/shard_map/ppermute | solution.py:410
  44.1 10.1 %copy-start.20 = (bf16[8,64,1792]{2,1,0:T(8,128)(2,1)S(1)}, bf16[8,64,1792]{2,1,0:T(8,128)(2,1)}, u32[]{:S(2)}) copy-start(bf16[8,64,1792]{2,1,0:T(8,128)(2,1)} %copy-done.19) | copy-start | bytes 5505028
  44.1 15.5 %copy-start.27 = (bf16[8,64,1792]{2,1,0:T(8,128)(2,1)S(1)}, bf16[8,64,1792]{2,1,0:T(8,128)(2,1)}, u32[]{:S(2)}) copy-start(bf16[8,64,1792]{2,1,0:T(8,128)(2,1)} %get-tuple-element.135.mine_ref) | copy-start | bytes 5505028
  44.1 15.5 %copy-start.29 = (bf16[128,256]{1,0:T(8,128)(2,1)S(1)}, bf16[128,256]{1,0:T(8,128)(2,1)}, u32[]{:S(2)}) copy-start(bf16[128,256]{1,0:T(8,128)(2,1)} %get-tuple-element.132.choose_ref) | copy-start | bytes 196612
  44.1 15.5 %copy-start.31 = (f32[128,128]{1,0:T(8,128)S(1)}, f32[128,128]{1,0:T(8,128)}, u32[]{:S(2)}) copy-start(f32[128,128]{1,0:T(8,128)} %get-tuple-element.133.live_ref) | copy-start | bytes 196612
  44.1 15.5 %copy-start.33 = (bf16[128,128]{1,0:T(8,128)(2,1)S(1)}, bf16[128,128]{1,0:T(8,128)(2,1)}, u32[]{:S(2)}) copy-start(bf16[128,128]{1,0:T(8,128)(2,1)} %get-tuple-element.134.fixed_ref) | copy-start | bytes 98308
  48.9 5.3 %collective-permute-start.9 = (f32[128,128]{1,0:T(8,128)S(1)}, f32[128,128]{1,0:T(8,128)S(1)}, u32[]{:S(2)}, u32[]{:S(2)}) collective-permute-start(f32[128,128]{1,0:T(8,128)S(1)} %get-tuple-element.126), channel_id=1, source_target_pairs={{0,1},{1,0},{2,3},{3,2},{4,5},{5,4},{6,7},{7,6},{8,9},{9,8},{10,11... | collective-permute-start | bytes 196616 | tf_op jit(solution)/shard_map/ppermute | solution.py:481
  49.0 3.9 %collective-permute-start.10 = (s32[1]{0:T(128)}, s32[1]{0:T(128)}, u32[]{:S(2)}, u32[]{:S(2)}) collective-permute-start(s32[1]{0:T(128)} %get-tuple-element.129), channel_id=1, source_target_pairs={{0,16},{16,0},{1,17},{17,1},{2,18},{18,2},{3,19},{19,3},{4,20},{20... | collective-permute-start | bytes 20 | tf_op jit(solution)/shard_map/ppermute | solution.py:426
  54.2 5.4 %collective-permute-start.12 = (bf16[8,64,1792]{2,1,0:T(8,128)(2,1)S(1)}, bf16[8,64,1792]{2,1,0:T(8,128)(2,1)S(1)}, u32[]{:S(2)}, u32[]{:S(2)}) collective-permute-start(bf16[8,64,1792]{2,1,0:T(8,128)(2,1)S(1)} %copy-done.20), channel_id=1, source_target_pairs={{0,1},{1,0},{2,3},{3,2},{4,5},{5,4},{6,7},{7,6},{8,9},{9,8},{10,11... | collective-permute-start | bytes 5505032 | tf_op jit(solution)/shard_map/ppermute | solution.py:479
  54.3 17.8 %collective-permute-start.16 = (bf16[256,4096]{1,0:T(8,128)(2,1)S(1)}, bf16[256,4096]{1,0:T(8,128)(2,1)}, u32[]{:S(2)}, u32[]{:S(2)}) collective-permute-start(bf16[256,4096]{1,0:T(8,128)(2,1)S(1)} %get-tuple-element.140), channel_id=1, source_target_pairs={{0,1},{1,0},{2,3},{3,2},{4,5},{5,4},{6,7},{7,6},{8,9},{9,8},{10,11... | collective-permute-start | bytes 6291464 | tf_op jit(solution)/shard_map/ppermute | solution.py:499
  54.8 3.9 %collective-permute-start.11 = (bf16[128,128]{1,0:T(8,128)(2,1)S(1)}, bf16[128,128]{1,0:T(8,128)(2,1)S(1)}, u32[]{:S(2)}, u32[]{:S(2)}) collective-permute-start(bf16[128,128]{1,0:T(8,128)(2,1)S(1)} %multiply_convert_fusion.coeff_ref), channel_id=1, source_target_pairs={{0,2},{1,3},{2,0},{3,1},{4,6},{5,7},{6,4},{7,5},{8,10},{9,11},{10,... | collective-permute-start | bytes 98312 | tf_op jit(solution)/shard_map/ppermute | solution.py:500
  59.5 3.3 %copy-start.28 = (bf16[8,64,1792]{2,1,0:T(8,128)(2,1)}, bf16[8,64,1792]{2,1,0:T(8,128)(2,1)S(1)}, u32[]{:S(2)}) copy-start(bf16[8,64,1792]{2,1,0:T(8,128)(2,1)S(1)} %collective-permute-done.12.other_ref) | copy-start | bytes 5505028
  62.8 5.2 %collective-permute-start.15 = (bf16[128,128]{1,0:T(8,128)(2,1)S(1)}, bf16[128,128]{1,0:T(8,128)(2,1)S(1)}, u32[]{:S(2)}, u32[]{:S(2)}) collective-permute-start(bf16[128,128]{1,0:T(8,128)(2,1)S(1)} %add.43), channel_id=1, source_target_pairs={{0,12},{1,13},{2,14},{3,15},{4,0},{5,1},{6,2},{7,3},{8,4},{9,5},{1... | collective-permute-start | bytes 98312 | tf_op jit(solution)/shard_map/ppermute | solution.py:503
  66.4 5.0 %collective-permute-start.14 = (bf16[128,128]{1,0:T(8,128)(2,1)S(1)}, bf16[128,128]{1,0:T(8,128)(2,1)S(1)}, u32[]{:S(2)}, u32[]{:S(2)}) collective-permute-start(bf16[128,128]{1,0:T(8,128)(2,1)S(1)} %add.43), channel_id=1, source_target_pairs={{0,8},{1,9},{2,10},{3,11},{4,12},{5,13},{6,14},{7,15},{8,0},{9,1},... | collective-permute-start | bytes 98312 | tf_op jit(solution)/shard_map/ppermute | solution.py:503
  66.4 5.7 %collective-permute-start.13 = (bf16[128,128]{1,0:T(8,128)(2,1)S(1)}, bf16[128,128]{1,0:T(8,128)(2,1)S(1)}, u32[]{:S(2)}, u32[]{:S(2)}) collective-permute-start(bf16[128,128]{1,0:T(8,128)(2,1)S(1)} %add.43), channel_id=1, source_target_pairs={{0,4},{1,5},{2,6},{3,7},{4,8},{5,9},{6,10},{7,11},{8,12},{9,13},{1... | collective-permute-start | bytes 98312 | tf_op jit(solution)/shard_map/ppermute | solution.py:503
  72.1 46.1 %all-to-all-start.3 = ((bf16[8,64,1792]{2,1,0:T(8,128)(2,1)}), bf16[8,64,1792]{2,1,0:T(8,128)(2,1)}, u32[]{:S(2)}, u32[]{:S(2)}) async-start(bf16[8,64,1792]{2,1,0:T(8,128)(2,1)} %shard_map.94), calls=%async_computation.3 | async-start | bytes 3670016 | tf_op jit(solution)/shard_map/all_to_all | solution.py:489
  78.4 39.9 %copy-start.30 = (bf16[128,256]{1,0:T(8,128)(2,1)S(1)}, bf16[128,256]{1,0:T(8,128)(2,1)}, u32[]{:S(2)}) copy-start(bf16[128,256]{1,0:T(8,128)(2,1)} %get-tuple-element.132.choose_ref) | copy-start | bytes 196612
  78.4 39.9 %copy-start.32 = (f32[128,128]{1,0:T(8,128)S(1)}, f32[128,128]{1,0:T(8,128)}, u32[]{:S(2)}) copy-start(f32[128,128]{1,0:T(8,128)} %get-tuple-element.133.live_ref) | copy-start | bytes 196612
  78.4 39.9 %copy-start.34 = (bf16[128,128]{1,0:T(8,128)(2,1)S(1)}, bf16[128,128]{1,0:T(8,128)(2,1)}, u32[]{:S(2)}) copy-start(bf16[128,128]{1,0:T(8,128)(2,1)} %get-tuple-element.134.fixed_ref) | copy-start | bytes 98308
  118.3 1.4 %copy-start.26 = (s32[256,128]{1,0:T(8,128)S(1)}, s32[256,128]{1,0:T(8,128)}, u32[]{:S(2)}) copy-start(s32[256,128]{1,0:T(8,128)} %copy-done.25) | copy-start | bytes 393220
  (21 other events, 17.3 us)

commit v4 on v3

--- a/solution.py
+++ b/solution.py
@@ -467,16 +467,21 @@
         nonlocal packed, own
         if step == 1:
             piece, own, which = lax.optimization_barrier((piece, own, core[None]))
-            packed = split_for_pair(adapter_up[0], adapter_down[0], which, chips)
+            mine, other, down_half = split_for_pair(
+                adapter_up[0], adapter_down[0], which, chips
+            )
+            packed = (mine, other, down_half)
         if step == 2:
             piece, packed = lax.optimization_barrier((piece, packed))
+            mine, other, down_half = packed
+            other = lax.ppermute(other, "tensor", sibling)
+            packed = (mine, other, lax.ppermute(down_half, "tensor", sibling))
+        if step == 3:
+            piece, packed = lax.optimization_barrier((piece, packed))
         return piece
 
     blocks, places = ring_gather(block, shards, halfway)
     mine, other, down_half = packed
-    down_half = lax.ppermute(down_half, "tensor", sibling)
-    blocks, other, down_half = lax.optimization_barrier((blocks, other, down_half))
-    other = lax.ppermute(other, "tensor", sibling)
     rows, shrink = collect_rows(blocks, places, core[None], adapter_down[0], down_half, own)
     shrink = shrink + lax.ppermute(shrink, "tensor", sibling)
     coeff = (shrink * gain).astype(jnp.bfloat16)
@@ -497,12 +502,12 @@
 
     near = payload(0, FIRST_ROWS)
     rows_other = lax.ppermute(rows, "tensor", sibling)
-    every = coeff + lax.ppermute(coeff, "tensor", [(t, t ^ 2) for t in range(shards)])
-    every, near = lax.optimization_barrier((every, near))
-    shifts = [[(t, (t + 4 * k) % shards) for t in range(shards)] for k in range(1, shards // 4)]
-    others = [lax.ppermute(every, "tensor", hop) for hop in shifts]
-    for value in others:
-        every = every + value
+    every, bit = coeff, 2
+    while bit < shards:
+        every = every + lax.ppermute(every, "tensor", [(t, t ^ bit) for t in range(shards)])
+        if bit == 2:
+            every, near = lax.optimization_barrier((every, near))
+        bit *= 2
     near, every, rows, rows_other = lax.optimization_barrier((near, every, rows, rows_other))
     incoming = exchange(near)
     halves = [jnp.where(core == c, rows, rows_other) for c in range(2)]

time: 125 us -> 132 us (1.056)
  waiting for transfers between devices: 44.2 us -> 50 us
  Pallas kernels: 16.9 us -> 18.4 us
  local copies, waits for them, and re-layouts: 23.7 us -> 22.3 us
    ppermute x3, waiting for transfers between devices: 6 us -> 13.7 us  [ring_gather(): held[step] = lax.ppermute(held[step - 1], 'tensor', back)]
    ppermute x6 -> x5, waiting for transfers between devices: 8.14 us -> 4.57 us  [the longest x3 4.56 us: pooled(): lax.ppermute(every, 'tensor', [(t, t ^ bit) for t in range(shards)])]
    ppermute x3, starting transfers between devices: 0.78 us -> 4.27 us  [ring_gather(): held[step] = lax.ppermute(held[step - 1], 'tensor', back)]
    ppermute x4, waiting for transfers between devices: 1.2 us -> 3.82 us  [ring_gather(): held[-step] = lax.ppermute(held[1 - step], 'tensor', ahead)]
    ppermute x4, starting transfers between devices: 8.06 us -> 5.99 us  [ring_gather(): held[-step] = lax.ppermute(held[1 - step], 'tensor', ahead)]
    pallas_call x1, Pallas kernels: 3.28 us -> 4.85 us  [build_payload(): pl.pallas_call(kernel, in_specs=[pl.BlockSpec(memory_space=pltpu.VMEM)] *...]
    unnamed x70 -> x58, local copies, waits for them, and re-layouts: 20.6 us -> 19.2 us
    ppermute x6 -> x5, starting transfers between devices: 5.87 us -> 6.17 us  [the longest x3 5.94 us: pooled(): lax.ppermute(every, 'tensor', [(t, t ^ bit) for t in range(shards)])]
  transfers between devices with their start and end apart: 18 -> 17, of which waited for: 11 -> 11; matrix products, arithmetic and copies ran while one was open for 14% -> 13% of each run, Pallas kernels for 6% -> 7%
where the time goes in v4:
time: 132 us
  waiting for transfers between devices  50 us (38%)
  starting transfers between devices  23 us (17%)
  local copies, waits for them, and re-layouts  22.3 us (17%)
  Pallas kernels  18.4 us (14%)
  matrix products  14.5 us (11%)
  other arithmetic  1.94 us (1%)
  between operations  1.45 us (1%)
    all_to_all x1, waiting for transfers between devices, exchange(): lax.all_to_all(value, 'tensor', split_axis=0, concat_axis=0, axis_index_g...  24.7 us
    unnamed x58, local copies, waits for them, and re-layouts  19.2 us
    dot_general x1, matrix products, pooled(): jnp.dot(jnp.concatenate(halves, axis=1), up_weight, preferred_element_typ...  14.5 us
    ppermute x3, waiting for transfers between devices, ring_gather(): held[step] = lax.ppermute(held[step - 1], 'tensor', back)  13.7 us
    ppermute x4, starting transfers between devices, ring_gather(): held[-step] = lax.ppermute(held[1 - step], 'tensor', ahead)  5.99 us
    ppermute x3, starting transfers between devices, pooled(): lax.ppermute(every, 'tensor', [(t, t ^ bit) for t in range(shards)])  5.94 us
    pallas_call x1, Pallas kernels, build_payload(): pl.pallas_call(kernel, in_specs=[pl.BlockSpec(memory_space=pltpu.VMEM)] *...  4.85 us
    pallas_call x1, Pallas kernels, collect_rows(): pl.pallas_call(kernel, in_specs=[smem, smem, whole] + [pl.BlockSpec(memor...  4.81 us
  transfers between devices with their start and end apart: 17, of which 11 were waited for; matrix products, arithmetic and copies ran while one was open for 13% of the time, Pallas kernels for 7%

profile of v4, /device:TPU:0, one launch (start us, length us, event | category | flops | bytes accessed | tf_op | source)
XLA Modules:
  0.0 131.6 jit_solution(481666382965151782)
XLA Ops:
  1.5 1.0 collective-permute-done
  2.5 3.0 %collective-permute-start.1 = (bf16[32,4096]{1,0:T(8,128)(2,1)S(1)}, bf16[32,4096]{1,0:T(8,128)(2,1)S(1)}, u32[]{:S(2)}, u32[]{:S(2)}) collective-permute-start(bf16[32,4096]{1,0:T(8,128)(2,1)S(1)} %pad_maximum_fusion.refs_0_), channel_id=1, source_target_pairs={{0,4},{1,5},{4,8},{5,9},{8,12},{9,13},{12,14},{13,15},{14,10},{15,... | collective-permute-start | bytes 786440 | tf_op jit(solution)/shard_map/ppermute | solution.py:410
  8.1 2.1 %shard_map.91 = (f32[128,128]{1,0:T(8,128)S(1)}, f32[128,128]{1,0:T(8,128)S(1)}, bf16[128,256]{1,0:T(8,128)(2,1)}, f32[128,128]{1,0:T(8,128)}, bf16[128,128]{1,0...) custom-call(s32[16]{0:T(128)S(1)} %copy-done.19, s32[16]{0:T(128)S(1)} %copy-done.20, ...), custom_call_target="tpu_custom_call" | custom-call | flops 6553600 | bytes 524288 | tf_op jit(solution)/shard_map/pallas_call | solution.py:158
  10.9 1.2 collective-permute-done.1.refs_1_
  12.1 1.8 %collective-permute-start.3 = (bf16[32,4096]{1,0:T(8,128)(2,1)S(1)}, bf16[32,4096]{1,0:T(8,128)(2,1)S(1)}, u32[]{:S(2)}, u32[]{:S(2)}) collective-permute-start(bf16[32,4096]{1,0:T(8,128)(2,1)S(1)} %collective-permute-done.1.refs_1_), channel_id=1, source_target_pairs={{0,4},{1,5},{4,8},{5,9},{8,12},{9,13},{12,14},{13,15},{14,10},{15,... | collective-permute-start | bytes 786440 | tf_op jit(solution)/shard_map/ppermute | solution.py:410
  13.9 1.2 copy-done
  15.1 2.0 %copy-done.2 = bf16[1,64,28672]{2,1,0:T(8,128)(2,1)S(1)} copy-done((bf16[1,64,28672]{2,1,0:T(8,128)(2,1)S(1)}, bf16[1,64,28672]{2,1,0:T(8,128)(2,1)}, u32[]{:S(2)}) %copy-start.2) | copy-done | bytes 3670040
  17.1 2.1 %shard_map.92 = (bf16[8,64,1792]{2,1,0:T(8,128)(2,1)}, bf16[8,64,1792]{2,1,0:T(8,128)(2,1)S(1)}, bf16[64,4096]{1,0:T(8,128)(2,1)S(1)}) custom-call(s32[1]{0:T(128)} %bitcast.2.core_ref, bf16[64,28672]{1,0:T(8,128)(2,1)S(1)} %bitcast.10, bf16[64,8192]{1,0:T(8,128)(2,1)S(1)} %bitcast.8), custom_call_target="tpu_custom_call" | custom-call | bytes 7340032 | tf_op jit(solution)/shard_map/pallas_call | solution.py:62
  19.9 1.4 %collective-permute-start.2 = (bf16[32,4096]{1,0:T(8,128)(2,1)S(1)}, bf16[32,4096]{1,0:T(8,128)(2,1)S(1)}, u32[]{:S(2)}, u32[]{:S(2)}) collective-permute-start(bf16[32,4096]{1,0:T(8,128)(2,1)S(1)} %pad_maximum_fusion.refs_0_), channel_id=1, source_target_pairs={{4,0},{5,1},{8,4},{9,5},{12,8},{13,9},{14,12},{15,13},{10,14},{11,... | collective-permute-start | bytes 786440 | tf_op jit(solution)/shard_map/ppermute | solution.py:412
  21.6 7.1 %collective-permute-done.2.refs_2_ = bf16[32,4096]{1,0:T(8,128)(2,1)S(1)} collective-permute-done((bf16[32,4096]{1,0:T(8,128)(2,1)S(1)}, bf16[32,4096]{1,0:T(8,128)(2,1)S(1)}, u32[]{:S(2)}, u32[]{:S(2)}) %collective-permute-start.2) | collective-permute-done | bytes 262176 | tf_op jit(solution)/shard_map/ppermute | solution.py:412
  28.6 1.4 %collective-permute-start.4 = (bf16[32,4096]{1,0:T(8,128)(2,1)S(1)}, bf16[32,4096]{1,0:T(8,128)(2,1)S(1)}, u32[]{:S(2)}, u32[]{:S(2)}) collective-permute-start(bf16[32,4096]{1,0:T(8,128)(2,1)S(1)} %collective-permute-done.2.refs_2_), channel_id=1, source_target_pairs={{4,0},{5,1},{8,4},{9,5},{12,8},{13,9},{14,12},{15,13},{10,14},{11,... | collective-permute-start | bytes 786440 | tf_op jit(solution)/shard_map/ppermute | solution.py:412
  32.1 4.5 %collective-permute-done.4.refs_4_ = bf16[32,4096]{1,0:T(8,128)(2,1)S(1)} collective-permute-done((bf16[32,4096]{1,0:T(8,128)(2,1)S(1)}, bf16[32,4096]{1,0:T(8,128)(2,1)S(1)}, u32[]{:S(2)}, u32[]{:S(2)}) %collective-permute-start.4) | collective-permute-done | bytes 262176 | tf_op jit(solution)/shard_map/ppermute | solution.py:412
  36.6 1.4 %collective-permute-start.8 = (bf16[32,4096]{1,0:T(8,128)(2,1)S(1)}, bf16[32,4096]{1,0:T(8,128)(2,1)S(1)}, u32[]{:S(2)}, u32[]{:S(2)}) collective-permute-start(bf16[32,4096]{1,0:T(8,128)(2,1)S(1)} %collective-permute-done.4.refs_4_), channel_id=1, source_target_pairs={{4,0},{5,1},{8,4},{9,5},{12,8},{13,9},{14,12},{15,13},{10,14},{11,... | collective-permute-start | bytes 786440 | tf_op jit(solution)/shard_map/ppermute | solution.py:412
  41.5 2.1 %collective-permute-done.8.refs_6_ = bf16[32,4096]{1,0:T(8,128)(2,1)S(1)} collective-permute-done((bf16[32,4096]{1,0:T(8,128)(2,1)S(1)}, bf16[32,4096]{1,0:T(8,128)(2,1)S(1)}, u32[]{:S(2)}, u32[]{:S(2)}) %collective-permute-start.8) | collective-permute-done | bytes 262176 | tf_op jit(solution)/shard_map/ppermute | solution.py:412
  44.3 1.9 %collective-permute-done.9.refs_7_ = bf16[32,4096]{1,0:T(8,128)(2,1)S(1)} collective-permute-done((bf16[32,4096]{1,0:T(8,128)(2,1)S(1)}, bf16[32,4096]{1,0:T(8,128)(2,1)S(1)}, u32[]{:S(2)}, u32[]{:S(2)}) %collective-permute-start.9) | collective-permute-done | bytes 262176 | tf_op jit(solution)/shard_map/ppermute | solution.py:410
  47.0 1.0 copy-done.4
  54.7 4.8 %shard_map.93 = (bf16[256,4096]{1,0:T(8,128)(2,1)S(1)}, f32[128,128]{1,0:T(8,128)S(1)}) custom-call(s32[16]{0:T(128)S(1)} %fusion.4.places_ref, s32[1]{0:T(128)} %bitcast.2.core_ref, f32[128,128]{1,0:T(8,128)S(1)} %get-tuple-element.102.own_ref, bf16[32,4096]{1,0:T(8,128)(2,1)S(1)} %pad_maximum_fusion.refs_0_, bf16[32,4096]{1,0:T(8,128)(2,1)S(1)} %copy-done.6, ...), custom_call_target="tpu_custom_call" | custom-call | flops 268435456 | bytes 4194304 | tf_op jit(solution)/shard_map/pallas_call | solution.py:242
  59.6 1.6 %collective-permute-start.11 = (s32[1]{0:T(128)}, s32[1]{0:T(128)}, u32[]{:S(2)}, u32[]{:S(2)}) collective-permute-start(s32[1]{0:T(128)} %get-tuple-element.117), channel_id=1, source_target_pairs={{0,16},{16,0},{1,17},{17,1},{2,18},{18,2},{3,19},{19,3},{4,20},{20... | collective-permute-start | bytes 20 | tf_op jit(solution)/shard_map/ppermute | solution.py:426
  61.1 2.2 %collective-permute-done.11 = s32[1]{0:T(128)} collective-permute-done((s32[1]{0:T(128)}, s32[1]{0:T(128)}, u32[]{:S(2)}, u32[]{:S(2)}) %collective-permute-start.11) | collective-permute-done | bytes 36 | tf_op jit(solution)/shard_map/ppermute | solution.py:426
  64.7 1.6 %collective-permute-start.12 = (bf16[128,128]{1,0:T(8,128)(2,1)S(1)}, bf16[128,128]{1,0:T(8,128)(2,1)S(1)}, u32[]{:S(2)}, u32[]{:S(2)}) collective-permute-start(bf16[128,128]{1,0:T(8,128)(2,1)S(1)} %multiply_convert_fusion.coeff_ref), channel_id=1, source_target_pairs={{0,2},{1,3},{2,0},{3,1},{4,6},{5,7},{6,4},{7,5},{8,10},{9,11},{10,... | collective-permute-start | bytes 98312 | tf_op jit(solution)/shard_map/ppermute | solution.py:507
  66.3 4.9 %shard_map.94 = bf16[8,64,1792]{2,1,0:T(8,128)(2,1)} custom-call(bf16[128,256]{1,0:T(8,128)(2,1)} %get-tuple-element.120.choose_ref, f32[128,128]{1,0:T(8,128)} %get-tuple-element.121.live_ref, bf16[128,128]{1,0:T(8,128)(2,1)} %get-tuple-element.122.fixed_ref, bf16[128,128]{1,0:T(8,128)(2,1)S(1)} %multiply_convert_fusion.coeff_ref, ...), custom_call_target="tpu_custom_call" | custom-call | flops 234881024 | bytes 5505024 | tf_op jit(solution)/shard_map/pallas_call | solution.py:285
  71.2 1.6 %collective-permute-start.13 = (bf16[128,128]{1,0:T(8,128)(2,1)S(1)}, bf16[128,128]{1,0:T(8,128)(2,1)S(1)}, u32[]{:S(2)}, u32[]{:S(2)}) collective-permute-start(bf16[128,128]{1,0:T(8,128)(2,1)S(1)} %add.40), channel_id=1, source_target_pairs={{0,4},{1,5},{2,6},{3,7},{4,0},{5,1},{6,2},{7,3},{8,12},{9,13},{10,... | collective-permute-start | bytes 98312 | tf_op jit(solution)/shard_map/ppermute | solution.py:507
  72.9 2.3 %collective-permute-done.13 = bf16[128,128]{1,0:T(8,128)(2,1)S(1)} collective-permute-done((bf16[128,128]{1,0:T(8,128)(2,1)S(1)}, bf16[128,128]{1,0:T(8,128)(2,1)S(1)}, u32[]{:S(2)}, u32[]{:S(2)}) %collective-permute-start.13) | collective-permute-done | bytes 32800 | tf_op jit(solution)/shard_map/ppermute | solution.py:507
  75.2 2.7 %collective-permute-start.14 = (bf16[128,128]{1,0:T(8,128)(2,1)S(1)}, bf16[128,128]{1,0:T(8,128)(2,1)S(1)}, u32[]{:S(2)}, u32[]{:S(2)}) collective-permute-start(bf16[128,128]{1,0:T(8,128)(2,1)S(1)} %add.41), channel_id=1, source_target_pairs={{0,8},{1,9},{2,10},{3,11},{4,12},{5,13},{6,14},{7,15},{8,0},{9,1},... | collective-permute-start | bytes 98312 | tf_op jit(solution)/shard_map/ppermute | solution.py:507
  77.9 2.2 %collective-permute-done.14 = bf16[128,128]{1,0:T(8,128)(2,1)S(1)} collective-permute-done((bf16[128,128]{1,0:T(8,128)(2,1)S(1)}, bf16[128,128]{1,0:T(8,128)(2,1)S(1)}, u32[]{:S(2)}, u32[]{:S(2)}) %collective-permute-start.14) | collective-permute-done | bytes 32800 | tf_op jit(solution)/shard_map/ppermute | solution.py:507
  80.1 4.3 %all-to-all-start.3 = ((bf16[8,64,1792]{2,1,0:T(8,128)(2,1)}), bf16[8,64,1792]{2,1,0:T(8,128)(2,1)}, u32[]{:S(2)}, u32[]{:S(2)}) async-start(bf16[8,64,1792]{2,1,0:T(8,128)(2,1)} %shard_map.94), calls=%async_computation.3 | async-start | bytes 3670016 | tf_op jit(solution)/shard_map/all_to_all | solution.py:494
  84.5 1.9 %broadcast_select_fusion.1 = (bf16[256,4096]{1,0:T(8,128)(2,1)S(1)}, bf16[256,4096]{1,0:T(8,128)(2,1)S(1)}) fusion(bf16[256,4096]{1,0:T(8,128)(2,1)S(1)} %get-tuple-element.128, bf16[256,4096]{1,0:T(8,128)(2,1)} %collective-permute-done.15, pred[]{:T(512)S(6)} %eq.6, pred[]{:T(512)S(6)} %eq.7), kind=kLoop, calls=%fused_computation.5 | loop fusion | flops 2097152 | bytes 8388610 | tf_op jit(solution)/shard_map/jit(_where)/select_n | solution.py:513
  86.4 14.5 %fusion.base_ref = f32[256,1792]{1,0:T(8,128)S(1)} fusion(bf16[8192,1792]{1,0:T(8,128)(2,1)} %param.14, bf16[256,4096]{1,0:T(8,128)(2,1)S(1)} %get-tuple-element.137, bf16[256,4096]{1,0:T(8,128)(2,1)S(1)} %get-tuple-element.136), kind=kOutput, calls=%fused_computation | convolution fusion | flops 7524581376 | bytes 35389440 | tf_op jit(solution)/shard_map/dot_general | solution.py:514
  100.9 24.7 %all-to-all-done.3.incoming_ref = bf16[8,64,1792]{2,1,0:T(8,128)(2,1)} async-done(((bf16[8,64,1792]{2,1,0:T(8,128)(2,1)}), bf16[8,64,1792]{2,1,0:T(8,128)(2,1)}, u32[]{:S(2)}, u32[]{:S(2)}) %all-to-all-start.3) | async-done | bytes 1835040 | tf_op jit(solution)/shard_map/all_to_all | solution.py:494
  125.6 1.4 %conditional.1 = (bf16[8,64,1792]{2,1,0:T(8,128)(2,1)}) conditional(s32[]{:T(128)} %bitcast.5, () %tuple.31, (bf16[128,256]{1,0:T(8,128)(2,1)S(1)}, f32[128,128]{1,0:T(8,128)S(1)}, bf16[128,128]{1,0:T(8,128)(2,1)S(1)}, bf16[128,128]{1,0:T(8,128)(2,1)S(1)}, bf16[8,64,1792]{2,1,0:T(8,128)(2,1)}, ...), branch_computations={%region_0.1_spmd, %region_1.2_spmd, %region_2.3_spmd, %region_3.4_... | conditional | flops 234881024 | bytes 9175050 | solution.py:532
  125.6 1.4 %broadcast.2 = bf16[8,64,1792]{2,1,0:T(8,128)(2,1)} broadcast(bf16[]{:T(256)} %constant.12.clone), dimensions={} | broadcast | bytes 1835010 | tf_op jit(solution)/shard_map/broadcast.1
  127.0 4.6 %shard_map.95 = bf16[256,1792]{1,0:T(8,128)(2,1)} custom-call(s32[16]{0:T(128)S(1)} %get-tuple-element.100.begin_ref, s32[1]{0:T(128)S(6)} %max.3.more_ref, f32[256,1792]{1,0:T(8,128)S(1)} %fusion.base_ref, s32[256,128]{1,0:T(8,128)S(1)} %copy-done.24, bf16[128,128]{1,0:T(8,128)(2,1)S(1)} %add.42.coeff_ref, ...), custom_call_target="tpu_custom_call" | custom-call | flops 1879048192 | bytes 6422528 | tf_op jit(solution)/shard_map/pallas_call | solution.py:377
  (76 shorter events, 19.4 us)
Async XLA Ops:
  1.0 1.5 %collective-permute-start = (bf16[16,4096]{1,0:T(8,128)(2,1)S(1)}, bf16[16,4096]{1,0:T(8,128)(2,1)S(1)}, u32[]{:S(2)}, u32[]{:S(2)}) collective-permute-start(bf16[16,4096]{1,0:T(8,128)(2,1)S(1)} %get-tuple-element.139), channel_id=1, source_target_pairs={{0,1},{1,0},{2,3},{3,2},{4,5},{5,4},{6,7},{7,6},{8,9},{9,8},{10,11... | collective-permute-start | bytes 393224 | tf_op jit(solution)/shard_map/ppermute | solution.py:456
  2.5 9.5 %collective-permute-start.1 = (bf16[32,4096]{1,0:T(8,128)(2,1)S(1)}, bf16[32,4096]{1,0:T(8,128)(2,1)S(1)}, u32[]{:S(2)}, u32[]{:S(2)}) collective-permute-start(bf16[32,4096]{1,0:T(8,128)(2,1)S(1)} %pad_maximum_fusion.refs_0_), channel_id=1, source_target_pairs={{0,4},{1,5},{4,8},{5,9},{8,12},{9,13},{12,14},{13,15},{14,10},{15,... | collective-permute-start | bytes 786440 | tf_op jit(solution)/shard_map/ppermute | solution.py:410
  12.1 7.2 %copy-start.5 = (bf16[32,4096]{1,0:T(8,128)(2,1)}, bf16[32,4096]{1,0:T(8,128)(2,1)S(1)}, u32[]{:S(2)}) copy-start(bf16[32,4096]{1,0:T(8,128)(2,1)S(1)} %collective-permute-done.1.refs_1_) | copy-start | bytes 786436
  12.1 7.8 %collective-permute-start.3 = (bf16[32,4096]{1,0:T(8,128)(2,1)S(1)}, bf16[32,4096]{1,0:T(8,128)(2,1)S(1)}, u32[]{:S(2)}, u32[]{:S(2)}) collective-permute-start(bf16[32,4096]{1,0:T(8,128)(2,1)S(1)} %collective-permute-done.1.refs_1_), channel_id=1, source_target_pairs={{0,4},{1,5},{4,8},{5,9},{8,12},{9,13},{12,14},{13,15},{14,10},{15,... | collective-permute-start | bytes 786440 | tf_op jit(solution)/shard_map/ppermute | solution.py:410
  13.9 1.2 copy-start
  15.1 2.0 %copy-start.2 = (bf16[1,64,28672]{2,1,0:T(8,128)(2,1)S(1)}, bf16[1,64,28672]{2,1,0:T(8,128)(2,1)}, u32[]{:S(2)}) copy-start(bf16[1,64,28672]{2,1,0:T(8,128)(2,1)} %param.16) | copy-start | bytes 11010052
  17.1 29.8 %copy-start.1 = (bf16[1,64,8192]{2,1,0:T(8,128)(2,1)S(1)}, bf16[1,64,8192]{2,1,0:T(8,128)(2,1)}, u32[]{:S(2)}) copy-start(bf16[1,64,8192]{2,1,0:T(8,128)(2,1)} %param.15) | copy-start | bytes 3145732
  19.9 19.6 %collective-permute-start.6 = (bf16[8,64,1792]{2,1,0:T(8,128)(2,1)S(1)}, bf16[8,64,1792]{2,1,0:T(8,128)(2,1)}, u32[]{:S(2)}, u32[]{:S(2)}) collective-permute-start(bf16[8,64,1792]{2,1,0:T(8,128)(2,1)S(1)} %get-tuple-element.110), channel_id=1, source_target_pairs={{0,1},{1,0},{2,3},{3,2},{4,5},{5,4},{6,7},{7,6},{8,9},{9,8},{10,11... | collective-permute-start | bytes 5505032 | tf_op jit(solution)/shard_map/ppermute | solution.py:477
  19.9 8.7 %collective-permute-start.2 = (bf16[32,4096]{1,0:T(8,128)(2,1)S(1)}, bf16[32,4096]{1,0:T(8,128)(2,1)S(1)}, u32[]{:S(2)}, u32[]{:S(2)}) collective-permute-start(bf16[32,4096]{1,0:T(8,128)(2,1)S(1)} %pad_maximum_fusion.refs_0_), channel_id=1, source_target_pairs={{4,0},{5,1},{8,4},{9,5},{12,8},{13,9},{14,12},{15,13},{10,14},{11,... | collective-permute-start | bytes 786440 | tf_op jit(solution)/shard_map/ppermute | solution.py:412
  21.3 17.4 %collective-permute-start.7 = (bf16[64,4096]{1,0:T(8,128)(2,1)S(1)}, bf16[64,4096]{1,0:T(8,128)(2,1)S(1)}, u32[]{:S(2)}, u32[]{:S(2)}) collective-permute-start(bf16[64,4096]{1,0:T(8,128)(2,1)S(1)} %get-tuple-element.111), channel_id=1, source_target_pairs={{0,1},{1,0},{2,3},{3,2},{4,5},{5,4},{6,7},{7,6},{8,9},{9,8},{10,11... | collective-permute-start | bytes 1572872 | tf_op jit(solution)/shard_map/ppermute | solution.py:478
  28.6 7.9 %collective-permute-start.4 = (bf16[32,4096]{1,0:T(8,128)(2,1)S(1)}, bf16[32,4096]{1,0:T(8,128)(2,1)S(1)}, u32[]{:S(2)}, u32[]{:S(2)}) collective-permute-start(bf16[32,4096]{1,0:T(8,128)(2,1)S(1)} %collective-permute-done.2.refs_2_), channel_id=1, source_target_pairs={{4,0},{5,1},{8,4},{9,5},{12,8},{13,9},{14,12},{15,13},{10,14},{11,... | collective-permute-start | bytes 786440 | tf_op jit(solution)/shard_map/ppermute | solution.py:412
  30.8 7.9 %collective-permute-start.5 = (bf16[32,4096]{1,0:T(8,128)(2,1)S(1)}, bf16[32,4096]{1,0:T(8,128)(2,1)S(1)}, u32[]{:S(2)}, u32[]{:S(2)}) collective-permute-start(bf16[32,4096]{1,0:T(8,128)(2,1)S(1)} %collective-permute-done.3.refs_3_), channel_id=1, source_target_pairs={{0,4},{1,5},{4,8},{5,9},{8,12},{9,13},{12,14},{13,15},{14,10},{15,... | collective-permute-start | bytes 786440 | tf_op jit(solution)/shard_map/ppermute | solution.py:410
  36.6 7.0 %collective-permute-start.8 = (bf16[32,4096]{1,0:T(8,128)(2,1)S(1)}, bf16[32,4096]{1,0:T(8,128)(2,1)S(1)}, u32[]{:S(2)}, u32[]{:S(2)}) collective-permute-start(bf16[32,4096]{1,0:T(8,128)(2,1)S(1)} %collective-permute-done.4.refs_4_), channel_id=1, source_target_pairs={{4,0},{5,1},{8,4},{9,5},{12,8},{13,9},{14,12},{15,13},{10,14},{11,... | collective-permute-start | bytes 786440 | tf_op jit(solution)/shard_map/ppermute | solution.py:412
  39.5 6.8 %collective-permute-start.9 = (bf16[32,4096]{1,0:T(8,128)(2,1)S(1)}, bf16[32,4096]{1,0:T(8,128)(2,1)S(1)}, u32[]{:S(2)}, u32[]{:S(2)}) collective-permute-start(bf16[32,4096]{1,0:T(8,128)(2,1)S(1)} %collective-permute-done.5.refs_5_), channel_id=1, source_target_pairs={{0,4},{1,5},{4,8},{5,9},{8,12},{9,13},{12,14},{13,15},{14,10},{15,... | collective-permute-start | bytes 786440 | tf_op jit(solution)/shard_map/ppermute | solution.py:410
  47.0 1.0 copy-start.4
  48.0 0.9 copy-start.6
  49.0 0.9 copy-start.8
  49.9 0.9 copy-start.10
  50.9 0.9 copy-start.12
  51.8 0.9 copy-start.14
  54.7 11.7 %copy-start.25 = (bf16[8,64,1792]{2,1,0:T(8,128)(2,1)S(1)}, bf16[8,64,1792]{2,1,0:T(8,128)(2,1)}, u32[]{:S(2)}) copy-start(bf16[8,64,1792]{2,1,0:T(8,128)(2,1)} %get-tuple-element.123.mine_ref) | copy-start | bytes 5505028
  59.5 5.1 %collective-permute-start.10 = (f32[128,128]{1,0:T(8,128)S(1)}, f32[128,128]{1,0:T(8,128)S(1)}, u32[]{:S(2)}, u32[]{:S(2)}) collective-permute-start(f32[128,128]{1,0:T(8,128)S(1)} %get-tuple-element.114), channel_id=1, source_target_pairs={{0,1},{1,0},{2,3},{3,2},{4,5},{5,4},{6,7},{7,6},{8,9},{9,8},{10,11... | collective-permute-start | bytes 196616 | tf_op jit(solution)/shard_map/ppermute | solution.py:486
  59.6 3.8 %collective-permute-start.11 = (s32[1]{0:T(128)}, s32[1]{0:T(128)}, u32[]{:S(2)}, u32[]{:S(2)}) collective-permute-start(s32[1]{0:T(128)} %get-tuple-element.117), channel_id=1, source_target_pairs={{0,16},{16,0},{1,17},{17,1},{2,18},{18,2},{3,19},{19,3},{4,20},{20... | collective-permute-start | bytes 20 | tf_op jit(solution)/shard_map/ppermute | solution.py:426
  64.6 15.5 %collective-permute-start.15 = (bf16[256,4096]{1,0:T(8,128)(2,1)S(1)}, bf16[256,4096]{1,0:T(8,128)(2,1)}, u32[]{:S(2)}, u32[]{:S(2)}) collective-permute-start(bf16[256,4096]{1,0:T(8,128)(2,1)S(1)} %get-tuple-element.128), channel_id=1, source_target_pairs={{0,1},{1,0},{2,3},{3,2},{4,5},{5,4},{6,7},{7,6},{8,9},{9,8},{10,11... | collective-permute-start | bytes 6291464 | tf_op jit(solution)/shard_map/ppermute | solution.py:504
  64.7 6.5 %collective-permute-start.12 = (bf16[128,128]{1,0:T(8,128)(2,1)S(1)}, bf16[128,128]{1,0:T(8,128)(2,1)S(1)}, u32[]{:S(2)}, u32[]{:S(2)}) collective-permute-start(bf16[128,128]{1,0:T(8,128)(2,1)S(1)} %multiply_convert_fusion.coeff_ref), channel_id=1, source_target_pairs={{0,2},{1,3},{2,0},{3,1},{4,6},{5,7},{6,4},{7,5},{8,10},{9,11},{10,... | collective-permute-start | bytes 98312 | tf_op jit(solution)/shard_map/ppermute | solution.py:507
  71.2 4.0 %collective-permute-start.13 = (bf16[128,128]{1,0:T(8,128)(2,1)S(1)}, bf16[128,128]{1,0:T(8,128)(2,1)S(1)}, u32[]{:S(2)}, u32[]{:S(2)}) collective-permute-start(bf16[128,128]{1,0:T(8,128)(2,1)S(1)} %add.40), channel_id=1, source_target_pairs={{0,4},{1,5},{2,6},{3,7},{4,0},{5,1},{6,2},{7,3},{8,12},{9,13},{10,... | collective-permute-start | bytes 98312 | tf_op jit(solution)/shard_map/ppermute | solution.py:507
  75.2 4.9 %collective-permute-start.14 = (bf16[128,128]{1,0:T(8,128)(2,1)S(1)}, bf16[128,128]{1,0:T(8,128)(2,1)S(1)}, u32[]{:S(2)}, u32[]{:S(2)}) collective-permute-start(bf16[128,128]{1,0:T(8,128)(2,1)S(1)} %add.41), channel_id=1, source_target_pairs={{0,8},{1,9},{2,10},{3,11},{4,12},{5,13},{6,14},{7,15},{8,0},{9,1},... | collective-permute-start | bytes 98312 | tf_op jit(solution)/shard_map/ppermute | solution.py:507
  80.1 45.5 %all-to-all-start.3 = ((bf16[8,64,1792]{2,1,0:T(8,128)(2,1)}), bf16[8,64,1792]{2,1,0:T(8,128)(2,1)}, u32[]{:S(2)}, u32[]{:S(2)}) async-start(bf16[8,64,1792]{2,1,0:T(8,128)(2,1)} %shard_map.94), calls=%async_computation.3 | async-start | bytes 3670016 | tf_op jit(solution)/shard_map/all_to_all | solution.py:494
  86.3 39.2 %copy-start.26 = (bf16[128,256]{1,0:T(8,128)(2,1)S(1)}, bf16[128,256]{1,0:T(8,128)(2,1)}, u32[]{:S(2)}) copy-start(bf16[128,256]{1,0:T(8,128)(2,1)} %get-tuple-element.120.choose_ref) | copy-start | bytes 196612
  86.3 39.2 %copy-start.27 = (f32[128,128]{1,0:T(8,128)S(1)}, f32[128,128]{1,0:T(8,128)}, u32[]{:S(2)}) copy-start(f32[128,128]{1,0:T(8,128)} %get-tuple-element.121.live_ref) | copy-start | bytes 196612
  86.4 39.2 %copy-start.28 = (bf16[128,128]{1,0:T(8,128)(2,1)S(1)}, bf16[128,128]{1,0:T(8,128)(2,1)}, u32[]{:S(2)}) copy-start(bf16[128,128]{1,0:T(8,128)(2,1)} %get-tuple-element.122.fixed_ref) | copy-start | bytes 98308
  125.6 1.4 %copy-start.24 = (s32[256,128]{1,0:T(8,128)S(1)}, s32[256,128]{1,0:T(8,128)}, u32[]{:S(2)}) copy-start(s32[256,128]{1,0:T(8,128)} %copy-done.23) | copy-start | bytes 393220
  (14 other events, 10.1 us)
